TPU v7x, 32 devices: a whole 2x2x4 slice. The times are simulated.
32 devices in a mesh: dp: 16 (over z, y, core), node: 2 (over x).
Axes of the slice: x: 2, y: 2, z: 4, core: 2. Of those that a mesh axis runs over, the one named last changes fastest.
Arguments:
- tokens: bfloat16 [256, 4096], P('dp', 'node'), may hold values from -200 to 200
- cotangent: bfloat16 [256, 4096], P('dp', 'node'), may hold values from -6 to 6
- norm_gain: float32 [4096], P('node'), may hold values from 0.1 to 1.9
- gate_weight: bfloat16 [10240, 4096], P('dp', 'node'), may hold values from -0.09375 to 0.09375
- up_weight: bfloat16 [10240, 4096], P('dp', 'node'), may hold values from -0.09375 to 0.09375
- down_weight: bfloat16 [10240, 4096], P('dp', 'node'), may hold values from -0.0625 to 0.0625
Outputs:
- branch_out: bfloat16 [256, 4096], P('dp', 'node')
- grad_tokens: bfloat16 [256, 4096], P('dp', 'node')
- grad_gate_weight: float32 [10240, 4096], P('dp', 'node')
- grad_up_weight: float32 [10240, 4096], P('dp', 'node')
- grad_down_weight: float32 [10240, 4096], P('dp', 'node')
- grad_norm_gain: float32 [4096], P('node')
All inputs are finite; a program needn't handle non-finite values.
Results may differ from a plain program's by a relative error of at most 0.0065.
Values may be sent and summed in bfloat16 or wider, within the bound.
No kernel may reach another device: no remote copies, remote signals or barrier semaphores. Data moves between devices by JAX's collectives and lax.ppermute only.
A program may use at most 64 MiB of HBM per device.

v0:
```python
import math

import jax
import jax.numpy as jnp
from jax import lax
from jax.sharding import PartitionSpec as P

D = 4096


EPSILON = 1e-06
GELU_SCALE = math.sqrt(2.0 / math.pi)


def gelu_parts(value):
    inner = GELU_SCALE * (value + 0.044715 * value * value * value)
    tanh_inner = jnp.tanh(inner)
    activated = 0.5 * value * (1.0 + tanh_inner)
    slope = 0.5 * (1.0 + tanh_inner) + 0.5 * value * (
        1.0 - tanh_inner * tanh_inner
    ) * GELU_SCALE * (1.0 + 3.0 * 0.044715 * value * value)
    return (activated, slope)


def activation_grads(back_sum, up_value, activated, slope):
    return jnp.stack([back_sum * up_value * slope, back_sum * activated]).astype(jnp.bfloat16)


def on_device(tokens, cotangent, norm_gain, gate_weight, up_weight, down_weight):
    widened = tokens.astype(jnp.float32)
    square_part = jnp.sum(widened * widened, axis=1)
    mean_square = lax.psum(square_part, "node") / D
    inv_rms = lax.rsqrt(mean_square + EPSILON)
    scaled = widened * inv_rms[:, None]
    normed = (scaled * norm_gain).astype(jnp.bfloat16)
    normed_all = lax.all_gather(normed, "dp", axis=0, tiled=True)
    both_weights = jnp.stack([gate_weight, up_weight])
    partials = lax.dot_general(
        both_weights, normed_all, (((2,), (1,)), ((), ())), preferred_element_type=jnp.float32
    )
    summed = lax.psum(partials, "node")
    gate_value, up_value = (summed[0], summed[1])
    activated, slope = gelu_parts(gate_value)
    hidden = (activated * up_value).astype(jnp.bfloat16)
    columns = hidden
    branch_out = lax.psum_scatter(
        lax.dot_general(
            columns, down_weight, (((0,), (0,)), ((), ())), preferred_element_type=jnp.float32
        ),
        "dp",
        scatter_dimension=0,
        tiled=True,
    ).astype(jnp.bfloat16)
    cot_all = lax.all_gather(cotangent, "dp", axis=0, tiled=True)
    back_part = lax.dot_general(
        down_weight, cot_all, (((1,), (1,)), ((), ())), preferred_element_type=jnp.float32
    )
    grad_down_weight = lax.dot_general(
        hidden, cot_all, (((1,), (0,)), ((), ())), preferred_element_type=jnp.float32
    )
    back_sum = lax.psum(back_part, "node")
    grad_pair = activation_grads(back_sum, up_value, activated, slope)
    weight_grads = lax.dot_general(
        grad_pair, normed_all, (((2,), (0,)), ((), ())), preferred_element_type=jnp.float32
    )
    columns = grad_pair
    grad_normed = lax.psum_scatter(
        lax.dot_general(
            columns, both_weights, (((0, 1), (0, 1)), ((), ())), preferred_element_type=jnp.float32
        ),
        "dp",
        scatter_dimension=0,
        tiled=True,
    )
    grad_scaled = grad_normed * norm_gain
    row_part = jnp.sum(grad_scaled * scaled, axis=1)
    gain_part = jnp.sum(grad_normed * scaled, axis=0)
    row_total = lax.psum(row_part, "node")
    gain_total = lax.psum(gain_part, "dp")
    grad_tokens = (inv_rms[:, None] * (grad_scaled - scaled * (row_total / D)[:, None])).astype(
        jnp.bfloat16
    )
    return (branch_out, grad_tokens, weight_grads[0], weight_grads[1], grad_down_weight, gain_total)


def solution(mesh):
    in_specs = (
        P("dp", "node"),
        P("dp", "node"),
        P("node"),
        P("dp", "node"),
        P("dp", "node"),
        P("dp", "node"),
    )
    out_specs = (
        P("dp", "node"),
        P("dp", "node"),
        P("dp", "node"),
        P("dp", "node"),
        P("dp", "node"),
        P("node"),
    )
    return jax.shard_map(
        on_device, mesh=mesh, in_specs=in_specs, out_specs=out_specs, check_vma=False
    )
```

profile of v0, /device:TPU:0, one launch (start us, length us, event | category | flops | bytes accessed | tf_op | source)
XLA Modules:
  0.0 296.7 jit_solution(16299246984243327166)
XLA Ops:
  7.2 0.0 all-gather.5.cloned.1.call-start
  7.2 0.7 all-gather.5.cloned.1.call-update
  7.9 0.0 all-gather.3.cloned.1.call-start
  8.0 1.0 fusion.25
  8.9 5.8 %psum.35 = f32[16]{0:T(128)S(1)} all-reduce(f32[16]{0:T(128)S(1)} %fusion.25), channel_id=1, replica_groups=mesh['dp'=16,'node'=2] {'node'}, use_global_device_ids=true, to_apply=%region_1.0 | all-reduce | flops 16 | bytes 128 | tf_op jit(solution)/shard_map/psum | solution.py:32
  14.8 1.6 fusion.19
  16.3 0.0 all-gather.3.cloned.1.call-update
  16.4 0.0 all-reduce.3.cloned.1.call-start
  16.4 34.4 %all-gather.5.cloned.1.call-done = bf16[256,2048]{1,0:T(8,128)(2,1)} async-done(((bf16[16,2048]{1,0:T(8,128)(2,1)}), bf16[256,2048]{1,0:T(8,128)(2,1)}) %all-gather.5.cloned.1.call-update) | async-done | bytes 1048592 | tf_op jit(solution)/shard_map/all_gather | solution.py:54
  50.9 2.9 fusion.30
  53.8 36.7 %all-gather.3.cloned.1.call-done = bf16[256,2048]{1,0:T(8,128)(2,1)} async-done(((bf16[16,2048]{1,0:T(8,128)(2,1)}), bf16[256,2048]{1,0:T(8,128)(2,1)}) %all-gather.3.cloned.1.call-update) | async-done | bytes 1048592 | tf_op jit(solution)/shard_map/all_gather | solution.py:36
  90.5 5.4 %fusion.1 = f32[2,640,256]{2,1,0:T(8,128)} fusion(bf16[1,640,2048]{2,1,0:T(8,128)(2,1)} %bitcast.49, bf16[1,640,2048]{2,1,0:T(8,128)(2,1)} %bitcast.51, bf16[256,2048]{1,0:T(8,128)(2,1)} %all-gather.3.cloned.1.call-done), kind=kOutput, calls=%fused_computation.4 | convolution fusion | flops 1344798720 | bytes 7602176 | tf_op jit(solution)/shard_map/dot_general | solution.py:38
  95.9 0.0 all-reduce.3.cloned.1.call-update
  95.9 0.0 reduce-scatter.5.cloned.1.call-start
  96.0 59.3 %all-reduce.3.cloned.1.call-done = (f32[2,640,256]{2,1,0:T(8,128)}, f32[640,256]{1,0:T(8,128)}) async-done(((f32[2,640,256]{2,1,0:T(8,128)}, f32[640,256]{1,0:T(8,128)}), (f32[2,640,256]{2,1,0:T(8,128)}, f32[640,256]{1,0:T(8,128)})) %all-reduce.3.cloned.1.call-update) | async-done | bytes 1966096 | tf_op jit(solution)/shard_map/psum | solution.py:41
  155.2 2.2 fusion.14
  157.4 0.7 copy-done.1
  158.1 4.6 %fusion.2 = f32[256,2048]{1,0:T(8,128)} fusion(bf16[1,640,2048]{2,1,0:T(8,128)(2,1)S(1)} %bitcast.50, bf16[1,640,2048]{2,1,0:T(8,128)(2,1)} %bitcast.52, bf16[1,640,256]{2,1,0:T(8,128)(2,1)S(1)} %get-tuple-element.13, bf16[1,640,256]{2,1,0:T(8,128)(2,1)S(1)} %get-tuple-element.12), kind=kOutput, calls=%fused_computation.5 | convolution fusion | flops 1345126400 | bytes 7995392 | tf_op jit(solution)/shard_map/dot_general | solution.py:68
  162.7 0.0 reduce-scatter.5.cloned.1.call-update
  162.7 0.0 reduce-scatter.3.cloned.1.call-start
  162.8 2.3 fusion.29
  165.1 0.0 reduce-scatter.3.cloned.1.call-update
  165.2 4.5 %fusion.31 = f32[640,2048]{1,0:T(8,128)} fusion(bf16[640,256]{1,0:T(8,128)(2,1)S(1)} %get-tuple-element.14, bf16[256,2048]{1,0:T(8,128)(2,1)} %all-gather.5.cloned.1.call-done), kind=kOutput, calls=%fused_computation.46 | convolution fusion | flops 671088640 | bytes 6619136 | tf_op jit(solution)/shard_map/dot_general | solution.py:58
  169.7 1.5 fusion.3
  171.3 4.9 %slice_bitcast_fusion = (f32[640,2048]{1,0:T(8,128)}, f32[640,2048]{1,0:T(8,128)}) fusion(f32[2,640,2048]{2,1,0:T(8,128)S(1)} %fusion.3), kind=kLoop, calls=%fused_computation | loop fusion | bytes 20971520 | tf_op jit(solution)/shard_map/squeeze | solution.py:83
  176.2 48.2 %reduce-scatter.5.cloned.1.call-done = f32[16,2048]{1,0:T(8,128)} async-done(((f32[256,2048]{1,0:T(8,128)}), f32[16,2048]{1,0:T(8,128)}) %reduce-scatter.5.cloned.1.call-update) | async-done | bytes 131088 | tf_op jit(solution)/shard_map/reduce_scatter | solution.py:67
  224.5 1.1 fusion.24
  225.6 4.9 %psum.38 = f32[16]{0:T(128)S(1)} all-reduce(f32[16]{0:T(128)S(1)} %get-tuple-element.7), channel_id=1, replica_groups=mesh['dp'=16,'node'=2] {'node'}, use_global_device_ids=true, to_apply=%region_7.0 | all-reduce | flops 16 | bytes 128 | tf_op jit(solution)/shard_map/psum | solution.py:78
  230.5 30.7 %psum.39 = f32[2048]{0:T(1024)} all-reduce(f32[2048]{0:T(1024)S(1)} %get-tuple-element.6), channel_id=1, replica_groups=mesh['dp'=16,'node'=2] {'dp'}, use_global_device_ids=true, to_apply=%region_9.0 | all-reduce | flops 2048 | bytes 16384 | tf_op jit(solution)/shard_map/psum | solution.py:79
  261.2 1.6 fusion.23
  262.8 25.8 %reduce-scatter.3.cloned.1.call-done = f32[16,2048]{1,0:T(8,128)} async-done(((f32[256,2048]{1,0:T(8,128)}), f32[16,2048]{1,0:T(8,128)}) %reduce-scatter.3.cloned.1.call-update) | async-done | bytes 131088 | tf_op jit(solution)/shard_map/reduce_scatter | solution.py:46
  288.6 1.5 convert_element_type.19
  (15 shorter events, 0.1 us)
Async XLA Ops:
  7.2 43.7 %copy-start = (bf16[640,2048]{1,0:T(8,128)(2,1)S(1)}, bf16[640,2048]{1,0:T(8,128)(2,1)}, u32[]{:S(2)}) copy-start(bf16[640,2048]{1,0:T(8,128)(2,1)} %param.11) | copy-start | bytes 7864324
  7.2 43.7 %all-gather.5.cloned.1.call-start = ((), (), s32[]{:S(2)}) async-start(), calls=%async_computation.4 | async-start | bytes 1114112 | tf_op jit(solution)/shard_map/all_gather | solution.py:54
  7.9 82.6 %all-gather.3.cloned.1.call-start = ((), (), s32[]{:S(2)}) async-start(), calls=%async_computation.2 | async-start | bytes 1114112 | tf_op jit(solution)/shard_map/all_gather | solution.py:36
  16.4 138.9 %all-reduce.3.cloned.1.call-start = ((), (), s32[]{:S(2)}) async-start(), calls=%async_computation.6 | async-start | bytes 3932160 | tf_op jit(solution)/shard_map/psum | solution.py:41
  95.9 128.5 %reduce-scatter.5.cloned.1.call-start = ((), (), s32[]{:S(2)}) async-start(), calls=%async_computation.5 | async-start | bytes 2228224 | tf_op jit(solution)/shard_map/reduce_scatter | solution.py:67
  155.2 2.9 copy-start.6
  157.4 0.7 copy-start.1
  162.7 125.9 %reduce-scatter.3.cloned.1.call-start = ((), (), s32[]{:S(2)}) async-start(), calls=%async_computation.3 | async-start | bytes 2228224 | tf_op jit(solution)/shard_map/reduce_scatter | solution.py:46
  165.2 4.6 %copy-start.2 = (bf16[1,640,256]{2,1,0:T(8,128)(2,1)S(1)}, bf16[1,640,256]{2,1,0:T(8,128)(2,1)}, u32[]{:S(2)}) copy-start(bf16[1,640,256]{2,1,0:T(8,128)(2,1)} %copy-done.1) | copy-start | bytes 983044
  165.2 4.6 %copy-start.3 = (bf16[256,2048]{1,0:T(8,128)(2,1)S(1)}, bf16[256,2048]{1,0:T(8,128)(2,1)}, u32[]{:S(2)}) copy-start(bf16[256,2048]{1,0:T(8,128)(2,1)} %all-gather.3.cloned.1.call-done) | copy-start | bytes 3145732
  171.2 53.2 %copy-start.4 = (bf16[16,2048]{1,0:T(8,128)(2,1)S(1)}, bf16[16,2048]{1,0:T(8,128)(2,1)}, u32[]{:S(2)}) copy-start(bf16[16,2048]{1,0:T(8,128)(2,1)} %param.6) | copy-start | bytes 196612
  171.3 53.2 %copy-start.5 = (f32[2048]{0:T(1024)S(1)}, f32[2048]{0:T(1024)}, u32[]{:S(2)}) copy-start(f32[2048]{0:T(1024)} %param.8) | copy-start | bytes 24580
Sparse Core Ops, SparseCore 0:
  10.2 40.6 all-gather.4
  53.6 36.8 all-gather.2
  96.0 59.1 all-reduce.2
  162.9 61.5 reduce-scatter.4
  228.0 60.5 reduce-scatter.2
where the time goes:
time: 297 us
  waiting for transfers between devices  205 us (69%)
  blocking collectives  41.4 us (14%)
  matrix products  21.3 us (7%)
  between operations  13.8 us (5%)
  other arithmetic  8.99 us (3%)
  local copies, waits for them, and re-layouts  5.69 us (2%)
    psum x1, waiting for transfers between devices, on_device(): summed = lax.psum(partials, 'node')  59.3 us
    reduce_scatter x1, waiting for transfers between devices, on_device(): lax.psum_scatter(lax.dot_general(columns, both_weights, (((0, 1), (0, 1))...  48.2 us
    all_gather x1, waiting for transfers between devices, on_device(): normed_all = lax.all_gather(normed, 'dp', axis=0, tiled=True)  36.7 us
    all_gather x1, waiting for transfers between devices, on_device(): cot_all = lax.all_gather(cotangent, 'dp', axis=0, tiled=True)  34.4 us
    psum x1, blocking collectives, on_device(): gain_total = lax.psum(gain_part, 'dp')  30.7 us
    reduce_scatter x1, waiting for transfers between devices, on_device(): lax.psum_scatter(lax.dot_general(columns, down_weight, (((0,), (0,)), (()...  25.8 us
  transfers between devices with their start and end apart: 5, of which 5 were waited for; matrix products, arithmetic and copies ran while one was open for 7% of the time, Pallas kernels for 0%

commit v1 on v0

v1 whole, which is shorter than its diff:
```python
import functools
import math

import jax
import jax.numpy as jnp
from jax import lax
from jax.experimental import pallas as pl
from jax.experimental.pallas import tpu as pltpu
from jax.sharding import PartitionSpec as P

EPSILON = 1e-06
GELU_SCALE = math.sqrt(2.0 / math.pi)
BF16 = jnp.bfloat16
F32 = jnp.float32


def gelu_parts(value):
    inner = GELU_SCALE * (value + 0.044715 * value * value * value)
    tanh_inner = jnp.tanh(inner)
    activated = 0.5 * value * (1.0 + tanh_inner)
    slope = 0.5 * (1.0 + tanh_inner) + 0.5 * value * (
        1.0 - tanh_inner * tanh_inner
    ) * GELU_SCALE * (1.0 + 3.0 * 0.044715 * value * value)
    return (activated, slope)


def swap(value, axis, size, distance):
    return lax.ppermute(value, axis, [(i, i ^ distance) for i in range(size)])


def node_sum(value, node):
    bit = 1
    while bit < node:
        value = value + swap(value.astype(BF16), "node", node, bit).astype(F32)
        bit *= 2
    return value


def halving_distances(dp):
    distances = []
    bit = 4
    while bit < dp:
        distances.append(bit)
        bit *= 2
    return distances


def direct_steps(dp):
    distances, steps = halving_distances(dp), []
    while distances:
        low, *high = distances[:2]
        steps.append([high[0], low, low ^ high[0]] if high else [low])
        distances = distances[2:]
    return steps


def gather_rows(rows, dp):
    for parts in reversed(direct_steps(dp)):
        rows = jnp.concatenate([rows] + [swap(rows, "dp", dp, d) for d in parts], axis=0)
    rows = lax.optimization_barrier(rows)
    return jnp.concatenate([rows, swap(rows, "dp", dp, 2)], axis=0), rows


def gather_rows_behind(rows, dp, behind, used_behind):
    for place, distance in enumerate(reversed(halving_distances(dp))):
        if place == 1:
            rows = after(rows, behind)
        rows = jnp.concatenate([rows, swap(rows, "dp", dp, distance)], axis=0)
    return jnp.concatenate([rows, after(swap(rows, "dp", dp, 2), used_behind)], axis=0)


def inward(rows, weight):
    return lax.dot_general(rows, weight, (((1,), (1,)), ((), ())), preferred_element_type=F32)


def outward(rows, weight):
    return lax.dot_general(rows, weight, (((1,), (0,)), ((), ())), preferred_element_type=F32)


def grad_kernel(count, *refs):
    rows, inputs = refs[: 2 * count], refs[2 * count : 2 * count + 2]
    outs, (mark, turned) = refs[-count - 2 : -2], refs[-2:]
    half, units = rows[0].shape

    @pl.when(pl.program_id(0) == 0)
    def _():
        mark[...] = jnp.zeros(mark.shape, F32)
        for place, ref in enumerate(rows):
            piece, k = divmod(place, count)
            turned[k * units : (k + 1) * units, piece * half : (piece + 1) * half] = ref[...].T

    block = jnp.concatenate([ref[...] for ref in inputs], axis=0)
    for k in range(count):
        outs[k][...] = jnp.dot(
            turned[k * units : (k + 1) * units, :], block, preferred_element_type=F32
        )


def weight_grads(count, rows, inputs, behind):
    units, width = rows[0].shape[1], inputs[0].shape[1]
    block = min(width, 512)
    whole = lambda a: pl.BlockSpec(a.shape, lambda i: (0, 0))
    columns = lambda a: pl.BlockSpec((a.shape[0], block), lambda i: (0, i))
    return pl.pallas_call(
        functools.partial(grad_kernel, count),
        grid=(width // block,),
        in_specs=[whole(a) for a in rows]
        + [columns(a) for a in inputs]
        + [pl.BlockSpec(memory_space=pl.ANY)] * len(behind),
        out_specs=[pl.BlockSpec((units, block), lambda i: (0, i))] * count
        + [pl.BlockSpec((8, width), lambda i: (0, 0))],
        out_shape=[jax.ShapeDtypeStruct((units, width), F32)] * count
        + [jax.ShapeDtypeStruct((8, width), F32)],
        scratch_shapes=[pltpu.VMEM((count * units, 2 * rows[0].shape[0]), BF16)],
        compiler_params=pltpu.CompilerParams(vmem_limit_bytes=20 * 2**20),
        cost_estimate=pl.CostEstimate(flops=1000, bytes_accessed=1000, transcendentals=0),
        name="weight_grads",
    )(*rows, *inputs, *behind)


def add_kernel(kept_ref, got_ref, *refs):
    refs[-1][...] = kept_ref[...] + got_ref[...].astype(F32)


def add_got(kept, got, bytes_accessed, behind=()):
    return pl.pallas_call(
        add_kernel,
        in_specs=[pl.BlockSpec(memory_space=pltpu.VMEM)] * 2
        + [pl.BlockSpec(memory_space=pl.ANY)] * len(behind),
        out_shape=jax.ShapeDtypeStruct(kept.shape, F32),
        compiler_params=pltpu.CompilerParams(vmem_limit_bytes=8 * 2**20),
        cost_estimate=pl.CostEstimate(flops=1, bytes_accessed=bytes_accessed, transcendentals=0),
        name="add_got",
    )(kept, got, *behind)


def gain_kernel(*refs):
    products, inputs, gain, out = refs[:3], refs[3:5], refs[5], refs[6]
    half = products[0].shape[0]
    rows = [inputs[0][:half], inputs[0][half:], inputs[1][...]]
    total = jnp.zeros(out.shape, F32)
    for product, tokens in zip(products, rows):
        terms = product[...].astype(F32) * tokens.astype(F32)
        total = total + jnp.sum(terms, axis=0, keepdims=True)
    out[...] = total / gain[...]


def gain_sums(products, inputs, gain):
    out = pl.pallas_call(
        gain_kernel,
        out_shape=jax.ShapeDtypeStruct((1, gain.shape[0]), F32),
        compiler_params=pltpu.CompilerParams(vmem_limit_bytes=8 * 2**20),
        cost_estimate=pl.CostEstimate(flops=1000, bytes_accessed=1000, transcendentals=0),
        name="gain_sums",
    )(*products, *inputs, gain[None, :])
    return out


def after(value, dep):
    width = value.shape[1]
    if dep.shape[1] >= width:
        row = lax.slice(dep, (0, 0), (1, width))
    else:
        row = lax.slice(dep, (0, 0), (1, math.gcd(dep.shape[1], width)))
        row = jnp.tile(row, (1, width // row.shape[1]))
    return jnp.where(row == row, value, jnp.zeros_like(value))


def on_device(dp, node, tokens, cotangent, norm_gain, gate_weight, up_weight, down_weight):
    features = tokens.shape[1] * node
    widened = tokens.astype(F32)
    square_sum = jnp.sum(widened * widened, axis=1)
    bit = 1
    while bit < node:
        square_sum = square_sum + swap(square_sum, "node", node, bit)
        bit *= 2
    inv_rms = lax.rsqrt(square_sum / features + EPSILON)[:, None]
    scaled = widened * inv_rms
    normed_rows = (scaled * norm_gain).astype(BF16)
    own_n, sent_n = gather_rows(normed_rows, dp)
    size = own_n.shape[0] // 2
    other_n = swap(own_n, "dp", dp, 1)

    def project(rows):
        return jnp.concatenate([inward(rows, gate_weight), inward(rows, up_weight)], axis=0)

    own_p = project(own_n)
    own_c = gather_rows_behind(cotangent, dp, sent_n, own_p)
    other_c = swap(own_c, "dp", dp, 1)
    other_p = project(other_n)
    other_b = after(inward(other_c, down_weight), other_p)
    own_b = after(inward(own_c, down_weight), other_b)
    own_p = after(node_sum(own_p, node), own_b)
    other_p, other_b = node_sum(other_p, node), node_sum(other_b, node)
    own_b = node_sum(own_b, node)

    def activate(both):
        gate_value, up_value = both[: 2 * size], both[2 * size :]
        activated, slope = gelu_parts(gate_value)
        hidden = (activated * up_value).astype(BF16)
        lean = slope * up_value
        row_factor = lean * gate_value + activated * up_value
        return lax.optimization_barrier((hidden, activated, lean, row_factor))

    def grads(back, activated, lean, row_factor):
        grad_gate, grad_up = (back * lean).astype(BF16), (back * activated).astype(BF16)
        row_part = jnp.sum(back * row_factor, axis=1)[None, :]
        return lax.optimization_barrier(((grad_gate, grad_up), row_part))

    def outward_pair(pair):
        return outward(pair[0], gate_weight) + outward(pair[1], up_weight)

    own_h, *own_f = activate(own_p)
    other_h, *other_f = activate(other_p)
    sent_h = outward(other_h, down_weight).astype(BF16)
    got_h = swap(sent_h, "dp", dp, 1)
    branch_sent = outward(own_h[size:], down_weight) + got_h[size:].astype(F32)
    branch_sent = lax.optimization_barrier(branch_sent.astype(BF16))
    branch = outward(own_h[:size], down_weight) + got_h[:size].astype(F32)
    grad_down_weight, mark = weight_grads(1, (own_h, other_h), (own_c, other_c), (sent_h,))

    other_g, other_r = grads(after(other_b, mark), *other_f)
    sent_g = outward_pair(other_g).astype(BF16)
    got_g = swap(sent_g, "dp", dp, 1)
    own_b = after(after(own_b, branch_sent), sent_g)
    own_g, own_r = grads(own_b, *own_f)
    normed_y = outward_pair([rows[size:] for rows in own_g])
    normed_sent = lax.optimization_barrier((normed_y + got_g[size:].astype(F32)).astype(BF16))
    normed_own = outward_pair([after(rows[:size], normed_sent) for rows in own_g])
    gain_part = gain_sums((normed_own, normed_y, sent_g), (own_n, other_n), norm_gain)
    width = gain_part.shape[1]

    def vector(distance, gain, rows):
        return swap(jnp.concatenate([gain, rows], axis=1), "dp", dp, distance)

    got_v = [
        vector(1, gain_part, other_r[:, :size]),
        vector(2, gain_part, own_r[:, size:]),
        vector(3, gain_part, other_r[:, size:]),
    ]
    branch = add_got(branch, swap(branch_sent, "dp", dp, 2), 40_000_000, (gain_part,))
    distances = halving_distances(dp)
    half = branch.shape[0] // 2
    sent_h = lax.optimization_barrier(branch[half:].astype(BF16))
    grad_gate_weight, grad_up_weight, mark = weight_grads(
        2, (*own_g, *other_g), (own_n, other_n), (gain_part, sent_h)
    )
    for distance in distances[1:]:
        branch = branch[:half] + swap(sent_h, "dp", dp, distances[0]).astype(F32)
        distances, half = distances[1:], half // 2
        sent_h = lax.optimization_barrier(branch[half:].astype(BF16))
    branch = branch[:half] + swap(sent_h, "dp", dp, distances[0]).astype(F32)

    normed = normed_own + got_g[:size].astype(F32)
    normed = add_got(normed, swap(normed_sent, "dp", dp, 2), 40_000_000, (mark,))
    normed = after(normed, sent_h)
    vectors = jnp.concatenate([after(gain_part, mark), own_r[:, :size]], axis=1)
    vectors = vectors + (got_v[0] + got_v[1] + got_v[2])
    gain_part, rows = after(vectors[:, :width], normed), after(vectors[:, width:], normed)
    for parts in direct_steps(dp):
        count = normed.shape[0] // (len(parts) + 1)
        extra = gain_part.reshape(count, -1)
        lanes = extra.shape[1]
        joined = [
            jnp.concatenate(
                [normed[place * count : (place + 1) * count], extra]
                + [jnp.pad(rows[:, place * count : (place + 1) * count], ((0, count - 1), (0, 0)))],
                axis=1,
            )
            for place in range(len(parts) + 1)
        ]
        total = joined[0]
        for place, distance in enumerate(parts):
            sent = joined[place + 1].astype(BF16)
            total = total + swap(sent, "dp", dp, distance).astype(F32)
        normed = total[:, :width]
        gain_part = total[:, width : width + lanes].reshape(1, width)
        rows = total[:1, width + lanes :]

    row_mean = (rows / features).reshape(-1, 1)
    grad_scaled = normed * norm_gain
    grad_tokens = (inv_rms * (grad_scaled - scaled * row_mean)).astype(BF16)
    return (
        branch.astype(BF16),
        grad_tokens,
        grad_gate_weight,
        grad_up_weight,
        grad_down_weight,
        gain_part[0],
    )


def solution(mesh):
    dp, node = mesh.shape["dp"], mesh.shape["node"]

    def run(*arrays):
        return on_device(dp, node, *arrays)

    grid = P("dp", "node")
    return jax.shard_map(
        run,
        mesh=mesh,
        in_specs=(grid, grid, P("node"), grid, grid, grid),
        out_specs=(grid, grid, grid, grid, grid, P("node")),
        check_vma=False,
    )
```

time: 297 us -> 86.6 us (0.29)
  waiting for transfers between devices: 205 us -> 25.7 us
  blocking collectives: 41.4 us -> 0 us
  starting transfers between devices: 0.2 us -> 31.2 us
  between operations: 13.8 us -> 1.09 us
  matrix products: 21.3 us -> 12.6 us
  Pallas kernels: 0 us -> 8.68 us
  local copies, waits for them, and re-layouts: 5.69 us -> 1.05 us
  other arithmetic: 8.99 us -> 6.01 us
    reduce_scatter x2 -> x0, waiting for transfers between devices: 74.1 us -> none  [the longest x1 48.2 us: on_device(): lax.psum_scatter(lax.dot_general(columns, both_weights, (((0, 1), (0, 1))...]
    all_gather x2 -> x0, waiting for transfers between devices: 71.1 us -> none  [the longest x1 36.7 us: on_device(): normed_all = lax.all_gather(normed, 'dp', axis=0, tiled=True)]
    psum x1 -> x0, waiting for transfers between devices: 59.3 us -> none  [on_device(): summed = lax.psum(partials, 'node')]
    psum x3 -> x0, blocking collectives: 41.4 us -> none  [the longest x1 30.7 us: on_device(): gain_total = lax.psum(gain_part, 'dp')]
    ppermute x0 -> x26, starting transfers between devices: none -> 31.2 us  [swap(): return lax.ppermute(value, axis, [(i, i ^ distance) for i in range(size)])]
    ppermute x0 -> x26, waiting for transfers between devices: none -> 25.7 us  [swap(): return lax.ppermute(value, axis, [(i, i ^ distance) for i in range(size)])]
    dot_general x6 -> x15, matrix products: 21.3 us -> 12.6 us  [the longest x6 7.33 us: inward(): lax.dot_general(rows, weight, (((1,), (1,)), ((), ())), preferred_element...]
    pallas_call x0 -> x5, Pallas kernels: none -> 8.68 us  [the longest x2 8.38 us: weight_grads(): pl.pallas_call(functools.partial(grad_kernel, count), grid=(width // bloc...]
  transfers between devices with their start and end apart: 5 -> 26, of which waited for: 5 -> 13; matrix products, arithmetic and copies ran while one was open for 7% -> 17% of each run, Pallas kernels for 0% -> 10%
where the time goes in v1:
time: 86.6 us; the launch traced here: 86.3 us
  starting transfers between devices  31.2 us (36%)
  waiting for transfers between devices  25.7 us (30%)
  matrix products  12.6 us (15%)
  Pallas kernels  8.68 us (10%)
  other arithmetic  6.01 us (7%)
  between operations  1.09 us (1%)
  local copies, waits for them, and re-layouts  1.05 us (1%)
    ppermute x26, starting transfers between devices, swap(): return lax.ppermute(value, axis, [(i, i ^ distance) for i in range(size)])  31.2 us
    ppermute x26, waiting for transfers between devices, swap(): return lax.ppermute(value, axis, [(i, i ^ distance) for i in range(size)])  25.7 us
    pallas_call x2, Pallas kernels, weight_grads(): pl.pallas_call(functools.partial(grad_kernel, count), grid=(width // bloc...  8.38 us
    dot_general x6, matrix products, inward(): lax.dot_general(rows, weight, (((1,), (1,)), ((), ())), preferred_element...  7.33 us
    dot_general x9, matrix products, outward(): lax.dot_general(rows, weight, (((1,), (0,)), ((), ())), preferred_element...  5.24 us
  transfers between devices with their start and end apart: 26, of which 13 were waited for; matrix products, arithmetic and copies ran while one was open for 17% of the time, Pallas kernels for 10%

profile of v1, /device:TPU:0, one launch (start us, length us, event | category | flops | bytes accessed | tf_op | source)
XLA Modules:
  0.0 86.3 jit_solution(14802099137501920777)
XLA Ops:
  0.6 1.1 %fusion.27 = f32[16]{0:T(128)S(1)} fusion(bf16[16,2048]{1,0:T(8,128)(2,1)} %param.6), kind=kLoop, calls=%fused_computation.71 | loop fusion | flops 98288 | bytes 65600 | tf_op jit(solution)/shard_map/reduce_sum | solution.py:172
  1.8 3.0 %collective-permute-start = (f32[16]{0:T(128)S(1)}, f32[16]{0:T(128)S(1)}, u32[]{:S(2)}, u32[]{:S(2)}) collective-permute-start(f32[16]{0:T(128)S(1)} %fusion.27), channel_id=1, source_target_pairs={{0,1},{1,0},{2,3},{3,2},{4,5},{5,4},{6,7},{7,6},{8,9},{9,8},{10,11... | collective-permute-start | bytes 200 | tf_op jit(solution)/shard_map/ppermute | solution.py:28
  4.8 1.5 %collective-permute-done = f32[16]{0:T(128)S(1)} collective-permute-done((f32[16]{0:T(128)S(1)}, f32[16]{0:T(128)S(1)}, u32[]{:S(2)}, u32[]{:S(2)}) %collective-permute-start) | collective-permute-done | bytes 96 | tf_op jit(solution)/shard_map/ppermute | solution.py:28
  7.2 4.2 %collective-permute-start.3 = (bf16[16,2048]{1,0:T(8,128)(2,1)S(1)}, bf16[16,2048]{1,0:T(8,128)(2,1)S(1)}, u32[]{:S(2)}, u32[]{:S(2)}) collective-permute-start(bf16[16,2048]{1,0:T(8,128)(2,1)S(1)} %fusion.23), channel_id=1, source_target_pairs={{0,24},{2,26},{4,28},{6,30},{8,16},{10,18},{12,20},{14,22},{16,8},... | collective-permute-start | bytes 196616 | tf_op jit(solution)/shard_map/ppermute | solution.py:28
  12.1 2.3 %collective-permute-start.6 = (bf16[16,2048]{1,0:T(8,128)(2,1)}, bf16[16,2048]{1,0:T(8,128)(2,1)S(1)}, u32[]{:S(2)}, u32[]{:S(2)}) collective-permute-start(bf16[16,2048]{1,0:T(8,128)(2,1)} %param.7), channel_id=1, source_target_pairs={{0,16},{2,18},{4,20},{6,22},{8,24},{10,26},{12,28},{14,30},{16,0},... | collective-permute-start | bytes 196616 | tf_op jit(solution)/shard_map/ppermute | solution.py:28
  14.4 1.3 %collective-permute-done.2 = bf16[16,2048]{1,0:T(8,128)(2,1)S(1)} collective-permute-done((bf16[16,2048]{1,0:T(8,128)(2,1)S(1)}, bf16[16,2048]{1,0:T(8,128)(2,1)S(1)}, u32[]{:S(2)}, u32[]{:S(2)}) %collective-permute-start.2) | collective-permute-done | bytes 65568 | tf_op jit(solution)/shard_map/ppermute | solution.py:28
  15.7 1.6 %collective-permute-done.1 = bf16[16,2048]{1,0:T(8,128)(2,1)S(1)} collective-permute-done((bf16[16,2048]{1,0:T(8,128)(2,1)S(1)}, bf16[16,2048]{1,0:T(8,128)(2,1)S(1)}, u32[]{:S(2)}, u32[]{:S(2)}) %collective-permute-start.1) | collective-permute-done | bytes 65568 | tf_op jit(solution)/shard_map/ppermute | solution.py:28
  17.4 2.0 %collective-permute-done.6 = bf16[16,2048]{1,0:T(8,128)(2,1)S(1)} collective-permute-done((bf16[16,2048]{1,0:T(8,128)(2,1)}, bf16[16,2048]{1,0:T(8,128)(2,1)S(1)}, u32[]{:S(2)}, u32[]{:S(2)}) %collective-permute-start.6) | collective-permute-done | bytes 65568 | tf_op jit(solution)/shard_map/ppermute | solution.py:28
  20.4 1.6 %collective-permute-start.4 = (bf16[64,2048]{1,0:T(8,128)(2,1)S(1)}, bf16[64,2048]{1,0:T(8,128)(2,1)S(1)}, u32[]{:S(2)}, u32[]{:S(2)}) collective-permute-start(bf16[64,2048]{1,0:T(8,128)(2,1)S(1)} %pad_maximum_fusion.4), channel_id=1, source_target_pairs={{0,4},{2,6},{4,0},{6,2},{8,12},{10,14},{12,8},{14,10},{16,20},{18,... | collective-permute-start | bytes 786440 | tf_op jit(solution)/shard_map/ppermute | solution.py:28
  22.0 3.3 %collective-permute-done.7 = bf16[32,2048]{1,0:T(8,128)(2,1)S(1)} collective-permute-done((bf16[32,2048]{1,0:T(8,128)(2,1)S(1)}, bf16[32,2048]{1,0:T(8,128)(2,1)S(1)}, u32[]{:S(2)}, u32[]{:S(2)}) %collective-permute-start.7) | collective-permute-done | bytes 131104 | tf_op jit(solution)/shard_map/ppermute | solution.py:28
  25.3 1.7 %collective-permute-start.8 = (bf16[64,2048]{1,0:T(8,128)(2,1)S(1)}, bf16[64,2048]{1,0:T(8,128)(2,1)S(1)}, u32[]{:S(2)}, u32[]{:S(2)}) collective-permute-start(bf16[64,2048]{1,0:T(8,128)(2,1)S(1)} %pad_maximum_fusion.5), channel_id=1, source_target_pairs={{0,4},{2,6},{4,0},{6,2},{8,12},{10,14},{12,8},{14,10},{16,20},{18,... | collective-permute-start | bytes 786440 | tf_op jit(solution)/shard_map/ppermute | solution.py:28
  27.0 2.7 %collective-permute-done.4 = bf16[64,2048]{1,0:T(8,128)(2,1)S(1)} collective-permute-done((bf16[64,2048]{1,0:T(8,128)(2,1)S(1)}, bf16[64,2048]{1,0:T(8,128)(2,1)S(1)}, u32[]{:S(2)}, u32[]{:S(2)}) %collective-permute-start.4) | collective-permute-done | bytes 262176 | tf_op jit(solution)/shard_map/ppermute | solution.py:28
  29.7 2.7 %fusion.58 = f32[128,640]{1,0:T(8,128)S(1)} fusion(bf16[640,2048]{1,0:T(8,128)(2,1)} %param.9, bf16[64,2048]{1,0:T(8,128)(2,1)S(1)} %collective-permute-done.4, bf16[64,2048]{1,0:T(8,128)(2,1)S(1)} %pad_maximum_fusion.4), kind=kOutput, calls=%fused_computation.126 | convolution fusion | flops 336592896 | bytes 3473408 | tf_op jit(solution)/shard_map/dot_general | solution.py:73
  32.4 0.9 %fusion.57 = f32[128,640]{1,0:T(8,128)S(1)} fusion(bf16[640,2048]{1,0:T(8,128)(2,1)S(1)} %copy-done, bf16[64,2048]{1,0:T(8,128)(2,1)S(1)} %collective-permute-done.4, bf16[64,2048]{1,0:T(8,128)(2,1)S(1)} %pad_maximum_fusion.4), kind=kOutput, calls=%fused_computation.125 | convolution fusion | flops 336592896 | bytes 3473408 | tf_op jit(solution)/shard_map/dot_general | solution.py:73
  33.4 1.6 %collective-permute-start.10 = (bf16[256,640]{1,0:T(8,128)(2,1)S(1)}, bf16[256,640]{1,0:T(8,128)(2,1)S(1)}, u32[]{:S(2)}, u32[]{:S(2)}) collective-permute-start(bf16[256,640]{1,0:T(8,128)(2,1)S(1)} %fusion.2), channel_id=1, source_target_pairs={{0,1},{1,0},{2,3},{3,2},{4,5},{5,4},{6,7},{7,6},{8,9},{9,8},{10,11... | collective-permute-start | bytes 983048 | tf_op jit(solution)/shard_map/ppermute | solution.py:28
  35.8 1.2 %collective-permute-done.5.refs_4_.refs_5_ = bf16[128,2048]{1,0:T(8,128)(2,1)S(1)} collective-permute-done((bf16[128,2048]{1,0:T(8,128)(2,1)S(1)}, bf16[128,2048]{1,0:T(8,128)(2,1)S(1)}, u32[]{:S(2)}, u32[]{:S(2)}) %collective-permute-start.5) | collective-permute-done | bytes 524320 | tf_op jit(solution)/shard_map/ppermute | solution.py:28
  37.0 0.9 %fusion.69 = f32[128,640]{1,0:T(8,128)S(1)} fusion(bf16[128,2048]{1,0:T(8,128)(2,1)S(1)} %collective-permute-done.5.refs_4_.refs_5_, bf16[640,2048]{1,0:T(8,128)(2,1)S(1)} %copy-done.2), kind=kOutput, calls=%fused_computation.135 | convolution fusion | flops 335544320 | bytes 3473408 | tf_op jit(solution)/shard_map/dot_general | solution.py:73
  39.7 0.9 %fusion.61 = (bf16[128,640]{1,0:T(8,128)(2,1)S(1)}, f32[128,640]{1,0:T(8,128)S(1)}) fusion(pred[640]{0:T(1024)(128)(4,1)S(1)} %compare_reduce_fusion.8, bf16[128,2048]{1,0:T(8,128)(2,1)S(1)} %collective-permute-done.9.refs_3_, bf16[640,2048]{1,0:T(8,128)(2,1)S(1)} %copy-done.3), kind=kOutput, calls=%fused_computation.129 | convolution fusion | flops 335708160 | bytes 3637888 | tf_op jit(solution)/shard_map/dot_general | solution.py:73
  40.7 0.9 %fusion.68 = (bf16[128,640]{1,0:T(8,128)(2,1)S(1)}, f32[128,640]{1,0:T(8,128)S(1)}) fusion(bf16[640,2048]{1,0:T(8,128)(2,1)S(1)} %copy-done.3, bf16[64,2048]{1,0:T(8,128)(2,1)S(1)} %broadcast_select_fusion.1, bf16[32,2048]{1,0:T(8,128)(2,1)S(1)} %collective-permute-done.7, bf16[32,2048]{1,0:T(8,128)(2,1)S(1)} %maximum_select_fusion, ...), kind=kOutput, calls=%fused_computation.134 | convolution fusion | flops 337281024 | bytes 3637888 | tf_op jit(solution)/shard_map/dot_general | solution.py:73
  41.6 1.4 %collective-permute-start.15 = (bf16[128,640]{1,0:T(8,128)(2,1)S(1)}, bf16[128,640]{1,0:T(8,128)(2,1)S(1)}, u32[]{:S(2)}, u32[]{:S(2)}) collective-permute-start(bf16[128,640]{1,0:T(8,128)(2,1)S(1)} %get-tuple-element.80), channel_id=1, source_target_pairs={{0,1},{1,0},{2,3},{3,2},{4,5},{5,4},{6,7},{7,6},{8,9},{9,8},{10,11... | collective-permute-start | bytes 491528 | tf_op jit(solution)/shard_map/ppermute | solution.py:28
  44.1 5.5 %collective-permute-done.11 = bf16[256,640]{1,0:T(8,128)(2,1)S(1)} collective-permute-done((bf16[256,640]{1,0:T(8,128)(2,1)S(1)}, bf16[256,640]{1,0:T(8,128)(2,1)S(1)}, u32[]{:S(2)}, u32[]{:S(2)}) %collective-permute-start.11) | collective-permute-done | bytes 327712 | tf_op jit(solution)/shard_map/ppermute | solution.py:28
  50.6 3.6 %weight_grads.2 = (f32[640,2048]{1,0:T(8,128)}, f32[8,2048]{1,0:T(8,128)S(1)}) custom-call(bf16[128,640]{1,0:T(8,128)(2,1)S(1)} %get-tuple-element.25.refs_0_, bf16[128,640]{1,0:T(8,128)(2,1)S(1)} %get-tuple-element.26.refs_1_, bf16[128,2048]{1,0:T(8,128)(2,1)S(1)} %pad_maximum_fusion.3.refs_2_, bf16[128,2048]{1,0:T(8,128)(2,1)S(1)} %collective-permute-done.9.refs_3_, ...), custom_call_target="tpu_custom_call" | custom-call | flops 1000 | bytes 1000 | tf_op jit(solution)/shard_map/weight_grads/pallas_call | solution.py:104
  54.2 1.6 %collective-permute-done.14 = bf16[128,640]{1,0:T(8,128)(2,1)S(1)} collective-permute-done((bf16[128,640]{1,0:T(8,128)(2,1)S(1)}, bf16[128,640]{1,0:T(8,128)(2,1)S(1)}, u32[]{:S(2)}, u32[]{:S(2)}) %collective-permute-start.14) | collective-permute-done | bytes 163872 | tf_op jit(solution)/shard_map/ppermute | solution.py:28
  57.8 1.6 %collective-permute-start.13 = (bf16[64,2048]{1,0:T(8,128)(2,1)S(1)}, bf16[64,2048]{1,0:T(8,128)(2,1)S(1)}, u32[]{:S(2)}, u32[]{:S(2)}) collective-permute-start(bf16[64,2048]{1,0:T(8,128)(2,1)S(1)} %add_convert_fusion.1), channel_id=1, source_target_pairs={{0,4},{2,6},{4,0},{6,2},{8,12},{10,14},{12,8},{14,10},{16,20},{18,... | collective-permute-start | bytes 786440 | tf_op jit(solution)/shard_map/ppermute | solution.py:28
  62.9 1.6 %collective-permute-start.21 = (f32[1,2112]{1,0:T(1,128)S(1)}, f32[1,2112]{1,0:T(1,128)S(1)}, u32[]{:S(2)}, u32[]{:S(2)}) collective-permute-start(f32[1,2112]{1,0:T(1,128)S(1)} %get-tuple-element.67), channel_id=1, source_target_pairs={{0,4},{2,6},{4,0},{6,2},{8,12},{10,14},{12,8},{14,10},{16,20},{18,... | collective-permute-start | bytes 25352 | tf_op jit(solution)/shard_map/ppermute | solution.py:28
  65.7 1.3 %collective-permute-done.13.got_ref = bf16[64,2048]{1,0:T(8,128)(2,1)S(1)} collective-permute-done((bf16[64,2048]{1,0:T(8,128)(2,1)S(1)}, bf16[64,2048]{1,0:T(8,128)(2,1)S(1)}, u32[]{:S(2)}, u32[]{:S(2)}) %collective-permute-start.13) | collective-permute-done | bytes 262176 | tf_op jit(solution)/shard_map/ppermute | solution.py:28
  67.1 1.6 %collective-permute-start.17 = (bf16[32,2048]{1,0:T(8,128)(2,1)S(1)}, bf16[32,2048]{1,0:T(8,128)(2,1)S(1)}, u32[]{:S(2)}, u32[]{:S(2)}) collective-permute-start(bf16[32,2048]{1,0:T(8,128)(2,1)S(1)} %slice.321.refs_7_), channel_id=1, source_target_pairs={{0,8},{2,10},{4,12},{6,14},{8,0},{10,2},{12,4},{14,6},{16,24},{18,... | collective-permute-start | bytes 393224 | tf_op jit(solution)/shard_map/ppermute | solution.py:28
  68.7 4.8 %weight_grads.3 = (f32[640,2048]{1,0:T(8,128)}, f32[640,2048]{1,0:T(8,128)}, f32[8,2048]{1,0:T(8,128)S(1)}) custom-call(bf16[128,640]{1,0:T(8,128)(2,1)S(1)} %get-tuple-element.36.refs_0_, bf16[128,640]{1,0:T(8,128)(2,1)S(1)} %get-tuple-element.37.refs_1_, bf16[128,640]{1,0:T(8,128)(2,1)S(1)} %get-tuple-element.31.refs_2_, ...), custom_call_target="tpu_custom_call" | custom-call | flops 1000 | bytes 1000 | tf_op jit(solution)/shard_map/weight_grads/pallas_call | solution.py:104
  73.7 2.3 %collective-permute-start.18 = (bf16[16,2048]{1,0:T(8,128)(2,1)S(1)}, bf16[16,2048]{1,0:T(8,128)(2,1)S(1)}, u32[]{:S(2)}, u32[]{:S(2)}) collective-permute-start(bf16[16,2048]{1,0:T(8,128)(2,1)S(1)} %slice.322), channel_id=1, source_target_pairs={{0,16},{2,18},{4,20},{6,22},{8,24},{10,26},{12,28},{14,30},{16,0},... | collective-permute-start | bytes 196616 | tf_op jit(solution)/shard_map/ppermute | solution.py:28
  77.8 2.8 %collective-permute-start.25 = (bf16[16,2192]{1,0:T(8,128)(2,1)S(1)}, bf16[16,2192]{1,0:T(8,128)(2,1)S(1)}, u32[]{:S(2)}, u32[]{:S(2)}) collective-permute-start(bf16[16,2192]{1,0:T(8,128)(2,1)S(1)} %get-tuple-element.72), channel_id=1, source_target_pairs={{0,24},{2,26},{4,28},{6,30},{8,16},{10,18},{12,20},{14,22},{16,8},... | collective-permute-start | bytes 210440 | tf_op jit(solution)/shard_map/ppermute | solution.py:28
  81.4 2.5 %collective-permute-done.23 = bf16[16,2192]{1,0:T(8,128)(2,1)S(1)} collective-permute-done((bf16[16,2192]{1,0:T(8,128)(2,1)S(1)}, bf16[16,2192]{1,0:T(8,128)(2,1)S(1)}, u32[]{:S(2)}, u32[]{:S(2)}) %collective-permute-start.23) | collective-permute-done | bytes 70176 | tf_op jit(solution)/shard_map/ppermute | solution.py:28
  83.9 1.0 %collective-permute-done.25 = bf16[16,2192]{1,0:T(8,128)(2,1)S(1)} collective-permute-done((bf16[16,2192]{1,0:T(8,128)(2,1)S(1)}, bf16[16,2192]{1,0:T(8,128)(2,1)S(1)}, u32[]{:S(2)}, u32[]{:S(2)}) %collective-permute-start.25) | collective-permute-done | bytes 70176 | tf_op jit(solution)/shard_map/ppermute | solution.py:28
  (98 shorter events, 18.1 us)
Async XLA Ops:
  0.6 31.7 %copy-start = (bf16[640,2048]{1,0:T(8,128)(2,1)S(1)}, bf16[640,2048]{1,0:T(8,128)(2,1)}, u32[]{:S(2)}) copy-start(bf16[640,2048]{1,0:T(8,128)(2,1)} %param.10) | copy-start | bytes 7864324
  1.8 4.5 %collective-permute-start = (f32[16]{0:T(128)S(1)}, f32[16]{0:T(128)S(1)}, u32[]{:S(2)}, u32[]{:S(2)}) collective-permute-start(f32[16]{0:T(128)S(1)} %fusion.27), channel_id=1, source_target_pairs={{0,1},{1,0},{2,3},{3,2},{4,5},{5,4},{6,7},{7,6},{8,9},{9,8},{10,11... | collective-permute-start | bytes 200 | tf_op jit(solution)/shard_map/ppermute | solution.py:28
  7.2 7.1 %collective-permute-start.3 = (bf16[16,2048]{1,0:T(8,128)(2,1)S(1)}, bf16[16,2048]{1,0:T(8,128)(2,1)S(1)}, u32[]{:S(2)}, u32[]{:S(2)}) collective-permute-start(bf16[16,2048]{1,0:T(8,128)(2,1)S(1)} %fusion.23), channel_id=1, source_target_pairs={{0,24},{2,26},{4,28},{6,30},{8,16},{10,18},{12,20},{14,22},{16,8},... | collective-permute-start | bytes 196616 | tf_op jit(solution)/shard_map/ppermute | solution.py:28
  11.4 4.3 %collective-permute-start.2 = (bf16[16,2048]{1,0:T(8,128)(2,1)S(1)}, bf16[16,2048]{1,0:T(8,128)(2,1)S(1)}, u32[]{:S(2)}, u32[]{:S(2)}) collective-permute-start(bf16[16,2048]{1,0:T(8,128)(2,1)S(1)} %fusion.23), channel_id=1, source_target_pairs={{0,8},{2,10},{4,12},{6,14},{8,0},{10,2},{12,4},{14,6},{16,24},{18,... | collective-permute-start | bytes 196616 | tf_op jit(solution)/shard_map/ppermute | solution.py:28
  11.4 5.9 %collective-permute-start.1 = (bf16[16,2048]{1,0:T(8,128)(2,1)S(1)}, bf16[16,2048]{1,0:T(8,128)(2,1)S(1)}, u32[]{:S(2)}, u32[]{:S(2)}) collective-permute-start(bf16[16,2048]{1,0:T(8,128)(2,1)S(1)} %fusion.23), channel_id=1, source_target_pairs={{0,16},{2,18},{4,20},{6,22},{8,24},{10,26},{12,28},{14,30},{16,0},... | collective-permute-start | bytes 196616 | tf_op jit(solution)/shard_map/ppermute | solution.py:28
  12.1 7.4 %collective-permute-start.6 = (bf16[16,2048]{1,0:T(8,128)(2,1)}, bf16[16,2048]{1,0:T(8,128)(2,1)S(1)}, u32[]{:S(2)}, u32[]{:S(2)}) collective-permute-start(bf16[16,2048]{1,0:T(8,128)(2,1)} %param.7), channel_id=1, source_target_pairs={{0,16},{2,18},{4,20},{6,22},{8,24},{10,26},{12,28},{14,30},{16,0},... | collective-permute-start | bytes 196616 | tf_op jit(solution)/shard_map/ppermute | solution.py:28
  20.3 5.0 %collective-permute-start.7 = (bf16[32,2048]{1,0:T(8,128)(2,1)S(1)}, bf16[32,2048]{1,0:T(8,128)(2,1)S(1)}, u32[]{:S(2)}, u32[]{:S(2)}) collective-permute-start(bf16[32,2048]{1,0:T(8,128)(2,1)S(1)} %maximum_select_fusion), channel_id=1, source_target_pairs={{0,8},{2,10},{4,12},{6,14},{8,0},{10,2},{12,4},{14,6},{16,24},{18,... | collective-permute-start | bytes 393224 | tf_op jit(solution)/shard_map/ppermute | solution.py:28
  20.4 9.2 %collective-permute-start.4 = (bf16[64,2048]{1,0:T(8,128)(2,1)S(1)}, bf16[64,2048]{1,0:T(8,128)(2,1)S(1)}, u32[]{:S(2)}, u32[]{:S(2)}) collective-permute-start(bf16[64,2048]{1,0:T(8,128)(2,1)S(1)} %pad_maximum_fusion.4), channel_id=1, source_target_pairs={{0,4},{2,6},{4,0},{6,2},{8,12},{10,14},{12,8},{14,10},{16,20},{18,... | collective-permute-start | bytes 786440 | tf_op jit(solution)/shard_map/ppermute | solution.py:28
  25.3 9.8 %collective-permute-start.8 = (bf16[64,2048]{1,0:T(8,128)(2,1)S(1)}, bf16[64,2048]{1,0:T(8,128)(2,1)S(1)}, u32[]{:S(2)}, u32[]{:S(2)}) collective-permute-start(bf16[64,2048]{1,0:T(8,128)(2,1)S(1)} %pad_maximum_fusion.5), channel_id=1, source_target_pairs={{0,4},{2,6},{4,0},{6,2},{8,12},{10,14},{12,8},{14,10},{16,20},{18,... | collective-permute-start | bytes 786440 | tf_op jit(solution)/shard_map/ppermute | solution.py:28
  33.3 3.7 %copy-start.2 = (bf16[640,2048]{1,0:T(8,128)(2,1)S(1)}, bf16[640,2048]{1,0:T(8,128)(2,1)}, u32[]{:S(2)}) copy-start(bf16[640,2048]{1,0:T(8,128)(2,1)} %param.9) | copy-start | bytes 7864324
  33.4 10.4 %collective-permute-start.10 = (bf16[256,640]{1,0:T(8,128)(2,1)S(1)}, bf16[256,640]{1,0:T(8,128)(2,1)S(1)}, u32[]{:S(2)}, u32[]{:S(2)}) collective-permute-start(bf16[256,640]{1,0:T(8,128)(2,1)S(1)} %fusion.2), channel_id=1, source_target_pairs={{0,1},{1,0},{2,3},{3,2},{4,5},{5,4},{6,7},{7,6},{8,9},{9,8},{10,11... | collective-permute-start | bytes 983048 | tf_op jit(solution)/shard_map/ppermute | solution.py:28
  35.1 2.0 %collective-permute-start.5 = (bf16[128,2048]{1,0:T(8,128)(2,1)S(1)}, bf16[128,2048]{1,0:T(8,128)(2,1)S(1)}, u32[]{:S(2)}, u32[]{:S(2)}) collective-permute-start(bf16[128,2048]{1,0:T(8,128)(2,1)S(1)} %pad_maximum_fusion.2.refs_3_.refs_4_), channel_id=1, source_target_pairs={{0,2},{2,0},{4,6},{6,4},{8,10},{10,8},{12,14},{14,12},{16,18},{18,... | collective-permute-start | bytes 1572872 | tf_op jit(solution)/shard_map/ppermute | solution.py:28
  35.2 4.3 %collective-permute-start.9 = (bf16[128,2048]{1,0:T(8,128)(2,1)S(1)}, bf16[128,2048]{1,0:T(8,128)(2,1)S(1)}, u32[]{:S(2)}, u32[]{:S(2)}) collective-permute-start(bf16[128,2048]{1,0:T(8,128)(2,1)S(1)} %pad_maximum_fusion.3.refs_2_), channel_id=1, source_target_pairs={{0,2},{2,0},{4,6},{6,4},{8,10},{10,8},{12,14},{14,12},{16,18},{18,... | collective-permute-start | bytes 1572872 | tf_op jit(solution)/shard_map/ppermute | solution.py:28
  38.0 1.7 %copy-start.3 = (bf16[640,2048]{1,0:T(8,128)(2,1)S(1)}, bf16[640,2048]{1,0:T(8,128)(2,1)}, u32[]{:S(2)}) copy-start(bf16[640,2048]{1,0:T(8,128)(2,1)} %param.11) | copy-start | bytes 7864324
  39.0 10.6 %collective-permute-start.11 = (bf16[256,640]{1,0:T(8,128)(2,1)S(1)}, bf16[256,640]{1,0:T(8,128)(2,1)S(1)}, u32[]{:S(2)}, u32[]{:S(2)}) collective-permute-start(bf16[256,640]{1,0:T(8,128)(2,1)S(1)} %fusion.1), channel_id=1, source_target_pairs={{0,1},{1,0},{2,3},{3,2},{4,5},{5,4},{6,7},{7,6},{8,9},{9,8},{10,11... | collective-permute-start | bytes 983048 | tf_op jit(solution)/shard_map/ppermute | solution.py:28
  41.6 17.8 %collective-permute-start.15 = (bf16[128,640]{1,0:T(8,128)(2,1)S(1)}, bf16[128,640]{1,0:T(8,128)(2,1)S(1)}, u32[]{:S(2)}, u32[]{:S(2)}) collective-permute-start(bf16[128,640]{1,0:T(8,128)(2,1)S(1)} %get-tuple-element.80), channel_id=1, source_target_pairs={{0,1},{1,0},{2,3},{3,2},{4,5},{5,4},{6,7},{7,6},{8,9},{9,8},{10,11... | collective-permute-start | bytes 491528 | tf_op jit(solution)/shard_map/ppermute | solution.py:28
  43.1 12.7 %collective-permute-start.14 = (bf16[128,640]{1,0:T(8,128)(2,1)S(1)}, bf16[128,640]{1,0:T(8,128)(2,1)S(1)}, u32[]{:S(2)}, u32[]{:S(2)}) collective-permute-start(bf16[128,640]{1,0:T(8,128)(2,1)S(1)} %get-tuple-element.48), channel_id=1, source_target_pairs={{0,1},{1,0},{2,3},{3,2},{4,5},{5,4},{6,7},{7,6},{8,9},{9,8},{10,11... | collective-permute-start | bytes 491528 | tf_op jit(solution)/shard_map/ppermute | solution.py:28
  50.5 6.7 %collective-permute-start.12 = (bf16[128,2048]{1,0:T(8,128)(2,1)S(1)}, bf16[128,2048]{1,0:T(8,128)(2,1)S(1)}, u32[]{:S(2)}, u32[]{:S(2)}) collective-permute-start(bf16[128,2048]{1,0:T(8,128)(2,1)S(1)} %convolution_convert_fusion.refs_4_), channel_id=1, source_target_pairs={{0,2},{2,0},{4,6},{6,4},{8,10},{10,8},{12,14},{14,12},{16,18},{18,... | collective-permute-start | bytes 1572872 | tf_op jit(solution)/shard_map/ppermute | solution.py:28
  57.1 3.1 %collective-permute-start.16 = (bf16[128,2048]{1,0:T(8,128)(2,1)S(1)}, bf16[128,2048]{1,0:T(8,128)(2,1)S(1)}, u32[]{:S(2)}, u32[]{:S(2)}) collective-permute-start(bf16[128,2048]{1,0:T(8,128)(2,1)S(1)} %fusion.refs_2_), channel_id=1, source_target_pairs={{0,2},{2,0},{4,6},{6,4},{8,10},{10,8},{12,14},{14,12},{16,18},{18,... | collective-permute-start | bytes 1572872 | tf_op jit(solution)/shard_map/ppermute | solution.py:28
  57.8 9.2 %collective-permute-start.13 = (bf16[64,2048]{1,0:T(8,128)(2,1)S(1)}, bf16[64,2048]{1,0:T(8,128)(2,1)S(1)}, u32[]{:S(2)}, u32[]{:S(2)}) collective-permute-start(bf16[64,2048]{1,0:T(8,128)(2,1)S(1)} %add_convert_fusion.1), channel_id=1, source_target_pairs={{0,4},{2,6},{4,0},{6,2},{8,12},{10,14},{12,8},{14,10},{16,20},{18,... | collective-permute-start | bytes 786440 | tf_op jit(solution)/shard_map/ppermute | solution.py:28
  60.9 12.7 %collective-permute-start.19 = (bf16[64,2048]{1,0:T(8,128)(2,1)S(1)}, bf16[64,2048]{1,0:T(8,128)(2,1)S(1)}, u32[]{:S(2)}, u32[]{:S(2)}) collective-permute-start(bf16[64,2048]{1,0:T(8,128)(2,1)S(1)} %get-tuple-element.82), channel_id=1, source_target_pairs={{0,4},{2,6},{4,0},{6,2},{8,12},{10,14},{12,8},{14,10},{16,20},{18,... | collective-permute-start | bytes 786440 | tf_op jit(solution)/shard_map/ppermute | solution.py:28
  62.0 0.7 copy-start.1
  62.9 10.5 %collective-permute-start.21 = (f32[1,2112]{1,0:T(1,128)S(1)}, f32[1,2112]{1,0:T(1,128)S(1)}, u32[]{:S(2)}, u32[]{:S(2)}) collective-permute-start(f32[1,2112]{1,0:T(1,128)S(1)} %get-tuple-element.67), channel_id=1, source_target_pairs={{0,4},{2,6},{4,0},{6,2},{8,12},{10,14},{12,8},{14,10},{16,20},{18,... | collective-permute-start | bytes 25352 | tf_op jit(solution)/shard_map/ppermute | solution.py:28
  64.5 9.0 %collective-permute-start.22 = (f32[1,2112]{1,0:T(1,128)S(1)}, f32[1,2112]{1,0:T(1,128)S(1)}, u32[]{:S(2)}, u32[]{:S(2)}) collective-permute-start(f32[1,2112]{1,0:T(1,128)S(1)} %get-tuple-element.68), channel_id=1, source_target_pairs={{0,6},{2,4},{4,2},{6,0},{8,14},{10,12},{12,10},{14,8},{16,22},{18,... | collective-permute-start | bytes 25352 | tf_op jit(solution)/shard_map/ppermute | solution.py:28
  64.5 9.0 %collective-permute-start.20 = (f32[1,2112]{1,0:T(1,128)S(1)}, f32[1,2112]{1,0:T(1,128)S(1)}, u32[]{:S(2)}, u32[]{:S(2)}) collective-permute-start(f32[1,2112]{1,0:T(1,128)S(1)} %get-tuple-element.69), channel_id=1, source_target_pairs={{0,2},{2,0},{4,6},{6,4},{8,10},{10,8},{12,14},{14,12},{16,18},{18,... | collective-permute-start | bytes 25352 | tf_op jit(solution)/shard_map/ppermute | solution.py:28
  67.1 6.5 %collective-permute-start.17 = (bf16[32,2048]{1,0:T(8,128)(2,1)S(1)}, bf16[32,2048]{1,0:T(8,128)(2,1)S(1)}, u32[]{:S(2)}, u32[]{:S(2)}) collective-permute-start(bf16[32,2048]{1,0:T(8,128)(2,1)S(1)} %slice.321.refs_7_), channel_id=1, source_target_pairs={{0,8},{2,10},{4,12},{6,14},{8,0},{10,2},{12,4},{14,6},{16,24},{18,... | collective-permute-start | bytes 393224 | tf_op jit(solution)/shard_map/ppermute | solution.py:28
  73.5 12.0 %copy-start.4 = (bf16[16,2048]{1,0:T(8,128)(2,1)S(1)}, bf16[16,2048]{1,0:T(8,128)(2,1)}, u32[]{:S(2)}) copy-start(bf16[16,2048]{1,0:T(8,128)(2,1)} %param.6) | copy-start | bytes 196612
  73.7 7.1 %collective-permute-start.18 = (bf16[16,2048]{1,0:T(8,128)(2,1)S(1)}, bf16[16,2048]{1,0:T(8,128)(2,1)S(1)}, u32[]{:S(2)}, u32[]{:S(2)}) collective-permute-start(bf16[16,2048]{1,0:T(8,128)(2,1)S(1)} %slice.322), channel_id=1, source_target_pairs={{0,16},{2,18},{4,20},{6,22},{8,24},{10,26},{12,28},{14,30},{16,0},... | collective-permute-start | bytes 196616 | tf_op jit(solution)/shard_map/ppermute | solution.py:28
  76.2 7.7 %collective-permute-start.23 = (bf16[16,2192]{1,0:T(8,128)(2,1)S(1)}, bf16[16,2192]{1,0:T(8,128)(2,1)S(1)}, u32[]{:S(2)}, u32[]{:S(2)}) collective-permute-start(bf16[16,2192]{1,0:T(8,128)(2,1)S(1)} %get-tuple-element.70), channel_id=1, source_target_pairs={{0,16},{2,18},{4,20},{6,22},{8,24},{10,26},{12,28},{14,30},{16,0},... | collective-permute-start | bytes 210440 | tf_op jit(solution)/shard_map/ppermute | solution.py:28
  77.0 6.9 %collective-permute-start.24 = (bf16[16,2192]{1,0:T(8,128)(2,1)S(1)}, bf16[16,2192]{1,0:T(8,128)(2,1)S(1)}, u32[]{:S(2)}, u32[]{:S(2)}) collective-permute-start(bf16[16,2192]{1,0:T(8,128)(2,1)S(1)} %get-tuple-element.71), channel_id=1, source_target_pairs={{0,8},{2,10},{4,12},{6,14},{8,0},{10,2},{12,4},{14,6},{16,24},{18,... | collective-permute-start | bytes 210440 | tf_op jit(solution)/shard_map/ppermute | solution.py:28
  77.8 7.1 %collective-permute-start.25 = (bf16[16,2192]{1,0:T(8,128)(2,1)S(1)}, bf16[16,2192]{1,0:T(8,128)(2,1)S(1)}, u32[]{:S(2)}, u32[]{:S(2)}) collective-permute-start(bf16[16,2192]{1,0:T(8,128)(2,1)S(1)} %get-tuple-element.72), channel_id=1, source_target_pairs={{0,24},{2,26},{4,28},{6,30},{8,16},{10,18},{12,20},{14,22},{16,8},... | collective-permute-start | bytes 210440 | tf_op jit(solution)/shard_map/ppermute | solution.py:28

commit v2 on v1

--- a/solution.py
+++ b/solution.py
@@ -57,16 +57,14 @@
 def gather_rows(rows, dp):
     for parts in reversed(direct_steps(dp)):
         rows = jnp.concatenate([rows] + [swap(rows, "dp", dp, d) for d in parts], axis=0)
-    rows = lax.optimization_barrier(rows)
-    return jnp.concatenate([rows, swap(rows, "dp", dp, 2)], axis=0), rows
-
-
-def gather_rows_behind(rows, dp, behind, used_behind):
-    for place, distance in enumerate(reversed(halving_distances(dp))):
-        if place == 1:
-            rows = after(rows, behind)
+    return jnp.concatenate([rows, swap(rows, "dp", dp, 2)], axis=0)
+
+
+def gather_rows_behind(rows, dp, used_behind):
+    for distance in reversed(halving_distances(dp)):
         rows = jnp.concatenate([rows, swap(rows, "dp", dp, distance)], axis=0)
-    return jnp.concatenate([rows, after(swap(rows, "dp", dp, 2), used_behind)], axis=0)
+    got = swap(rows, "dp", dp, 2)
+    return jnp.concatenate([rows, after(got, used_behind)], axis=0)
 
 
 def inward(rows, weight):
@@ -96,7 +94,7 @@
         )
 
 
-def weight_grads(count, rows, inputs, behind):
+def weight_grads(count, rows, inputs, behind, bytes_accessed):
     units, width = rows[0].shape[1], inputs[0].shape[1]
     block = min(width, 512)
     whole = lambda a: pl.BlockSpec(a.shape, lambda i: (0, 0))
@@ -113,7 +111,7 @@
         + [jax.ShapeDtypeStruct((8, width), F32)],
         scratch_shapes=[pltpu.VMEM((count * units, 2 * rows[0].shape[0]), BF16)],
         compiler_params=pltpu.CompilerParams(vmem_limit_bytes=20 * 2**20),
-        cost_estimate=pl.CostEstimate(flops=1000, bytes_accessed=1000, transcendentals=0),
+        cost_estimate=pl.CostEstimate(flops=1, bytes_accessed=bytes_accessed, transcendentals=0),
         name="weight_grads",
     )(*rows, *inputs, *behind)
 
@@ -177,7 +175,7 @@
     inv_rms = lax.rsqrt(square_sum / features + EPSILON)[:, None]
     scaled = widened * inv_rms
     normed_rows = (scaled * norm_gain).astype(BF16)
-    own_n, sent_n = gather_rows(normed_rows, dp)
+    own_n = gather_rows(normed_rows, dp)
     size = own_n.shape[0] // 2
     other_n = swap(own_n, "dp", dp, 1)
 
@@ -185,14 +183,13 @@
         return jnp.concatenate([inward(rows, gate_weight), inward(rows, up_weight)], axis=0)
 
     own_p = project(own_n)
-    own_c = gather_rows_behind(cotangent, dp, sent_n, own_p)
+    other_p = project(other_n)
+    own_c = gather_rows_behind(cotangent, dp, own_p[2 * size :])
     other_c = swap(own_c, "dp", dp, 1)
-    other_p = project(other_n)
     other_b = after(inward(other_c, down_weight), other_p)
     own_b = after(inward(own_c, down_weight), other_b)
     own_p = after(node_sum(own_p, node), own_b)
-    other_p, other_b = node_sum(other_p, node), node_sum(other_b, node)
-    own_b = node_sum(own_b, node)
+    other_p, own_b = node_sum(other_p, node), node_sum(own_b, node)
 
     def activate(both):
         gate_value, up_value = both[: 2 * size], both[2 * size :]
@@ -217,9 +214,12 @@
     branch_sent = outward(own_h[size:], down_weight) + got_h[size:].astype(F32)
     branch_sent = lax.optimization_barrier(branch_sent.astype(BF16))
     branch = outward(own_h[:size], down_weight) + got_h[:size].astype(F32)
-    grad_down_weight, mark = weight_grads(1, (own_h, other_h), (own_c, other_c), (sent_h,))
-
-    other_g, other_r = grads(after(other_b, mark), *other_f)
+    bit = 1
+    while bit < node:
+        got = swap(other_b.astype(BF16), "node", node, bit)
+        other_b = add_got(other_b, got, 40_000_000, (sent_h,))
+        bit *= 2
+    other_g, other_r = grads(other_b, *other_f)
     sent_g = outward_pair(other_g).astype(BF16)
     got_g = swap(sent_g, "dp", dp, 1)
     own_b = after(after(own_b, branch_sent), sent_g)
@@ -238,44 +238,49 @@
         vector(2, gain_part, own_r[:, size:]),
         vector(3, gain_part, other_r[:, size:]),
     ]
-    branch = add_got(branch, swap(branch_sent, "dp", dp, 2), 40_000_000, (gain_part,))
-    distances = halving_distances(dp)
-    half = branch.shape[0] // 2
-    sent_h = lax.optimization_barrier(branch[half:].astype(BF16))
-    grad_gate_weight, grad_up_weight, mark = weight_grads(
-        2, (*own_g, *other_g), (own_n, other_n), (gain_part, sent_h)
+    grad_down_weight, mark = weight_grads(
+        1, (own_h, other_h), (own_c, other_c), (gain_part,), 1_000
     )
-    for distance in distances[1:]:
-        branch = branch[:half] + swap(sent_h, "dp", dp, distances[0]).astype(F32)
-        distances, half = distances[1:], half // 2
-        sent_h = lax.optimization_barrier(branch[half:].astype(BF16))
-    branch = branch[:half] + swap(sent_h, "dp", dp, distances[0]).astype(F32)
+    branch = add_got(branch, swap(branch_sent, "dp", dp, 2), 40_000_000, (mark,))
+    sent_h = lax.optimization_barrier(branch[branch.shape[0] // 2 :].astype(BF16))
 
     normed = normed_own + got_g[:size].astype(F32)
     normed = add_got(normed, swap(normed_sent, "dp", dp, 2), 40_000_000, (mark,))
     normed = after(normed, sent_h)
-    vectors = jnp.concatenate([after(gain_part, mark), own_r[:, :size]], axis=1)
+    vectors = jnp.concatenate([after(gain_part, normed), own_r[:, :size]], axis=1)
     vectors = vectors + (got_v[0] + got_v[1] + got_v[2])
-    gain_part, rows = after(vectors[:, :width], normed), after(vectors[:, width:], normed)
+    gain_part, rows = vectors[:, :width], vectors[:, width:]
     for parts in direct_steps(dp):
         count = normed.shape[0] // (len(parts) + 1)
         extra = gain_part.reshape(count, -1)
         lanes = extra.shape[1]
-        joined = [
-            jnp.concatenate(
-                [normed[place * count : (place + 1) * count], extra]
-                + [jnp.pad(rows[:, place * count : (place + 1) * count], ((0, count - 1), (0, 0)))],
-                axis=1,
+
+        def joined(place):
+            own_rows = rows[:, place * count : (place + 1) * count]
+            return [
+                normed[place * count : (place + 1) * count],
+                extra,
+                jnp.pad(own_rows, ((0, count - 1), (0, 0))),
+            ]
+
+        sent = [jnp.concatenate(joined(k + 1), axis=1).astype(BF16) for k in range(len(parts))]
+        for place, distance in enumerate(sorted(parts)[:2]):
+            half = branch.shape[0] // 2
+            if place:
+                sent_h = after(branch[half:].astype(BF16), sent[0])
+            branch = branch[:half] + swap(sent_h, "dp", dp, distance).astype(F32)
+        if branch.shape[0] == count and count == tokens.shape[0]:
+            grad_gate_weight, grad_up_weight, sent_h = weight_grads(
+                2, (*own_g, *other_g), (own_n, other_n), (sent[-1], sent_h), 60_000_000
             )
-            for place in range(len(parts) + 1)
-        ]
-        total = joined[0]
-        for place, distance in enumerate(parts):
-            sent = joined[place + 1].astype(BF16)
-            total = total + swap(sent, "dp", dp, distance).astype(F32)
+        kept, *others = joined(0)
+        total = jnp.concatenate([after(kept, sent_h), *others], axis=1)
+        for part, distance in zip(sent, parts):
+            total = total + swap(part, "dp", dp, distance).astype(F32)
         normed = total[:, :width]
         gain_part = total[:, width : width + lanes].reshape(1, width)
         rows = total[:1, width + lanes :]
+        sent_h = branch[branch.shape[0] // 2 :].astype(BF16)
 
     row_mean = (rows / features).reshape(-1, 1)
     grad_scaled = normed * norm_gain

time: 86.6 us -> 81 us (0.935)
  starting transfers between devices: 31.2 us -> 28.5 us
  waiting for transfers between devices: 25.7 us -> 23.8 us
  matrix products: 12.6 us -> 10.9 us
    ppermute x26, starting transfers between devices: 31.2 us -> 28.5 us  [swap(): return lax.ppermute(value, axis, [(i, i ^ distance) for i in range(size)])]
    ppermute x26, waiting for transfers between devices: 25.7 us -> 23.8 us  [swap(): return lax.ppermute(value, axis, [(i, i ^ distance) for i in range(size)])]
    dot_general x6, matrix products: 7.33 us -> 5.61 us  [inward(): lax.dot_general(rows, weight, (((1,), (1,)), ((), ())), preferred_element...]
    concatenate x1 -> x2, other arithmetic: 0.02 us -> 1.71 us  [gather_rows_behind(): rows = jnp.concatenate([rows, swap(rows, 'dp', dp, distance)], axis=0)]
    unnamed x0 -> x1, other arithmetic: none -> 0.94 us
    convert_element_type x1 -> x0, other arithmetic: 0.93 us -> none  [on_device(): normed_rows = (scaled * norm_gain).astype(BF16)]
  transfers between devices with their start and end apart: 26 -> 26, of which waited for: 13 -> 8; matrix products, arithmetic and copies ran while one was open for 17% -> 21% of each run, Pallas kernels for 10% -> 11%
where the time goes in v2:
time: 81 us; the launch traced here: 80.7 us
  starting transfers between devices  28.5 us (35%)
  waiting for transfers between devices  23.8 us (29%)
  matrix products  10.9 us (13%)
  Pallas kernels  8.55 us (11%)
  other arithmetic  6.84 us (8%)
  between operations  1.14 us (1%)
  local copies, waits for them, and re-layouts  0.95 us (1%)
    ppermute x26, starting transfers between devices, swap(): return lax.ppermute(value, axis, [(i, i ^ distance) for i in range(size)])  28.5 us
    ppermute x26, waiting for transfers between devices, swap(): return lax.ppermute(value, axis, [(i, i ^ distance) for i in range(size)])  23.8 us
    pallas_call x2, Pallas kernels, weight_grads(): pl.pallas_call(functools.partial(grad_kernel, count), grid=(width // bloc...  8.2 us
    dot_general x6, matrix products, inward(): lax.dot_general(rows, weight, (((1,), (1,)), ((), ())), preferred_element...  5.61 us
    dot_general x9, matrix products, outward(): lax.dot_general(rows, weight, (((1,), (0,)), ((), ())), preferred_element...  5.28 us
    concatenate x2, other arithmetic, gather_rows_behind(): rows = jnp.concatenate([rows, swap(rows, 'dp', dp, distance)], axis=0)  1.71 us
  transfers between devices with their start and end apart: 26, of which 8 were waited for; matrix products, arithmetic and copies ran while one was open for 21% of the time, Pallas kernels for 11%

profile of v2, /device:TPU:0, one launch (start us, length us, event | category | flops | bytes accessed | tf_op | source)
XLA Modules:
  0.0 80.7 jit_solution(8980345685908103691)
XLA Ops:
  0.6 1.1 %fusion.27 = f32[16]{0:T(128)S(1)} fusion(bf16[16,2048]{1,0:T(8,128)(2,1)} %param.6), kind=kLoop, calls=%fused_computation.69 | loop fusion | flops 98288 | bytes 65600 | tf_op jit(solution)/shard_map/reduce_sum | solution.py:170
  1.8 3.0 %collective-permute-start = (f32[16]{0:T(128)S(1)}, f32[16]{0:T(128)S(1)}, u32[]{:S(2)}, u32[]{:S(2)}) collective-permute-start(f32[16]{0:T(128)S(1)} %fusion.27), channel_id=1, source_target_pairs={{0,1},{1,0},{2,3},{3,2},{4,5},{5,4},{6,7},{7,6},{8,9},{9,8},{10,11... | collective-permute-start | bytes 200 | tf_op jit(solution)/shard_map/ppermute | solution.py:28
  4.8 2.6 %collective-permute-start.6 = (bf16[16,2048]{1,0:T(8,128)(2,1)}, bf16[16,2048]{1,0:T(8,128)(2,1)S(1)}, u32[]{:S(2)}, u32[]{:S(2)}) collective-permute-start(bf16[16,2048]{1,0:T(8,128)(2,1)} %param.7), channel_id=1, source_target_pairs={{0,16},{2,18},{4,20},{6,22},{8,24},{10,26},{12,28},{14,30},{16,0},... | collective-permute-start | bytes 196616 | tf_op jit(solution)/shard_map/ppermute | solution.py:28
  7.4 0.9 %constant_dynamic-update-slice_fusion.4 = (bf16[128,2048]{1,0:T(8,128)(2,1)S(1)}, bf16[16,2048]{1,0:T(8,128)(2,1)S(1)}) fusion(f32[2048]{0:T(1024)} %param.8, f32[16]{0:T(128)S(1)} %add_rsqrt_fusion, bf16[16,2048]{1,0:T(8,128)(2,1)} %param.6), kind=kLoop, calls=%fused_computation.109 | loop fusion | flops 131071 | bytes 204864
  8.3 2.1 %collective-permute-start.1 = (bf16[16,2048]{1,0:T(8,128)(2,1)S(1)}, bf16[16,2048]{1,0:T(8,128)(2,1)S(1)}, u32[]{:S(2)}, u32[]{:S(2)}) collective-permute-start(bf16[16,2048]{1,0:T(8,128)(2,1)S(1)} %get-tuple-element.55), channel_id=1, source_target_pairs={{0,16},{2,18},{4,20},{6,22},{8,24},{10,26},{12,28},{14,30},{16,0},... | collective-permute-start | bytes 196616 | tf_op jit(solution)/shard_map/ppermute | solution.py:28
  10.4 1.6 %collective-permute-start.2 = (bf16[16,2048]{1,0:T(8,128)(2,1)S(1)}, bf16[16,2048]{1,0:T(8,128)(2,1)S(1)}, u32[]{:S(2)}, u32[]{:S(2)}) collective-permute-start(bf16[16,2048]{1,0:T(8,128)(2,1)S(1)} %get-tuple-element.55), channel_id=1, source_target_pairs={{0,8},{2,10},{4,12},{6,14},{8,0},{10,2},{12,4},{14,6},{16,24},{18,... | collective-permute-start | bytes 196616 | tf_op jit(solution)/shard_map/ppermute | solution.py:28
  14.4 1.1 %collective-permute-done.1 = bf16[16,2048]{1,0:T(8,128)(2,1)S(1)} collective-permute-done((bf16[16,2048]{1,0:T(8,128)(2,1)S(1)}, bf16[16,2048]{1,0:T(8,128)(2,1)S(1)}, u32[]{:S(2)}, u32[]{:S(2)}) %collective-permute-start.1) | collective-permute-done | bytes 65568 | tf_op jit(solution)/shard_map/ppermute | solution.py:28
  15.5 2.7 %collective-permute-done.3 = bf16[16,2048]{1,0:T(8,128)(2,1)S(1)} collective-permute-done((bf16[16,2048]{1,0:T(8,128)(2,1)S(1)}, bf16[16,2048]{1,0:T(8,128)(2,1)S(1)}, u32[]{:S(2)}, u32[]{:S(2)}) %collective-permute-start.3) | collective-permute-done | bytes 65568 | tf_op jit(solution)/shard_map/ppermute | solution.py:28
  18.2 1.6 %collective-permute-start.4 = (bf16[64,2048]{1,0:T(8,128)(2,1)S(1)}, bf16[64,2048]{1,0:T(8,128)(2,1)S(1)}, u32[]{:S(2)}, u32[]{:S(2)}) collective-permute-start(bf16[64,2048]{1,0:T(8,128)(2,1)S(1)} %pad_maximum_fusion.3), channel_id=1, source_target_pairs={{0,4},{2,6},{4,0},{6,2},{8,12},{10,14},{12,8},{14,10},{16,20},{18,... | collective-permute-start | bytes 786440 | tf_op jit(solution)/shard_map/ppermute | solution.py:28
  20.7 1.1 %collective-permute-start.8 = (bf16[64,2048]{1,0:T(8,128)(2,1)S(1)}, bf16[64,2048]{1,0:T(8,128)(2,1)S(1)}, u32[]{:S(2)}, u32[]{:S(2)}) collective-permute-start(bf16[64,2048]{1,0:T(8,128)(2,1)S(1)} %pad_maximum_fusion.4), channel_id=1, source_target_pairs={{0,4},{2,6},{4,0},{6,2},{8,12},{10,14},{12,8},{14,10},{16,20},{18,... | collective-permute-start | bytes 786440 | tf_op jit(solution)/shard_map/ppermute | solution.py:28
  21.8 5.0 %collective-permute-done.4 = bf16[64,2048]{1,0:T(8,128)(2,1)S(1)} collective-permute-done((bf16[64,2048]{1,0:T(8,128)(2,1)S(1)}, bf16[64,2048]{1,0:T(8,128)(2,1)S(1)}, u32[]{:S(2)}, u32[]{:S(2)}) %collective-permute-start.4) | collective-permute-done | bytes 262176 | tf_op jit(solution)/shard_map/ppermute | solution.py:28
  26.9 0.9 %fusion.70 = f32[128,640]{1,0:T(8,128)S(1)} fusion(bf16[128,2048]{1,0:T(8,128)(2,1)S(1)} %constant_dynamic-update-slice_fusion.refs_3_.refs_4_, bf16[640,2048]{1,0:T(8,128)(2,1)S(1)} %copy-done), kind=kOutput, calls=%fused_computation.137 | convolution fusion | flops 335544320 | bytes 3473408 | tf_op jit(solution)/shard_map/dot_general | solution.py:71
  27.9 0.9 %fusion.71 = f32[128,640]{1,0:T(8,128)S(1)} fusion(bf16[128,2048]{1,0:T(8,128)(2,1)S(1)} %constant_dynamic-update-slice_fusion.refs_3_.refs_4_, bf16[640,2048]{1,0:T(8,128)(2,1)S(1)} %copy-done.2), kind=kOutput, calls=%fused_computation.138 | convolution fusion | flops 335544320 | bytes 3473408 | tf_op jit(solution)/shard_map/dot_general | solution.py:71
  28.9 1.2 %collective-permute-start.10 = (bf16[256,640]{1,0:T(8,128)(2,1)S(1)}, bf16[256,640]{1,0:T(8,128)(2,1)S(1)}, u32[]{:S(2)}, u32[]{:S(2)}) collective-permute-start(bf16[256,640]{1,0:T(8,128)(2,1)S(1)} %fusion.2), channel_id=1, source_target_pairs={{0,1},{1,0},{2,3},{3,2},{4,5},{5,4},{6,7},{7,6},{8,9},{9,8},{10,11... | collective-permute-start | bytes 983048 | tf_op jit(solution)/shard_map/ppermute | solution.py:28
  30.4 0.9 %fusion.72 = f32[128,640]{1,0:T(8,128)S(1)} fusion(bf16[128,2048]{1,0:T(8,128)(2,1)S(1)} %collective-permute-done.5.refs_4_.refs_5_, bf16[640,2048]{1,0:T(8,128)(2,1)S(1)} %copy-done), kind=kOutput, calls=%fused_computation.139 | convolution fusion | flops 335544320 | bytes 3473408 | tf_op jit(solution)/shard_map/dot_general | solution.py:71
  31.4 0.9 %fusion.69 = f32[128,640]{1,0:T(8,128)S(1)} fusion(bf16[128,2048]{1,0:T(8,128)(2,1)S(1)} %collective-permute-done.5.refs_4_.refs_5_, bf16[640,2048]{1,0:T(8,128)(2,1)S(1)} %copy-done.2), kind=kOutput, calls=%fused_computation.136 | convolution fusion | flops 335544320 | bytes 3473408 | tf_op jit(solution)/shard_map/dot_general | solution.py:71
  32.4 1.0 %collective-permute-start.11 = (bf16[256,640]{1,0:T(8,128)(2,1)S(1)}, bf16[256,640]{1,0:T(8,128)(2,1)S(1)}, u32[]{:S(2)}, u32[]{:S(2)}) collective-permute-start(bf16[256,640]{1,0:T(8,128)(2,1)S(1)} %fusion.1), channel_id=1, source_target_pairs={{0,1},{1,0},{2,3},{3,2},{4,5},{5,4},{6,7},{7,6},{8,9},{9,8},{10,11... | collective-permute-start | bytes 983048 | tf_op jit(solution)/shard_map/ppermute | solution.py:28
  33.4 0.9 %fusion.60 = (bf16[128,640]{1,0:T(8,128)(2,1)S(1)}, f32[128,640]{1,0:T(8,128)S(1)}) fusion(pred[640]{0:T(1024)(128)(4,1)S(1)} %compare_reduce_fusion.8, bf16[128,2048]{1,0:T(8,128)(2,1)S(1)} %collective-permute-done.9.refs_3_, bf16[640,2048]{1,0:T(8,128)(2,1)S(1)} %copy-done.3), kind=kOutput, calls=%fused_computation.130 | convolution fusion | flops 335708160 | bytes 3637888 | tf_op jit(solution)/shard_map/dot_general | solution.py:71
  34.4 0.9 %fusion.68 = (bf16[128,640]{1,0:T(8,128)(2,1)S(1)}, f32[128,640]{1,0:T(8,128)S(1)}) fusion(bf16[640,2048]{1,0:T(8,128)(2,1)S(1)} %copy-done.3, bf16[64,2048]{1,0:T(8,128)(2,1)S(1)} %broadcast_select_fusion.1, bf16[32,2048]{1,0:T(8,128)(2,1)S(1)} %collective-permute-done.7, bf16[16,2048]{1,0:T(8,128)(2,1)S(1)} %collective-permute-done.6, ...), kind=kOutput, calls=%fused_computation.135 | convolution fusion | flops 337805312 | bytes 3637888 | tf_op jit(solution)/shard_map/dot_general | solution.py:71
  35.3 4.1 %collective-permute-done.10 = bf16[256,640]{1,0:T(8,128)(2,1)S(1)} collective-permute-done((bf16[256,640]{1,0:T(8,128)(2,1)S(1)}, bf16[256,640]{1,0:T(8,128)(2,1)S(1)}, u32[]{:S(2)}, u32[]{:S(2)}) %collective-permute-start.10) | collective-permute-done | bytes 327712 | tf_op jit(solution)/shard_map/ppermute | solution.py:28
  39.8 1.2 %collective-permute-start.14 = (bf16[128,640]{1,0:T(8,128)(2,1)S(1)}, bf16[128,640]{1,0:T(8,128)(2,1)S(1)}, u32[]{:S(2)}, u32[]{:S(2)}) collective-permute-start(bf16[128,640]{1,0:T(8,128)(2,1)S(1)} %get-tuple-element.48), channel_id=1, source_target_pairs={{0,1},{1,0},{2,3},{3,2},{4,5},{5,4},{6,7},{7,6},{8,9},{9,8},{10,11... | collective-permute-start | bytes 491528 | tf_op jit(solution)/shard_map/ppermute | solution.py:28
  41.0 0.9 %collective-permute-start.15 = (bf16[128,640]{1,0:T(8,128)(2,1)S(1)}, bf16[128,640]{1,0:T(8,128)(2,1)S(1)}, u32[]{:S(2)}, u32[]{:S(2)}) collective-permute-start(bf16[128,640]{1,0:T(8,128)(2,1)S(1)} %get-tuple-element.82), channel_id=1, source_target_pairs={{0,1},{1,0},{2,3},{3,2},{4,5},{5,4},{6,7},{7,6},{8,9},{9,8},{10,11... | collective-permute-start | bytes 491528 | tf_op jit(solution)/shard_map/ppermute | solution.py:28
  41.9 4.6 %collective-permute-done.11 = bf16[256,640]{1,0:T(8,128)(2,1)S(1)} collective-permute-done((bf16[256,640]{1,0:T(8,128)(2,1)S(1)}, bf16[256,640]{1,0:T(8,128)(2,1)S(1)}, u32[]{:S(2)}, u32[]{:S(2)}) %collective-permute-start.11) | collective-permute-done | bytes 327712 | tf_op jit(solution)/shard_map/ppermute | solution.py:28
  47.5 2.5 %collective-permute-done.14.got_ref = bf16[128,640]{1,0:T(8,128)(2,1)S(1)} collective-permute-done((bf16[128,640]{1,0:T(8,128)(2,1)S(1)}, bf16[128,640]{1,0:T(8,128)(2,1)S(1)}, u32[]{:S(2)}, u32[]{:S(2)}) %collective-permute-start.14) | collective-permute-done | bytes 163872 | tf_op jit(solution)/shard_map/ppermute | solution.py:28
  52.2 1.6 %collective-permute-start.13 = (bf16[64,2048]{1,0:T(8,128)(2,1)S(1)}, bf16[64,2048]{1,0:T(8,128)(2,1)S(1)}, u32[]{:S(2)}, u32[]{:S(2)}) collective-permute-start(bf16[64,2048]{1,0:T(8,128)(2,1)S(1)} %add_convert_fusion.1), channel_id=1, source_target_pairs={{0,4},{2,6},{4,0},{6,2},{8,12},{10,14},{12,8},{14,10},{16,20},{18,... | collective-permute-start | bytes 786440 | tf_op jit(solution)/shard_map/ppermute | solution.py:28
  60.4 3.4 %weight_grads.2 = (f32[640,2048]{1,0:T(8,128)}, f32[8,2048]{1,0:T(8,128)S(1)}) custom-call(bf16[128,640]{1,0:T(8,128)(2,1)S(1)} %get-tuple-element.25.refs_0_, bf16[128,640]{1,0:T(8,128)(2,1)S(1)} %get-tuple-element.26.refs_1_, bf16[128,2048]{1,0:T(8,128)(2,1)S(1)} %pad_maximum_fusion.2.refs_2_, bf16[128,2048]{1,0:T(8,128)(2,1)S(1)} %collective-permute-done.9.refs_3_, ...), custom_call_target="tpu_custom_call" | custom-call | flops 1 | bytes 1000 | tf_op jit(solution)/shard_map/weight_grads/pallas_call | solution.py:102
  64.1 2.7 %collective-permute-done.18.got_ref = bf16[64,2048]{1,0:T(8,128)(2,1)S(1)} collective-permute-done((bf16[64,2048]{1,0:T(8,128)(2,1)S(1)}, bf16[64,2048]{1,0:T(8,128)(2,1)S(1)}, u32[]{:S(2)}, u32[]{:S(2)}) %collective-permute-start.18) | collective-permute-done | bytes 262176 | tf_op jit(solution)/shard_map/ppermute | solution.py:28
  67.1 2.5 %collective-permute-start.25 = (bf16[16,2192]{1,0:T(8,128)(2,1)S(1)}, bf16[16,2192]{1,0:T(8,128)(2,1)S(1)}, u32[]{:S(2)}, u32[]{:S(2)}) collective-permute-start(bf16[16,2192]{1,0:T(8,128)(2,1)S(1)} %get-tuple-element.77.refs_6_), channel_id=1, source_target_pairs={{0,24},{2,26},{4,28},{6,30},{8,16},{10,18},{12,20},{14,22},{16,8},... | collective-permute-start | bytes 210440 | tf_op jit(solution)/shard_map/ppermute | solution.py:28
  69.7 1.9 %collective-permute-start.23 = (bf16[16,2192]{1,0:T(8,128)(2,1)S(1)}, bf16[16,2192]{1,0:T(8,128)(2,1)S(1)}, u32[]{:S(2)}, u32[]{:S(2)}) collective-permute-start(bf16[16,2192]{1,0:T(8,128)(2,1)S(1)} %get-tuple-element.75), channel_id=1, source_target_pairs={{0,16},{2,18},{4,20},{6,22},{8,24},{10,26},{12,28},{14,30},{16,0},... | collective-permute-start | bytes 210440 | tf_op jit(solution)/shard_map/ppermute | solution.py:28
  71.7 1.1 %collective-permute-start.19 = (bf16[16,2048]{1,0:T(8,128)(2,1)S(1)}, bf16[16,2048]{1,0:T(8,128)(2,1)S(1)}, u32[]{:S(2)}, u32[]{:S(2)}) collective-permute-start(bf16[16,2048]{1,0:T(8,128)(2,1)S(1)} %fusion.52.refs_7_), channel_id=1, source_target_pairs={{0,16},{2,18},{4,20},{6,22},{8,24},{10,26},{12,28},{14,30},{16,0},... | collective-permute-start | bytes 196616 | tf_op jit(solution)/shard_map/ppermute | solution.py:28
  72.8 4.8 %weight_grads.3 = (f32[640,2048]{1,0:T(8,128)}, f32[640,2048]{1,0:T(8,128)}, f32[8,2048]{1,0:T(8,128)S(1)}) custom-call(bf16[128,640]{1,0:T(8,128)(2,1)S(1)} %get-tuple-element.35.refs_0_, bf16[128,640]{1,0:T(8,128)(2,1)S(1)} %get-tuple-element.36.refs_1_, bf16[128,640]{1,0:T(8,128)(2,1)S(1)} %get-tuple-element.30.refs_2_, ...), custom_call_target="tpu_custom_call" | custom-call | flops 1 | bytes 60000000 | tf_op jit(solution)/shard_map/weight_grads/pallas_call | solution.py:102
  77.6 1.1 %collective-permute-done.23 = bf16[16,2192]{1,0:T(8,128)(2,1)S(1)} collective-permute-done((bf16[16,2192]{1,0:T(8,128)(2,1)S(1)}, bf16[16,2192]{1,0:T(8,128)(2,1)S(1)}, u32[]{:S(2)}, u32[]{:S(2)}) %collective-permute-start.23) | collective-permute-done | bytes 70176 | tf_op jit(solution)/shard_map/ppermute | solution.py:28
  (105 shorter events, 16.6 us)
Async XLA Ops:
  0.6 26.3 %copy-start = (bf16[640,2048]{1,0:T(8,128)(2,1)S(1)}, bf16[640,2048]{1,0:T(8,128)(2,1)}, u32[]{:S(2)}) copy-start(bf16[640,2048]{1,0:T(8,128)(2,1)} %param.10) | copy-start | bytes 7864324
  1.8 5.6 %collective-permute-start = (f32[16]{0:T(128)S(1)}, f32[16]{0:T(128)S(1)}, u32[]{:S(2)}, u32[]{:S(2)}) collective-permute-start(f32[16]{0:T(128)S(1)} %fusion.27), channel_id=1, source_target_pairs={{0,1},{1,0},{2,3},{3,2},{4,5},{5,4},{6,7},{7,6},{8,9},{9,8},{10,11... | collective-permute-start | bytes 200 | tf_op jit(solution)/shard_map/ppermute | solution.py:28
  4.8 8.0 %collective-permute-start.6 = (bf16[16,2048]{1,0:T(8,128)(2,1)}, bf16[16,2048]{1,0:T(8,128)(2,1)S(1)}, u32[]{:S(2)}, u32[]{:S(2)}) collective-permute-start(bf16[16,2048]{1,0:T(8,128)(2,1)} %param.7), channel_id=1, source_target_pairs={{0,16},{2,18},{4,20},{6,22},{8,24},{10,26},{12,28},{14,30},{16,0},... | collective-permute-start | bytes 196616 | tf_op jit(solution)/shard_map/ppermute | solution.py:28
  8.3 7.1 %collective-permute-start.1 = (bf16[16,2048]{1,0:T(8,128)(2,1)S(1)}, bf16[16,2048]{1,0:T(8,128)(2,1)S(1)}, u32[]{:S(2)}, u32[]{:S(2)}) collective-permute-start(bf16[16,2048]{1,0:T(8,128)(2,1)S(1)} %get-tuple-element.55), channel_id=1, source_target_pairs={{0,16},{2,18},{4,20},{6,22},{8,24},{10,26},{12,28},{14,30},{16,0},... | collective-permute-start | bytes 196616 | tf_op jit(solution)/shard_map/ppermute | solution.py:28
  10.4 5.0 %collective-permute-start.2 = (bf16[16,2048]{1,0:T(8,128)(2,1)S(1)}, bf16[16,2048]{1,0:T(8,128)(2,1)S(1)}, u32[]{:S(2)}, u32[]{:S(2)}) collective-permute-start(bf16[16,2048]{1,0:T(8,128)(2,1)S(1)} %get-tuple-element.55), channel_id=1, source_target_pairs={{0,8},{2,10},{4,12},{6,14},{8,0},{10,2},{12,4},{14,6},{16,24},{18,... | collective-permute-start | bytes 196616 | tf_op jit(solution)/shard_map/ppermute | solution.py:28
  12.0 6.2 %collective-permute-start.3 = (bf16[16,2048]{1,0:T(8,128)(2,1)S(1)}, bf16[16,2048]{1,0:T(8,128)(2,1)S(1)}, u32[]{:S(2)}, u32[]{:S(2)}) collective-permute-start(bf16[16,2048]{1,0:T(8,128)(2,1)S(1)} %get-tuple-element.55), channel_id=1, source_target_pairs={{0,24},{2,26},{4,28},{6,30},{8,16},{10,18},{12,20},{14,22},{16,8},... | collective-permute-start | bytes 196616 | tf_op jit(solution)/shard_map/ppermute | solution.py:28
  13.6 14.2 %copy-start.2 = (bf16[640,2048]{1,0:T(8,128)(2,1)S(1)}, bf16[640,2048]{1,0:T(8,128)(2,1)}, u32[]{:S(2)}) copy-start(bf16[640,2048]{1,0:T(8,128)(2,1)} %param.9) | copy-start | bytes 7864324
  13.6 6.2 %collective-permute-start.7 = (bf16[32,2048]{1,0:T(8,128)(2,1)S(1)}, bf16[32,2048]{1,0:T(8,128)(2,1)S(1)}, u32[]{:S(2)}, u32[]{:S(2)}) collective-permute-start(bf16[32,2048]{1,0:T(8,128)(2,1)S(1)} %pad_maximum_fusion.5), channel_id=1, source_target_pairs={{0,8},{2,10},{4,12},{6,14},{8,0},{10,2},{12,4},{14,6},{16,24},{18,... | collective-permute-start | bytes 393224 | tf_op jit(solution)/shard_map/ppermute | solution.py:28
  18.2 8.6 %collective-permute-start.4 = (bf16[64,2048]{1,0:T(8,128)(2,1)S(1)}, bf16[64,2048]{1,0:T(8,128)(2,1)S(1)}, u32[]{:S(2)}, u32[]{:S(2)}) collective-permute-start(bf16[64,2048]{1,0:T(8,128)(2,1)S(1)} %pad_maximum_fusion.3), channel_id=1, source_target_pairs={{0,4},{2,6},{4,0},{6,2},{8,12},{10,14},{12,8},{14,10},{16,20},{18,... | collective-permute-start | bytes 786440 | tf_op jit(solution)/shard_map/ppermute | solution.py:28
  20.7 9.4 %collective-permute-start.8 = (bf16[64,2048]{1,0:T(8,128)(2,1)S(1)}, bf16[64,2048]{1,0:T(8,128)(2,1)S(1)}, u32[]{:S(2)}, u32[]{:S(2)}) collective-permute-start(bf16[64,2048]{1,0:T(8,128)(2,1)S(1)} %pad_maximum_fusion.4), channel_id=1, source_target_pairs={{0,4},{2,6},{4,0},{6,2},{8,12},{10,14},{12,8},{14,10},{16,20},{18,... | collective-permute-start | bytes 786440 | tf_op jit(solution)/shard_map/ppermute | solution.py:28
  26.8 3.6 %collective-permute-start.5 = (bf16[128,2048]{1,0:T(8,128)(2,1)S(1)}, bf16[128,2048]{1,0:T(8,128)(2,1)S(1)}, u32[]{:S(2)}, u32[]{:S(2)}) collective-permute-start(bf16[128,2048]{1,0:T(8,128)(2,1)S(1)} %constant_dynamic-update-slice_fusion.refs_3_.refs_4_), channel_id=1, source_target_pairs={{0,2},{2,0},{4,6},{6,4},{8,10},{10,8},{12,14},{14,12},{16,18},{18,... | collective-permute-start | bytes 1572872 | tf_op jit(solution)/shard_map/ppermute | solution.py:28
  27.9 2.2 %copy-start.5 = (bf16[16,2048]{1,0:T(8,128)(2,1)S(1)}, bf16[16,2048]{1,0:T(8,128)(2,1)}, u32[]{:S(2)}) copy-start(bf16[16,2048]{1,0:T(8,128)(2,1)} %param.7) | copy-start | bytes 196612
  28.9 10.6 %collective-permute-start.10 = (bf16[256,640]{1,0:T(8,128)(2,1)S(1)}, bf16[256,640]{1,0:T(8,128)(2,1)S(1)}, u32[]{:S(2)}, u32[]{:S(2)}) collective-permute-start(bf16[256,640]{1,0:T(8,128)(2,1)S(1)} %fusion.2), channel_id=1, source_target_pairs={{0,1},{1,0},{2,3},{3,2},{4,5},{5,4},{6,7},{7,6},{8,9},{9,8},{10,11... | collective-permute-start | bytes 983048 | tf_op jit(solution)/shard_map/ppermute | solution.py:28
  30.2 3.2 %collective-permute-start.9 = (bf16[128,2048]{1,0:T(8,128)(2,1)S(1)}, bf16[128,2048]{1,0:T(8,128)(2,1)S(1)}, u32[]{:S(2)}, u32[]{:S(2)}) collective-permute-start(bf16[128,2048]{1,0:T(8,128)(2,1)S(1)} %pad_maximum_fusion.2.refs_2_), channel_id=1, source_target_pairs={{0,2},{2,0},{4,6},{6,4},{8,10},{10,8},{12,14},{14,12},{16,18},{18,... | collective-permute-start | bytes 1572872 | tf_op jit(solution)/shard_map/ppermute | solution.py:28
  31.4 2.0 %copy-start.3 = (bf16[640,2048]{1,0:T(8,128)(2,1)S(1)}, bf16[640,2048]{1,0:T(8,128)(2,1)}, u32[]{:S(2)}) copy-start(bf16[640,2048]{1,0:T(8,128)(2,1)} %param.11) | copy-start | bytes 7864324
  32.4 14.1 %collective-permute-start.11 = (bf16[256,640]{1,0:T(8,128)(2,1)S(1)}, bf16[256,640]{1,0:T(8,128)(2,1)S(1)}, u32[]{:S(2)}, u32[]{:S(2)}) collective-permute-start(bf16[256,640]{1,0:T(8,128)(2,1)S(1)} %fusion.1), channel_id=1, source_target_pairs={{0,1},{1,0},{2,3},{3,2},{4,5},{5,4},{6,7},{7,6},{8,9},{9,8},{10,11... | collective-permute-start | bytes 983048 | tf_op jit(solution)/shard_map/ppermute | solution.py:28
  39.8 10.2 %collective-permute-start.14 = (bf16[128,640]{1,0:T(8,128)(2,1)S(1)}, bf16[128,640]{1,0:T(8,128)(2,1)S(1)}, u32[]{:S(2)}, u32[]{:S(2)}) collective-permute-start(bf16[128,640]{1,0:T(8,128)(2,1)S(1)} %get-tuple-element.48), channel_id=1, source_target_pairs={{0,1},{1,0},{2,3},{3,2},{4,5},{5,4},{6,7},{7,6},{8,9},{9,8},{10,11... | collective-permute-start | bytes 491528 | tf_op jit(solution)/shard_map/ppermute | solution.py:28
  41.0 12.8 %collective-permute-start.15 = (bf16[128,640]{1,0:T(8,128)(2,1)S(1)}, bf16[128,640]{1,0:T(8,128)(2,1)S(1)}, u32[]{:S(2)}, u32[]{:S(2)}) collective-permute-start(bf16[128,640]{1,0:T(8,128)(2,1)S(1)} %get-tuple-element.82), channel_id=1, source_target_pairs={{0,1},{1,0},{2,3},{3,2},{4,5},{5,4},{6,7},{7,6},{8,9},{9,8},{10,11... | collective-permute-start | bytes 491528 | tf_op jit(solution)/shard_map/ppermute | solution.py:28
  47.4 4.2 %collective-permute-start.12 = (bf16[128,2048]{1,0:T(8,128)(2,1)S(1)}, bf16[128,2048]{1,0:T(8,128)(2,1)S(1)}, u32[]{:S(2)}, u32[]{:S(2)}) collective-permute-start(bf16[128,2048]{1,0:T(8,128)(2,1)S(1)} %convolution_convert_fusion.refs_0_), channel_id=1, source_target_pairs={{0,2},{2,0},{4,6},{6,4},{8,10},{10,8},{12,14},{14,12},{16,18},{18,... | collective-permute-start | bytes 1572872 | tf_op jit(solution)/shard_map/ppermute | solution.py:28
  51.4 3.2 %collective-permute-start.16 = (bf16[128,2048]{1,0:T(8,128)(2,1)S(1)}, bf16[128,2048]{1,0:T(8,128)(2,1)S(1)}, u32[]{:S(2)}, u32[]{:S(2)}) collective-permute-start(bf16[128,2048]{1,0:T(8,128)(2,1)S(1)} %fusion.refs_2_), channel_id=1, source_target_pairs={{0,2},{2,0},{4,6},{6,4},{8,10},{10,8},{12,14},{14,12},{16,18},{18,... | collective-permute-start | bytes 1572872 | tf_op jit(solution)/shard_map/ppermute | solution.py:28
  52.2 11.7 %collective-permute-start.13 = (bf16[64,2048]{1,0:T(8,128)(2,1)S(1)}, bf16[64,2048]{1,0:T(8,128)(2,1)S(1)}, u32[]{:S(2)}, u32[]{:S(2)}) collective-permute-start(bf16[64,2048]{1,0:T(8,128)(2,1)S(1)} %add_convert_fusion.1), channel_id=1, source_target_pairs={{0,4},{2,6},{4,0},{6,2},{8,12},{10,14},{12,8},{14,10},{16,20},{18,... | collective-permute-start | bytes 786440 | tf_op jit(solution)/shard_map/ppermute | solution.py:28
  55.2 11.5 %collective-permute-start.18 = (bf16[64,2048]{1,0:T(8,128)(2,1)S(1)}, bf16[64,2048]{1,0:T(8,128)(2,1)S(1)}, u32[]{:S(2)}, u32[]{:S(2)}) collective-permute-start(bf16[64,2048]{1,0:T(8,128)(2,1)S(1)} %get-tuple-element.84), channel_id=1, source_target_pairs={{0,4},{2,6},{4,0},{6,2},{8,12},{10,14},{12,8},{14,10},{16,20},{18,... | collective-permute-start | bytes 786440 | tf_op jit(solution)/shard_map/ppermute | solution.py:28
  56.7 0.7 copy-start.1
  57.6 9.2 %collective-permute-start.22 = (f32[1,2112]{1,0:T(1,128)S(1)}, f32[1,2112]{1,0:T(1,128)S(1)}, u32[]{:S(2)}, u32[]{:S(2)}) collective-permute-start(f32[1,2112]{1,0:T(1,128)S(1)} %get-tuple-element.73), channel_id=1, source_target_pairs={{0,6},{2,4},{4,2},{6,0},{8,14},{10,12},{12,10},{14,8},{16,22},{18,... | collective-permute-start | bytes 25352 | tf_op jit(solution)/shard_map/ppermute | solution.py:28
  58.4 8.5 %collective-permute-start.20 = (f32[1,2112]{1,0:T(1,128)S(1)}, f32[1,2112]{1,0:T(1,128)S(1)}, u32[]{:S(2)}, u32[]{:S(2)}) collective-permute-start(f32[1,2112]{1,0:T(1,128)S(1)} %get-tuple-element.74), channel_id=1, source_target_pairs={{0,2},{2,0},{4,6},{6,4},{8,10},{10,8},{12,14},{14,12},{16,18},{18,... | collective-permute-start | bytes 25352 | tf_op jit(solution)/shard_map/ppermute | solution.py:28
  59.0 7.9 %collective-permute-start.21 = (f32[1,2112]{1,0:T(1,128)S(1)}, f32[1,2112]{1,0:T(1,128)S(1)}, u32[]{:S(2)}, u32[]{:S(2)}) collective-permute-start(f32[1,2112]{1,0:T(1,128)S(1)} %get-tuple-element.72), channel_id=1, source_target_pairs={{0,4},{2,6},{4,0},{6,2},{8,12},{10,14},{12,8},{14,10},{16,20},{18,... | collective-permute-start | bytes 25352 | tf_op jit(solution)/shard_map/ppermute | solution.py:28
  64.0 7.7 %collective-permute-start.17 = (bf16[32,2048]{1,0:T(8,128)(2,1)S(1)}, bf16[32,2048]{1,0:T(8,128)(2,1)S(1)}, u32[]{:S(2)}, u32[]{:S(2)}) collective-permute-start(bf16[32,2048]{1,0:T(8,128)(2,1)S(1)} %slice.317), channel_id=1, source_target_pairs={{0,8},{2,10},{4,12},{6,14},{8,0},{10,2},{12,4},{14,6},{16,24},{18,... | collective-permute-start | bytes 393224 | tf_op jit(solution)/shard_map/ppermute | solution.py:28
  66.8 12.0 %copy-start.4 = (bf16[16,2048]{1,0:T(8,128)(2,1)S(1)}, bf16[16,2048]{1,0:T(8,128)(2,1)}, u32[]{:S(2)}) copy-start(bf16[16,2048]{1,0:T(8,128)(2,1)} %param.6) | copy-start | bytes 196612
  67.1 10.5 %collective-permute-start.25 = (bf16[16,2192]{1,0:T(8,128)(2,1)S(1)}, bf16[16,2192]{1,0:T(8,128)(2,1)S(1)}, u32[]{:S(2)}, u32[]{:S(2)}) collective-permute-start(bf16[16,2192]{1,0:T(8,128)(2,1)S(1)} %get-tuple-element.77.refs_6_), channel_id=1, source_target_pairs={{0,24},{2,26},{4,28},{6,30},{8,16},{10,18},{12,20},{14,22},{16,8},... | collective-permute-start | bytes 210440 | tf_op jit(solution)/shard_map/ppermute | solution.py:28
  69.7 7.9 %collective-permute-start.24 = (bf16[16,2192]{1,0:T(8,128)(2,1)S(1)}, bf16[16,2192]{1,0:T(8,128)(2,1)S(1)}, u32[]{:S(2)}, u32[]{:S(2)}) collective-permute-start(bf16[16,2192]{1,0:T(8,128)(2,1)S(1)} %get-tuple-element.76), channel_id=1, source_target_pairs={{0,8},{2,10},{4,12},{6,14},{8,0},{10,2},{12,4},{14,6},{16,24},{18,... | collective-permute-start | bytes 210440 | tf_op jit(solution)/shard_map/ppermute | solution.py:28
  69.7 9.0 %collective-permute-start.23 = (bf16[16,2192]{1,0:T(8,128)(2,1)S(1)}, bf16[16,2192]{1,0:T(8,128)(2,1)S(1)}, u32[]{:S(2)}, u32[]{:S(2)}) collective-permute-start(bf16[16,2192]{1,0:T(8,128)(2,1)S(1)} %get-tuple-element.75), channel_id=1, source_target_pairs={{0,16},{2,18},{4,20},{6,22},{8,24},{10,26},{12,28},{14,30},{16,0},... | collective-permute-start | bytes 210440 | tf_op jit(solution)/shard_map/ppermute | solution.py:28
  71.7 8.4 %collective-permute-start.19 = (bf16[16,2048]{1,0:T(8,128)(2,1)S(1)}, bf16[16,2048]{1,0:T(8,128)(2,1)S(1)}, u32[]{:S(2)}, u32[]{:S(2)}) collective-permute-start(bf16[16,2048]{1,0:T(8,128)(2,1)S(1)} %fusion.52.refs_7_), channel_id=1, source_target_pairs={{0,16},{2,18},{4,20},{6,22},{8,24},{10,26},{12,28},{14,30},{16,0},... | collective-permute-start | bytes 196616 | tf_op jit(solution)/shard_map/ppermute | solution.py:28

commit v3 on v2

--- a/solution.py
+++ b/solution.py
@@ -54,6 +54,12 @@
     return steps
 
 
+def halve(rows):
+    half, quarter = rows.shape[0] // 2, rows.shape[0] // 4
+    kept = jnp.concatenate([rows[:quarter], rows[half : half + quarter]], axis=0)
+    return kept, jnp.concatenate([rows[quarter:half], rows[half + quarter :]], axis=0)
+
+
 def gather_rows(rows, dp):
     for parts in reversed(direct_steps(dp)):
         rows = jnp.concatenate([rows] + [swap(rows, "dp", dp, d) for d in parts], axis=0)
@@ -75,45 +81,45 @@
     return lax.dot_general(rows, weight, (((1,), (0,)), ((), ())), preferred_element_type=F32)
 
 
-def grad_kernel(count, *refs):
-    rows, inputs = refs[: 2 * count], refs[2 * count : 2 * count + 2]
-    outs, (mark, turned) = refs[-count - 2 : -2], refs[-2:]
+def grad_kernel(*refs):
+    rows, normed, cotangent = refs[:6], refs[6:8], refs[8:10]
+    outs, (mark, turned) = refs[-5:-2], refs[-2:]
     half, units = rows[0].shape
 
     @pl.when(pl.program_id(0) == 0)
     def _():
         mark[...] = jnp.zeros(mark.shape, F32)
         for place, ref in enumerate(rows):
-            piece, k = divmod(place, count)
+            piece, k = divmod(place, 3)
             turned[k * units : (k + 1) * units, piece * half : (piece + 1) * half] = ref[...].T
 
-    block = jnp.concatenate([ref[...] for ref in inputs], axis=0)
-    for k in range(count):
+    for k, inputs in enumerate((normed, normed, cotangent)):
+        block = jnp.concatenate([ref[...] for ref in inputs], axis=0)
         outs[k][...] = jnp.dot(
             turned[k * units : (k + 1) * units, :], block, preferred_element_type=F32
         )
 
 
-def weight_grads(count, rows, inputs, behind, bytes_accessed):
-    units, width = rows[0].shape[1], inputs[0].shape[1]
+def weight_grads(rows, normed, cotangent, behind):
+    units, width = rows[0].shape[1], normed[0].shape[1]
     block = min(width, 512)
     whole = lambda a: pl.BlockSpec(a.shape, lambda i: (0, 0))
     columns = lambda a: pl.BlockSpec((a.shape[0], block), lambda i: (0, i))
     return pl.pallas_call(
-        functools.partial(grad_kernel, count),
+        grad_kernel,
         grid=(width // block,),
         in_specs=[whole(a) for a in rows]
-        + [columns(a) for a in inputs]
+        + [columns(a) for a in (*normed, *cotangent)]
         + [pl.BlockSpec(memory_space=pl.ANY)] * len(behind),
-        out_specs=[pl.BlockSpec((units, block), lambda i: (0, i))] * count
+        out_specs=[pl.BlockSpec((units, block), lambda i: (0, i))] * 3
         + [pl.BlockSpec((8, width), lambda i: (0, 0))],
-        out_shape=[jax.ShapeDtypeStruct((units, width), F32)] * count
+        out_shape=[jax.ShapeDtypeStruct((units, width), F32)] * 3
         + [jax.ShapeDtypeStruct((8, width), F32)],
-        scratch_shapes=[pltpu.VMEM((count * units, 2 * rows[0].shape[0]), BF16)],
-        compiler_params=pltpu.CompilerParams(vmem_limit_bytes=20 * 2**20),
-        cost_estimate=pl.CostEstimate(flops=1, bytes_accessed=bytes_accessed, transcendentals=0),
+        scratch_shapes=[pltpu.VMEM((3 * units, 2 * rows[0].shape[0]), BF16)],
+        compiler_params=pltpu.CompilerParams(vmem_limit_bytes=24 * 2**20),
+        cost_estimate=pl.CostEstimate(flops=1, bytes_accessed=60_000_000, transcendentals=0),
         name="weight_grads",
-    )(*rows, *inputs, *behind)
+    )(*rows, *normed, *cotangent, *behind)
 
 
 def add_kernel(kept_ref, got_ref, *refs):
@@ -211,9 +217,11 @@
     other_h, *other_f = activate(other_p)
     sent_h = outward(other_h, down_weight).astype(BF16)
     got_h = swap(sent_h, "dp", dp, 1)
-    branch_sent = outward(own_h[size:], down_weight) + got_h[size:].astype(F32)
+    own_kept, own_sent = halve(own_h)
+    got_kept, got_sent = halve(got_h)
+    branch_sent = outward(own_sent, down_weight) + got_sent.astype(F32)
     branch_sent = lax.optimization_barrier(branch_sent.astype(BF16))
-    branch = outward(own_h[:size], down_weight) + got_h[:size].astype(F32)
+    branch = outward(own_kept, down_weight) + got_kept.astype(F32)
     bit = 1
     while bit < node:
         got = swap(other_b.astype(BF16), "node", node, bit)
@@ -238,14 +246,15 @@
         vector(2, gain_part, own_r[:, size:]),
         vector(3, gain_part, other_r[:, size:]),
     ]
-    grad_down_weight, mark = weight_grads(
-        1, (own_h, other_h), (own_c, other_c), (gain_part,), 1_000
-    )
-    branch = add_got(branch, swap(branch_sent, "dp", dp, 2), 40_000_000, (mark,))
-    sent_h = lax.optimization_barrier(branch[branch.shape[0] // 2 :].astype(BF16))
+    first, *others = halving_distances(dp)
+    branch = add_got(branch, swap(branch_sent, "dp", dp, first), 40_000_000, (gain_part,))
+    for distance in (2, *others[:-1]):
+        half = branch.shape[0] // 2
+        sent_h = lax.optimization_barrier(branch[half:].astype(BF16))
+        branch = branch[:half] + swap(sent_h, "dp", dp, distance).astype(F32)
 
     normed = normed_own + got_g[:size].astype(F32)
-    normed = add_got(normed, swap(normed_sent, "dp", dp, 2), 40_000_000, (mark,))
+    normed = add_got(normed, swap(normed_sent, "dp", dp, 2), 40_000_000)
     normed = after(normed, sent_h)
     vectors = jnp.concatenate([after(gain_part, normed), own_r[:, :size]], axis=1)
     vectors = vectors + (got_v[0] + got_v[1] + got_v[2])
@@ -264,23 +273,23 @@
             ]
 
         sent = [jnp.concatenate(joined(k + 1), axis=1).astype(BF16) for k in range(len(parts))]
-        for place, distance in enumerate(sorted(parts)[:2]):
-            half = branch.shape[0] // 2
-            if place:
-                sent_h = after(branch[half:].astype(BF16), sent[0])
-            branch = branch[:half] + swap(sent_h, "dp", dp, distance).astype(F32)
-        if branch.shape[0] == count and count == tokens.shape[0]:
-            grad_gate_weight, grad_up_weight, sent_h = weight_grads(
-                2, (*own_g, *other_g), (own_n, other_n), (sent[-1], sent_h), 60_000_000
+        if count == tokens.shape[0]:
+            for distance in others[-1:]:
+                sent_h = after(branch[count:].astype(BF16), sent[0])
+                branch = branch[:count] + swap(sent_h, "dp", dp, distance).astype(F32)
+            grad_gate_weight, grad_up_weight, grad_down_weight, sent_h = weight_grads(
+                (*own_g, own_h, *other_g, other_h),
+                (own_n, other_n),
+                (own_c, other_c),
+                (sent[-1], sent_h),
             )
-        kept, *others = joined(0)
-        total = jnp.concatenate([after(kept, sent_h), *others], axis=1)
+        kept, *extras = joined(0)
+        total = jnp.concatenate([after(kept, sent_h), *extras], axis=1)
         for part, distance in zip(sent, parts):
             total = total + swap(part, "dp", dp, distance).astype(F32)
         normed = total[:, :width]
         gain_part = total[:, width : width + lanes].reshape(1, width)
         rows = total[:1, width + lanes :]
-        sent_h = branch[branch.shape[0] // 2 :].astype(BF16)
 
     row_mean = (rows / features).reshape(-1, 1)
     grad_scaled = normed * norm_gain

time: 81 us -> 78.9 us (0.974)
  waiting for transfers between devices: 23.8 us -> 21.4 us
  starting transfers between devices: 28.5 us -> 30.5 us
  Pallas kernels: 8.55 us -> 6.84 us
    ppermute x26, waiting for transfers between devices: 23.8 us -> 21.4 us  [swap(): return lax.ppermute(value, axis, [(i, i ^ distance) for i in range(size)])]
    ppermute x26, starting transfers between devices: 28.5 us -> 30.5 us  [swap(): return lax.ppermute(value, axis, [(i, i ^ distance) for i in range(size)])]
    pallas_call x2 -> x1, Pallas kernels: 8.2 us -> 6.49 us  [weight_grads(): pl.pallas_call(grad_kernel, grid=(width // block,), in_specs=[whole(a) fo...]
  transfers between devices with their start and end apart: 26 -> 26, of which waited for: 8 -> 8; matrix products, arithmetic and copies ran while one was open for 21% -> 21% of each run, Pallas kernels for 11% -> 9%
where the time goes in v3:
time: 78.9 us; the launch traced here: 78.6 us
  starting transfers between devices  30.5 us (39%)
  waiting for transfers between devices  21.4 us (27%)
  matrix products  10.9 us (14%)
  Pallas kernels  6.84 us (9%)
  other arithmetic  6.83 us (9%)
  between operations  1.15 us (1%)
  local copies, waits for them, and re-layouts  0.99 us (1%)
    ppermute x26, starting transfers between devices, swap(): return lax.ppermute(value, axis, [(i, i ^ distance) for i in range(size)])  30.5 us
    ppermute x26, waiting for transfers between devices, swap(): return lax.ppermute(value, axis, [(i, i ^ distance) for i in range(size)])  21.4 us
    pallas_call x1, Pallas kernels, weight_grads(): pl.pallas_call(grad_kernel, grid=(width // block,), in_specs=[whole(a) fo...  6.49 us
    dot_general x6, matrix products, inward(): lax.dot_general(rows, weight, (((1,), (1,)), ((), ())), preferred_element...  5.6 us
    dot_general x9, matrix products, outward(): lax.dot_general(rows, weight, (((1,), (0,)), ((), ())), preferred_element...  5.26 us
    concatenate x2, other arithmetic, gather_rows_behind(): rows = jnp.concatenate([rows, swap(rows, 'dp', dp, distance)], axis=0)  1.71 us
  transfers between devices with their start and end apart: 26, of which 8 were waited for; matrix products, arithmetic and copies ran while one was open for 21% of the time, Pallas kernels for 9%

profile of v3, /device:TPU:0, one launch (start us, length us, event | category | flops | bytes accessed | tf_op | source)
XLA Modules:
  0.0 78.6 jit_solution(1329717553165404563)
XLA Ops:
  0.6 1.1 %fusion.27 = f32[16]{0:T(128)S(1)} fusion(bf16[16,2048]{1,0:T(8,128)(2,1)} %param.6), kind=kLoop, calls=%fused_computation.69 | loop fusion | flops 98288 | bytes 65600 | tf_op jit(solution)/shard_map/reduce_sum | solution.py:176
  1.8 3.0 %collective-permute-start = (f32[16]{0:T(128)S(1)}, f32[16]{0:T(128)S(1)}, u32[]{:S(2)}, u32[]{:S(2)}) collective-permute-start(f32[16]{0:T(128)S(1)} %fusion.27), channel_id=1, source_target_pairs={{0,1},{1,0},{2,3},{3,2},{4,5},{5,4},{6,7},{7,6},{8,9},{9,8},{10,11... | collective-permute-start | bytes 200 | tf_op jit(solution)/shard_map/ppermute | solution.py:28
  4.8 2.6 %collective-permute-start.6 = (bf16[16,2048]{1,0:T(8,128)(2,1)}, bf16[16,2048]{1,0:T(8,128)(2,1)S(1)}, u32[]{:S(2)}, u32[]{:S(2)}) collective-permute-start(bf16[16,2048]{1,0:T(8,128)(2,1)} %param.7), channel_id=1, source_target_pairs={{0,16},{2,18},{4,20},{6,22},{8,24},{10,26},{12,28},{14,30},{16,0},... | collective-permute-start | bytes 196616 | tf_op jit(solution)/shard_map/ppermute | solution.py:28
  7.4 0.9 %constant_dynamic-update-slice_fusion.4 = (bf16[128,2048]{1,0:T(8,128)(2,1)S(1)}, bf16[16,2048]{1,0:T(8,128)(2,1)S(1)}) fusion(f32[2048]{0:T(1024)} %param.8, f32[16]{0:T(128)S(1)} %add_rsqrt_fusion, bf16[16,2048]{1,0:T(8,128)(2,1)} %param.6), kind=kLoop, calls=%fused_computation.113 | loop fusion | flops 131071 | bytes 204864
  8.3 2.1 %collective-permute-start.1 = (bf16[16,2048]{1,0:T(8,128)(2,1)S(1)}, bf16[16,2048]{1,0:T(8,128)(2,1)S(1)}, u32[]{:S(2)}, u32[]{:S(2)}) collective-permute-start(bf16[16,2048]{1,0:T(8,128)(2,1)S(1)} %get-tuple-element.53), channel_id=1, source_target_pairs={{0,16},{2,18},{4,20},{6,22},{8,24},{10,26},{12,28},{14,30},{16,0},... | collective-permute-start | bytes 196616 | tf_op jit(solution)/shard_map/ppermute | solution.py:28
  10.4 1.6 %collective-permute-start.2 = (bf16[16,2048]{1,0:T(8,128)(2,1)S(1)}, bf16[16,2048]{1,0:T(8,128)(2,1)S(1)}, u32[]{:S(2)}, u32[]{:S(2)}) collective-permute-start(bf16[16,2048]{1,0:T(8,128)(2,1)S(1)} %get-tuple-element.53), channel_id=1, source_target_pairs={{0,8},{2,10},{4,12},{6,14},{8,0},{10,2},{12,4},{14,6},{16,24},{18,... | collective-permute-start | bytes 196616 | tf_op jit(solution)/shard_map/ppermute | solution.py:28
  14.4 1.1 %collective-permute-done.1 = bf16[16,2048]{1,0:T(8,128)(2,1)S(1)} collective-permute-done((bf16[16,2048]{1,0:T(8,128)(2,1)S(1)}, bf16[16,2048]{1,0:T(8,128)(2,1)S(1)}, u32[]{:S(2)}, u32[]{:S(2)}) %collective-permute-start.1) | collective-permute-done | bytes 65568 | tf_op jit(solution)/shard_map/ppermute | solution.py:28
  15.5 2.7 %collective-permute-done.3 = bf16[16,2048]{1,0:T(8,128)(2,1)S(1)} collective-permute-done((bf16[16,2048]{1,0:T(8,128)(2,1)S(1)}, bf16[16,2048]{1,0:T(8,128)(2,1)S(1)}, u32[]{:S(2)}, u32[]{:S(2)}) %collective-permute-start.3) | collective-permute-done | bytes 65568 | tf_op jit(solution)/shard_map/ppermute | solution.py:28
  18.2 1.6 %collective-permute-start.4 = (bf16[64,2048]{1,0:T(8,128)(2,1)S(1)}, bf16[64,2048]{1,0:T(8,128)(2,1)S(1)}, u32[]{:S(2)}, u32[]{:S(2)}) collective-permute-start(bf16[64,2048]{1,0:T(8,128)(2,1)S(1)} %pad_maximum_fusion.3), channel_id=1, source_target_pairs={{0,4},{2,6},{4,0},{6,2},{8,12},{10,14},{12,8},{14,10},{16,20},{18,... | collective-permute-start | bytes 786440 | tf_op jit(solution)/shard_map/ppermute | solution.py:28
  19.8 0.9 %pad_maximum_fusion.4 = bf16[64,2048]{1,0:T(8,128)(2,1)S(1)} fusion(bf16[32,2048]{1,0:T(8,128)(2,1)S(1)} %collective-permute-done.7, bf16[16,2048]{1,0:T(8,128)(2,1)S(1)} %collective-permute-done.6, bf16[16,2048]{1,0:T(8,128)(2,1)} %param.7), kind=kLoop, calls=%fused_computation.49 | loop fusion | flops 786432 | bytes 524288 | tf_op jit(solution)/shard_map/concatenate | solution.py:71
  20.7 1.1 %collective-permute-start.8 = (bf16[64,2048]{1,0:T(8,128)(2,1)S(1)}, bf16[64,2048]{1,0:T(8,128)(2,1)S(1)}, u32[]{:S(2)}, u32[]{:S(2)}) collective-permute-start(bf16[64,2048]{1,0:T(8,128)(2,1)S(1)} %pad_maximum_fusion.4), channel_id=1, source_target_pairs={{0,4},{2,6},{4,0},{6,2},{8,12},{10,14},{12,8},{14,10},{16,20},{18,... | collective-permute-start | bytes 786440 | tf_op jit(solution)/shard_map/ppermute | solution.py:28
  21.8 5.0 %collective-permute-done.4 = bf16[64,2048]{1,0:T(8,128)(2,1)S(1)} collective-permute-done((bf16[64,2048]{1,0:T(8,128)(2,1)S(1)}, bf16[64,2048]{1,0:T(8,128)(2,1)S(1)}, u32[]{:S(2)}, u32[]{:S(2)}) %collective-permute-start.4) | collective-permute-done | bytes 262176 | tf_op jit(solution)/shard_map/ppermute | solution.py:28
  26.9 0.9 %fusion.78 = f32[128,640]{1,0:T(8,128)S(1)} fusion(bf16[128,2048]{1,0:T(8,128)(2,1)S(1)} %constant_dynamic-update-slice_fusion.refs_3_.refs_6_, bf16[640,2048]{1,0:T(8,128)(2,1)S(1)} %copy-done), kind=kOutput, calls=%fused_computation.145 | convolution fusion | flops 335544320 | bytes 3473408 | tf_op jit(solution)/shard_map/dot_general | solution.py:77
  27.9 0.9 %fusion.79 = f32[128,640]{1,0:T(8,128)S(1)} fusion(bf16[128,2048]{1,0:T(8,128)(2,1)S(1)} %constant_dynamic-update-slice_fusion.refs_3_.refs_6_, bf16[640,2048]{1,0:T(8,128)(2,1)S(1)} %copy-done.2), kind=kOutput, calls=%fused_computation.146 | convolution fusion | flops 335544320 | bytes 3473408 | tf_op jit(solution)/shard_map/dot_general | solution.py:77
  28.9 1.2 %collective-permute-start.10 = (bf16[256,640]{1,0:T(8,128)(2,1)S(1)}, bf16[256,640]{1,0:T(8,128)(2,1)S(1)}, u32[]{:S(2)}, u32[]{:S(2)}) collective-permute-start(bf16[256,640]{1,0:T(8,128)(2,1)S(1)} %fusion.2), channel_id=1, source_target_pairs={{0,1},{1,0},{2,3},{3,2},{4,5},{5,4},{6,7},{7,6},{8,9},{9,8},{10,11... | collective-permute-start | bytes 983048 | tf_op jit(solution)/shard_map/ppermute | solution.py:28
  30.4 0.9 %fusion.80 = f32[128,640]{1,0:T(8,128)S(1)} fusion(bf16[128,2048]{1,0:T(8,128)(2,1)S(1)} %collective-permute-done.5.refs_4_.refs_7_, bf16[640,2048]{1,0:T(8,128)(2,1)S(1)} %copy-done), kind=kOutput, calls=%fused_computation.147 | convolution fusion | flops 335544320 | bytes 3473408 | tf_op jit(solution)/shard_map/dot_general | solution.py:77
  31.4 0.9 %fusion.77 = f32[128,640]{1,0:T(8,128)S(1)} fusion(bf16[128,2048]{1,0:T(8,128)(2,1)S(1)} %collective-permute-done.5.refs_4_.refs_7_, bf16[640,2048]{1,0:T(8,128)(2,1)S(1)} %copy-done.2), kind=kOutput, calls=%fused_computation.144 | convolution fusion | flops 335544320 | bytes 3473408 | tf_op jit(solution)/shard_map/dot_general | solution.py:77
  32.4 1.0 %collective-permute-start.11 = (bf16[256,640]{1,0:T(8,128)(2,1)S(1)}, bf16[256,640]{1,0:T(8,128)(2,1)S(1)}, u32[]{:S(2)}, u32[]{:S(2)}) collective-permute-start(bf16[256,640]{1,0:T(8,128)(2,1)S(1)} %fusion.1), channel_id=1, source_target_pairs={{0,1},{1,0},{2,3},{3,2},{4,5},{5,4},{6,7},{7,6},{8,9},{9,8},{10,11... | collective-permute-start | bytes 983048 | tf_op jit(solution)/shard_map/ppermute | solution.py:28
  33.4 0.9 %fusion.66 = (bf16[128,640]{1,0:T(8,128)(2,1)S(1)}, f32[128,640]{1,0:T(8,128)S(1)}) fusion(pred[640]{0:T(1024)(128)(4,1)S(1)} %compare_reduce_fusion.8, bf16[128,2048]{1,0:T(8,128)(2,1)S(1)} %collective-permute-done.9.refs_9_, bf16[640,2048]{1,0:T(8,128)(2,1)S(1)} %copy-done.3), kind=kOutput, calls=%fused_computation.136 | convolution fusion | flops 335708160 | bytes 3637888 | tf_op jit(solution)/shard_map/dot_general | solution.py:77
  34.3 0.9 %fusion.76 = (bf16[128,640]{1,0:T(8,128)(2,1)S(1)}, f32[128,640]{1,0:T(8,128)S(1)}) fusion(bf16[640,2048]{1,0:T(8,128)(2,1)S(1)} %copy-done.3, bf16[64,2048]{1,0:T(8,128)(2,1)S(1)} %broadcast_select_fusion.1, bf16[32,2048]{1,0:T(8,128)(2,1)S(1)} %collective-permute-done.7, bf16[16,2048]{1,0:T(8,128)(2,1)S(1)} %collective-permute-done.6, ...), kind=kOutput, calls=%fused_computation.143 | convolution fusion | flops 337805312 | bytes 3637888 | tf_op jit(solution)/shard_map/dot_general | solution.py:77
  35.3 4.1 %collective-permute-done.10 = bf16[256,640]{1,0:T(8,128)(2,1)S(1)} collective-permute-done((bf16[256,640]{1,0:T(8,128)(2,1)S(1)}, bf16[256,640]{1,0:T(8,128)(2,1)S(1)}, u32[]{:S(2)}, u32[]{:S(2)}) %collective-permute-start.10) | collective-permute-done | bytes 327712 | tf_op jit(solution)/shard_map/ppermute | solution.py:28
  39.8 1.2 %collective-permute-start.14 = (bf16[128,640]{1,0:T(8,128)(2,1)S(1)}, bf16[128,640]{1,0:T(8,128)(2,1)S(1)}, u32[]{:S(2)}, u32[]{:S(2)}) collective-permute-start(bf16[128,640]{1,0:T(8,128)(2,1)S(1)} %get-tuple-element.46), channel_id=1, source_target_pairs={{0,1},{1,0},{2,3},{3,2},{4,5},{5,4},{6,7},{7,6},{8,9},{9,8},{10,11... | collective-permute-start | bytes 491528 | tf_op jit(solution)/shard_map/ppermute | solution.py:28
  41.0 0.9 %collective-permute-start.15 = (bf16[128,640]{1,0:T(8,128)(2,1)S(1)}, bf16[128,640]{1,0:T(8,128)(2,1)S(1)}, u32[]{:S(2)}, u32[]{:S(2)}) collective-permute-start(bf16[128,640]{1,0:T(8,128)(2,1)S(1)} %get-tuple-element.88), channel_id=1, source_target_pairs={{0,1},{1,0},{2,3},{3,2},{4,5},{5,4},{6,7},{7,6},{8,9},{9,8},{10,11... | collective-permute-start | bytes 491528 | tf_op jit(solution)/shard_map/ppermute | solution.py:28
  41.9 4.6 %collective-permute-done.11 = bf16[256,640]{1,0:T(8,128)(2,1)S(1)} collective-permute-done((bf16[256,640]{1,0:T(8,128)(2,1)S(1)}, bf16[256,640]{1,0:T(8,128)(2,1)S(1)}, u32[]{:S(2)}, u32[]{:S(2)}) %collective-permute-start.11) | collective-permute-done | bytes 327712 | tf_op jit(solution)/shard_map/ppermute | solution.py:28
  47.5 2.5 %collective-permute-done.14.got_ref = bf16[128,640]{1,0:T(8,128)(2,1)S(1)} collective-permute-done((bf16[128,640]{1,0:T(8,128)(2,1)S(1)}, bf16[128,640]{1,0:T(8,128)(2,1)S(1)}, u32[]{:S(2)}, u32[]{:S(2)}) %collective-permute-start.14) | collective-permute-done | bytes 163872 | tf_op jit(solution)/shard_map/ppermute | solution.py:28
  54.5 1.6 %collective-permute-start.18 = (bf16[64,2048]{1,0:T(8,128)(2,1)S(1)}, bf16[64,2048]{1,0:T(8,128)(2,1)S(1)}, u32[]{:S(2)}, u32[]{:S(2)}) collective-permute-start(bf16[64,2048]{1,0:T(8,128)(2,1)S(1)} %get-tuple-element.90), channel_id=1, source_target_pairs={{0,4},{2,6},{4,0},{6,2},{8,12},{10,14},{12,8},{14,10},{16,20},{18,... | collective-permute-start | bytes 786440 | tf_op jit(solution)/shard_map/ppermute | solution.py:28
  58.3 1.5 %collective-permute-start.21 = (f32[1,2112]{1,0:T(1,128)S(1)}, f32[1,2112]{1,0:T(1,128)S(1)}, u32[]{:S(2)}, u32[]{:S(2)}) collective-permute-start(f32[1,2112]{1,0:T(1,128)S(1)} %get-tuple-element.78), channel_id=1, source_target_pairs={{0,4},{2,6},{4,0},{6,2},{8,12},{10,14},{12,8},{14,10},{16,20},{18,... | collective-permute-start | bytes 25352 | tf_op jit(solution)/shard_map/ppermute | solution.py:28
  61.0 1.6 %collective-permute-start.17 = (bf16[32,2048]{1,0:T(8,128)(2,1)S(1)}, bf16[32,2048]{1,0:T(8,128)(2,1)S(1)}, u32[]{:S(2)}, u32[]{:S(2)}) collective-permute-start(bf16[32,2048]{1,0:T(8,128)(2,1)S(1)} %slice.325), channel_id=1, source_target_pairs={{0,4},{2,6},{4,0},{6,2},{8,12},{10,14},{12,8},{14,10},{16,20},{18,... | collective-permute-start | bytes 393224 | tf_op jit(solution)/shard_map/ppermute | solution.py:28
  63.0 2.6 %collective-permute-start.25 = (bf16[16,2192]{1,0:T(8,128)(2,1)S(1)}, bf16[16,2192]{1,0:T(8,128)(2,1)S(1)}, u32[]{:S(2)}, u32[]{:S(2)}) collective-permute-start(bf16[16,2192]{1,0:T(8,128)(2,1)S(1)} %get-tuple-element.83.refs_10_), channel_id=1, source_target_pairs={{0,24},{2,26},{4,28},{6,30},{8,16},{10,18},{12,20},{14,22},{16,8},... | collective-permute-start | bytes 210440 | tf_op jit(solution)/shard_map/ppermute | solution.py:28
  65.6 1.2 %collective-permute-start.24 = (bf16[16,2192]{1,0:T(8,128)(2,1)S(1)}, bf16[16,2192]{1,0:T(8,128)(2,1)S(1)}, u32[]{:S(2)}, u32[]{:S(2)}) collective-permute-start(bf16[16,2192]{1,0:T(8,128)(2,1)S(1)} %get-tuple-element.82), channel_id=1, source_target_pairs={{0,8},{2,10},{4,12},{6,14},{8,0},{10,2},{12,4},{14,6},{16,24},{18,... | collective-permute-start | bytes 210440 | tf_op jit(solution)/shard_map/ppermute | solution.py:28
  67.6 2.3 %collective-permute-start.19 = (bf16[16,2048]{1,0:T(8,128)(2,1)S(1)}, bf16[16,2048]{1,0:T(8,128)(2,1)S(1)}, u32[]{:S(2)}, u32[]{:S(2)}) collective-permute-start(bf16[16,2048]{1,0:T(8,128)(2,1)S(1)} %fusion.56.refs_11_), channel_id=1, source_target_pairs={{0,16},{2,18},{4,20},{6,22},{8,24},{10,26},{12,28},{14,30},{16,0},... | collective-permute-start | bytes 196616 | tf_op jit(solution)/shard_map/ppermute | solution.py:28
  69.9 6.5 %weight_grads.1 = (f32[640,2048]{1,0:T(8,128)}, f32[640,2048]{1,0:T(8,128)}, f32[640,2048]{1,0:T(8,128)}, f32[8,2048]{1,0:T(8,128)S(1)}) custom-call(bf16[128,640]{1,0:T(8,128)(2,1)S(1)} %get-tuple-element.34.refs_0_, bf16[128,640]{1,0:T(8,128)(2,1)S(1)} %get-tuple-element.35.refs_1_, bf16[128,640]{1,0:T(8,128)(2,1)S(1)} %get-tuple-element.24.refs_2_, ...), custom_call_target="tpu_custom_call" | custom-call | flops 1 | bytes 60000000 | tf_op jit(solution)/shard_map/weight_grads/pallas_call | solution.py:108
  (106 shorter events, 15.3 us)
Async XLA Ops:
  0.6 26.3 %copy-start = (bf16[640,2048]{1,0:T(8,128)(2,1)S(1)}, bf16[640,2048]{1,0:T(8,128)(2,1)}, u32[]{:S(2)}) copy-start(bf16[640,2048]{1,0:T(8,128)(2,1)} %param.10) | copy-start | bytes 7864324
  1.8 5.6 %collective-permute-start = (f32[16]{0:T(128)S(1)}, f32[16]{0:T(128)S(1)}, u32[]{:S(2)}, u32[]{:S(2)}) collective-permute-start(f32[16]{0:T(128)S(1)} %fusion.27), channel_id=1, source_target_pairs={{0,1},{1,0},{2,3},{3,2},{4,5},{5,4},{6,7},{7,6},{8,9},{9,8},{10,11... | collective-permute-start | bytes 200 | tf_op jit(solution)/shard_map/ppermute | solution.py:28
  4.8 8.0 %collective-permute-start.6 = (bf16[16,2048]{1,0:T(8,128)(2,1)}, bf16[16,2048]{1,0:T(8,128)(2,1)S(1)}, u32[]{:S(2)}, u32[]{:S(2)}) collective-permute-start(bf16[16,2048]{1,0:T(8,128)(2,1)} %param.7), channel_id=1, source_target_pairs={{0,16},{2,18},{4,20},{6,22},{8,24},{10,26},{12,28},{14,30},{16,0},... | collective-permute-start | bytes 196616 | tf_op jit(solution)/shard_map/ppermute | solution.py:28
  8.3 7.1 %collective-permute-start.1 = (bf16[16,2048]{1,0:T(8,128)(2,1)S(1)}, bf16[16,2048]{1,0:T(8,128)(2,1)S(1)}, u32[]{:S(2)}, u32[]{:S(2)}) collective-permute-start(bf16[16,2048]{1,0:T(8,128)(2,1)S(1)} %get-tuple-element.53), channel_id=1, source_target_pairs={{0,16},{2,18},{4,20},{6,22},{8,24},{10,26},{12,28},{14,30},{16,0},... | collective-permute-start | bytes 196616 | tf_op jit(solution)/shard_map/ppermute | solution.py:28
  10.4 5.0 %collective-permute-start.2 = (bf16[16,2048]{1,0:T(8,128)(2,1)S(1)}, bf16[16,2048]{1,0:T(8,128)(2,1)S(1)}, u32[]{:S(2)}, u32[]{:S(2)}) collective-permute-start(bf16[16,2048]{1,0:T(8,128)(2,1)S(1)} %get-tuple-element.53), channel_id=1, source_target_pairs={{0,8},{2,10},{4,12},{6,14},{8,0},{10,2},{12,4},{14,6},{16,24},{18,... | collective-permute-start | bytes 196616 | tf_op jit(solution)/shard_map/ppermute | solution.py:28
  12.0 6.2 %collective-permute-start.3 = (bf16[16,2048]{1,0:T(8,128)(2,1)S(1)}, bf16[16,2048]{1,0:T(8,128)(2,1)S(1)}, u32[]{:S(2)}, u32[]{:S(2)}) collective-permute-start(bf16[16,2048]{1,0:T(8,128)(2,1)S(1)} %get-tuple-element.53), channel_id=1, source_target_pairs={{0,24},{2,26},{4,28},{6,30},{8,16},{10,18},{12,20},{14,22},{16,8},... | collective-permute-start | bytes 196616 | tf_op jit(solution)/shard_map/ppermute | solution.py:28
  13.6 14.2 %copy-start.2 = (bf16[640,2048]{1,0:T(8,128)(2,1)S(1)}, bf16[640,2048]{1,0:T(8,128)(2,1)}, u32[]{:S(2)}) copy-start(bf16[640,2048]{1,0:T(8,128)(2,1)} %param.9) | copy-start | bytes 7864324
  13.6 6.2 %collective-permute-start.7 = (bf16[32,2048]{1,0:T(8,128)(2,1)S(1)}, bf16[32,2048]{1,0:T(8,128)(2,1)S(1)}, u32[]{:S(2)}, u32[]{:S(2)}) collective-permute-start(bf16[32,2048]{1,0:T(8,128)(2,1)S(1)} %pad_maximum_fusion.5), channel_id=1, source_target_pairs={{0,8},{2,10},{4,12},{6,14},{8,0},{10,2},{12,4},{14,6},{16,24},{18,... | collective-permute-start | bytes 393224 | tf_op jit(solution)/shard_map/ppermute | solution.py:28
  18.2 8.6 %collective-permute-start.4 = (bf16[64,2048]{1,0:T(8,128)(2,1)S(1)}, bf16[64,2048]{1,0:T(8,128)(2,1)S(1)}, u32[]{:S(2)}, u32[]{:S(2)}) collective-permute-start(bf16[64,2048]{1,0:T(8,128)(2,1)S(1)} %pad_maximum_fusion.3), channel_id=1, source_target_pairs={{0,4},{2,6},{4,0},{6,2},{8,12},{10,14},{12,8},{14,10},{16,20},{18,... | collective-permute-start | bytes 786440 | tf_op jit(solution)/shard_map/ppermute | solution.py:28
  20.7 9.4 %collective-permute-start.8 = (bf16[64,2048]{1,0:T(8,128)(2,1)S(1)}, bf16[64,2048]{1,0:T(8,128)(2,1)S(1)}, u32[]{:S(2)}, u32[]{:S(2)}) collective-permute-start(bf16[64,2048]{1,0:T(8,128)(2,1)S(1)} %pad_maximum_fusion.4), channel_id=1, source_target_pairs={{0,4},{2,6},{4,0},{6,2},{8,12},{10,14},{12,8},{14,10},{16,20},{18,... | collective-permute-start | bytes 786440 | tf_op jit(solution)/shard_map/ppermute | solution.py:28
  26.8 3.6 %collective-permute-start.5 = (bf16[128,2048]{1,0:T(8,128)(2,1)S(1)}, bf16[128,2048]{1,0:T(8,128)(2,1)S(1)}, u32[]{:S(2)}, u32[]{:S(2)}) collective-permute-start(bf16[128,2048]{1,0:T(8,128)(2,1)S(1)} %constant_dynamic-update-slice_fusion.refs_3_.refs_6_), channel_id=1, source_target_pairs={{0,2},{2,0},{4,6},{6,4},{8,10},{10,8},{12,14},{14,12},{16,18},{18,... | collective-permute-start | bytes 1572872 | tf_op jit(solution)/shard_map/ppermute | solution.py:28
  27.9 2.2 %copy-start.5 = (bf16[16,2048]{1,0:T(8,128)(2,1)S(1)}, bf16[16,2048]{1,0:T(8,128)(2,1)}, u32[]{:S(2)}) copy-start(bf16[16,2048]{1,0:T(8,128)(2,1)} %param.7) | copy-start | bytes 196612
  28.9 10.6 %collective-permute-start.10 = (bf16[256,640]{1,0:T(8,128)(2,1)S(1)}, bf16[256,640]{1,0:T(8,128)(2,1)S(1)}, u32[]{:S(2)}, u32[]{:S(2)}) collective-permute-start(bf16[256,640]{1,0:T(8,128)(2,1)S(1)} %fusion.2), channel_id=1, source_target_pairs={{0,1},{1,0},{2,3},{3,2},{4,5},{5,4},{6,7},{7,6},{8,9},{9,8},{10,11... | collective-permute-start | bytes 983048 | tf_op jit(solution)/shard_map/ppermute | solution.py:28
  30.2 3.2 %collective-permute-start.9 = (bf16[128,2048]{1,0:T(8,128)(2,1)S(1)}, bf16[128,2048]{1,0:T(8,128)(2,1)S(1)}, u32[]{:S(2)}, u32[]{:S(2)}) collective-permute-start(bf16[128,2048]{1,0:T(8,128)(2,1)S(1)} %pad_maximum_fusion.2.refs_8_), channel_id=1, source_target_pairs={{0,2},{2,0},{4,6},{6,4},{8,10},{10,8},{12,14},{14,12},{16,18},{18,... | collective-permute-start | bytes 1572872 | tf_op jit(solution)/shard_map/ppermute | solution.py:28
  31.4 2.0 %copy-start.3 = (bf16[640,2048]{1,0:T(8,128)(2,1)S(1)}, bf16[640,2048]{1,0:T(8,128)(2,1)}, u32[]{:S(2)}) copy-start(bf16[640,2048]{1,0:T(8,128)(2,1)} %param.11) | copy-start | bytes 7864324
  32.4 14.1 %collective-permute-start.11 = (bf16[256,640]{1,0:T(8,128)(2,1)S(1)}, bf16[256,640]{1,0:T(8,128)(2,1)S(1)}, u32[]{:S(2)}, u32[]{:S(2)}) collective-permute-start(bf16[256,640]{1,0:T(8,128)(2,1)S(1)} %fusion.1), channel_id=1, source_target_pairs={{0,1},{1,0},{2,3},{3,2},{4,5},{5,4},{6,7},{7,6},{8,9},{9,8},{10,11... | collective-permute-start | bytes 983048 | tf_op jit(solution)/shard_map/ppermute | solution.py:28
  39.8 10.2 %collective-permute-start.14 = (bf16[128,640]{1,0:T(8,128)(2,1)S(1)}, bf16[128,640]{1,0:T(8,128)(2,1)S(1)}, u32[]{:S(2)}, u32[]{:S(2)}) collective-permute-start(bf16[128,640]{1,0:T(8,128)(2,1)S(1)} %get-tuple-element.46), channel_id=1, source_target_pairs={{0,1},{1,0},{2,3},{3,2},{4,5},{5,4},{6,7},{7,6},{8,9},{9,8},{10,11... | collective-permute-start | bytes 491528 | tf_op jit(solution)/shard_map/ppermute | solution.py:28
  41.0 12.1 %collective-permute-start.15 = (bf16[128,640]{1,0:T(8,128)(2,1)S(1)}, bf16[128,640]{1,0:T(8,128)(2,1)S(1)}, u32[]{:S(2)}, u32[]{:S(2)}) collective-permute-start(bf16[128,640]{1,0:T(8,128)(2,1)S(1)} %get-tuple-element.88), channel_id=1, source_target_pairs={{0,1},{1,0},{2,3},{3,2},{4,5},{5,4},{6,7},{7,6},{8,9},{9,8},{10,11... | collective-permute-start | bytes 491528 | tf_op jit(solution)/shard_map/ppermute | solution.py:28
  47.4 4.1 %collective-permute-start.12 = (bf16[128,2048]{1,0:T(8,128)(2,1)S(1)}, bf16[128,2048]{1,0:T(8,128)(2,1)S(1)}, u32[]{:S(2)}, u32[]{:S(2)}) collective-permute-start(bf16[128,2048]{1,0:T(8,128)(2,1)S(1)} %convolution_convert_fusion.refs_0_), channel_id=1, source_target_pairs={{0,2},{2,0},{4,6},{6,4},{8,10},{10,8},{12,14},{14,12},{16,18},{18,... | collective-permute-start | bytes 1572872 | tf_op jit(solution)/shard_map/ppermute | solution.py:28
  51.4 2.5 %collective-permute-start.16 = (bf16[128,2048]{1,0:T(8,128)(2,1)S(1)}, bf16[128,2048]{1,0:T(8,128)(2,1)S(1)}, u32[]{:S(2)}, u32[]{:S(2)}) collective-permute-start(bf16[128,2048]{1,0:T(8,128)(2,1)S(1)} %fusion.refs_2_), channel_id=1, source_target_pairs={{0,2},{2,0},{4,6},{6,4},{8,10},{10,8},{12,14},{14,12},{16,18},{18,... | collective-permute-start | bytes 1572872 | tf_op jit(solution)/shard_map/ppermute | solution.py:28
  52.2 8.8 %collective-permute-start.13 = (bf16[64,2048]{1,0:T(8,128)(2,1)S(1)}, bf16[64,2048]{1,0:T(8,128)(2,1)S(1)}, u32[]{:S(2)}, u32[]{:S(2)}) collective-permute-start(bf16[64,2048]{1,0:T(8,128)(2,1)S(1)} %add_convert_fusion.1), channel_id=1, source_target_pairs={{0,8},{2,10},{4,12},{6,14},{8,0},{10,2},{12,4},{14,6},{16,24},{18,... | collective-permute-start | bytes 786440 | tf_op jit(solution)/shard_map/ppermute | solution.py:28
  54.5 8.2 %collective-permute-start.18 = (bf16[64,2048]{1,0:T(8,128)(2,1)S(1)}, bf16[64,2048]{1,0:T(8,128)(2,1)S(1)}, u32[]{:S(2)}, u32[]{:S(2)}) collective-permute-start(bf16[64,2048]{1,0:T(8,128)(2,1)S(1)} %get-tuple-element.90), channel_id=1, source_target_pairs={{0,4},{2,6},{4,0},{6,2},{8,12},{10,14},{12,8},{14,10},{16,20},{18,... | collective-permute-start | bytes 786440 | tf_op jit(solution)/shard_map/ppermute | solution.py:28
  56.7 0.7 copy-start.1
  57.6 5.2 %collective-permute-start.22 = (f32[1,2112]{1,0:T(1,128)S(1)}, f32[1,2112]{1,0:T(1,128)S(1)}, u32[]{:S(2)}, u32[]{:S(2)}) collective-permute-start(f32[1,2112]{1,0:T(1,128)S(1)} %get-tuple-element.79), channel_id=1, source_target_pairs={{0,6},{2,4},{4,2},{6,0},{8,14},{10,12},{12,10},{14,8},{16,22},{18,... | collective-permute-start | bytes 25352 | tf_op jit(solution)/shard_map/ppermute | solution.py:28
  57.7 5.1 %collective-permute-start.20 = (f32[1,2112]{1,0:T(1,128)S(1)}, f32[1,2112]{1,0:T(1,128)S(1)}, u32[]{:S(2)}, u32[]{:S(2)}) collective-permute-start(f32[1,2112]{1,0:T(1,128)S(1)} %get-tuple-element.80), channel_id=1, source_target_pairs={{0,2},{2,0},{4,6},{6,4},{8,10},{10,8},{12,14},{14,12},{16,18},{18,... | collective-permute-start | bytes 25352 | tf_op jit(solution)/shard_map/ppermute | solution.py:28
  58.3 4.5 %collective-permute-start.21 = (f32[1,2112]{1,0:T(1,128)S(1)}, f32[1,2112]{1,0:T(1,128)S(1)}, u32[]{:S(2)}, u32[]{:S(2)}) collective-permute-start(f32[1,2112]{1,0:T(1,128)S(1)} %get-tuple-element.78), channel_id=1, source_target_pairs={{0,4},{2,6},{4,0},{6,2},{8,12},{10,14},{12,8},{14,10},{16,20},{18,... | collective-permute-start | bytes 25352 | tf_op jit(solution)/shard_map/ppermute | solution.py:28
  61.0 6.5 %collective-permute-start.17 = (bf16[32,2048]{1,0:T(8,128)(2,1)S(1)}, bf16[32,2048]{1,0:T(8,128)(2,1)S(1)}, u32[]{:S(2)}, u32[]{:S(2)}) collective-permute-start(bf16[32,2048]{1,0:T(8,128)(2,1)S(1)} %slice.325), channel_id=1, source_target_pairs={{0,4},{2,6},{4,0},{6,2},{8,12},{10,14},{12,8},{14,10},{16,20},{18,... | collective-permute-start | bytes 393224 | tf_op jit(solution)/shard_map/ppermute | solution.py:28
  63.0 13.6 %copy-start.4 = (bf16[16,2048]{1,0:T(8,128)(2,1)S(1)}, bf16[16,2048]{1,0:T(8,128)(2,1)}, u32[]{:S(2)}) copy-start(bf16[16,2048]{1,0:T(8,128)(2,1)} %param.6) | copy-start | bytes 196612
  63.0 13.5 %collective-permute-start.25 = (bf16[16,2192]{1,0:T(8,128)(2,1)S(1)}, bf16[16,2192]{1,0:T(8,128)(2,1)S(1)}, u32[]{:S(2)}, u32[]{:S(2)}) collective-permute-start(bf16[16,2192]{1,0:T(8,128)(2,1)S(1)} %get-tuple-element.83.refs_10_), channel_id=1, source_target_pairs={{0,24},{2,26},{4,28},{6,30},{8,16},{10,18},{12,20},{14,22},{16,8},... | collective-permute-start | bytes 210440 | tf_op jit(solution)/shard_map/ppermute | solution.py:28
  65.6 10.9 %collective-permute-start.24 = (bf16[16,2192]{1,0:T(8,128)(2,1)S(1)}, bf16[16,2192]{1,0:T(8,128)(2,1)S(1)}, u32[]{:S(2)}, u32[]{:S(2)}) collective-permute-start(bf16[16,2192]{1,0:T(8,128)(2,1)S(1)} %get-tuple-element.82), channel_id=1, source_target_pairs={{0,8},{2,10},{4,12},{6,14},{8,0},{10,2},{12,4},{14,6},{16,24},{18,... | collective-permute-start | bytes 210440 | tf_op jit(solution)/shard_map/ppermute | solution.py:28
  66.9 9.7 %collective-permute-start.23 = (bf16[16,2192]{1,0:T(8,128)(2,1)S(1)}, bf16[16,2192]{1,0:T(8,128)(2,1)S(1)}, u32[]{:S(2)}, u32[]{:S(2)}) collective-permute-start(bf16[16,2192]{1,0:T(8,128)(2,1)S(1)} %get-tuple-element.81), channel_id=1, source_target_pairs={{0,16},{2,18},{4,20},{6,22},{8,24},{10,26},{12,28},{14,30},{16,0},... | collective-permute-start | bytes 210440 | tf_op jit(solution)/shard_map/ppermute | solution.py:28
  67.6 10.3 %collective-permute-start.19 = (bf16[16,2048]{1,0:T(8,128)(2,1)S(1)}, bf16[16,2048]{1,0:T(8,128)(2,1)S(1)}, u32[]{:S(2)}, u32[]{:S(2)}) collective-permute-start(bf16[16,2048]{1,0:T(8,128)(2,1)S(1)} %fusion.56.refs_11_), channel_id=1, source_target_pairs={{0,16},{2,18},{4,20},{6,22},{8,24},{10,26},{12,28},{14,30},{16,0},... | collective-permute-start | bytes 196616 | tf_op jit(solution)/shard_map/ppermute | solution.py:28

commit v4 on v3

--- a/solution.py
+++ b/solution.py
@@ -86,36 +86,47 @@
     outs, (mark, turned) = refs[-5:-2], refs[-2:]
     half, units = rows[0].shape
 
-    @pl.when(pl.program_id(0) == 0)
+    @pl.when(jnp.logical_and(pl.program_id(0) == 0, pl.program_id(1) == 0))
     def _():
         mark[...] = jnp.zeros(mark.shape, F32)
-        for place, ref in enumerate(rows):
-            piece, k = divmod(place, 3)
-            turned[k * units : (k + 1) * units, piece * half : (piece + 1) * half] = ref[...].T
 
     for k, inputs in enumerate((normed, normed, cotangent)):
-        block = jnp.concatenate([ref[...] for ref in inputs], axis=0)
-        outs[k][...] = jnp.dot(
-            turned[k * units : (k + 1) * units, :], block, preferred_element_type=F32
-        )
+
+        @pl.when(pl.program_id(0) == k)
+        def _():
+            @pl.when(pl.program_id(1) == 0)
+            def _():
+                turned[:, :half] = rows[k][...].T
+                turned[:, half:] = rows[3 + k][...].T
+
+            block = jnp.concatenate([ref[...] for ref in inputs], axis=0)
+            outs[k][...] = jnp.dot(turned[...], block, preferred_element_type=F32)
 
 
 def weight_grads(rows, normed, cotangent, behind):
     units, width = rows[0].shape[1], normed[0].shape[1]
     block = min(width, 512)
-    whole = lambda a: pl.BlockSpec(a.shape, lambda i: (0, 0))
-    columns = lambda a: pl.BlockSpec((a.shape[0], block), lambda i: (0, i))
+    steps = width // block
+    whole = lambda a: pl.BlockSpec(a.shape, lambda k, i: (0, 0))
+
+    def columns(height, first, last):
+        def place(k, i):
+            return (0, jnp.where(k < first, 0, jnp.where(k > last, steps - 1, i)))
+
+        return pl.BlockSpec((height, block), place)
+
     return pl.pallas_call(
         grad_kernel,
-        grid=(width // block,),
+        grid=(3, steps),
         in_specs=[whole(a) for a in rows]
-        + [columns(a) for a in (*normed, *cotangent)]
+        + [columns(a.shape[0], 0, 1) for a in normed]
+        + [columns(a.shape[0], 2, 2) for a in cotangent]
         + [pl.BlockSpec(memory_space=pl.ANY)] * len(behind),
-        out_specs=[pl.BlockSpec((units, block), lambda i: (0, i))] * 3
-        + [pl.BlockSpec((8, width), lambda i: (0, 0))],
+        out_specs=[columns(units, k, k) for k in range(3)]
+        + [pl.BlockSpec((8, width), lambda k, i: (0, 0))],
         out_shape=[jax.ShapeDtypeStruct((units, width), F32)] * 3
         + [jax.ShapeDtypeStruct((8, width), F32)],
-        scratch_shapes=[pltpu.VMEM((3 * units, 2 * rows[0].shape[0]), BF16)],
+        scratch_shapes=[pltpu.VMEM((units, 2 * rows[0].shape[0]), BF16)],
         compiler_params=pltpu.CompilerParams(vmem_limit_bytes=24 * 2**20),
         cost_estimate=pl.CostEstimate(flops=1, bytes_accessed=60_000_000, transcendentals=0),
         name="weight_grads",

time: 78.9 us -> 82.8 us (1.049)
  Pallas kernels: 6.84 us -> 10.8 us
    pallas_call x1, Pallas kernels: 6.49 us -> 10.4 us  [weight_grads(): pl.pallas_call(grad_kernel, grid=(3, steps), in_specs=[whole(a) for a in...]
  transfers between devices with their start and end apart: 26 -> 26, of which waited for: 8 -> 8; matrix products, arithmetic and copies ran while one was open for 21% -> 20% of each run, Pallas kernels for 9% -> 13%
where the time goes in v4:
time: 82.8 us; the launch traced here: 82.5 us
  starting transfers between devices  30.5 us (37%)
  waiting for transfers between devices  21.4 us (26%)
  matrix products  10.9 us (13%)
  Pallas kernels  10.8 us (13%)
  other arithmetic  6.83 us (8%)
  between operations  1.15 us (1%)
  local copies, waits for them, and re-layouts  0.99 us (1%)
    ppermute x26, starting transfers between devices, swap(): return lax.ppermute(value, axis, [(i, i ^ distance) for i in range(size)])  30.5 us
    ppermute x26, waiting for transfers between devices, swap(): return lax.ppermute(value, axis, [(i, i ^ distance) for i in range(size)])  21.4 us
    pallas_call x1, Pallas kernels, weight_grads(): pl.pallas_call(grad_kernel, grid=(3, steps), in_specs=[whole(a) for a in...  10.4 us
    dot_general x6, matrix products, inward(): lax.dot_general(rows, weight, (((1,), (1,)), ((), ())), preferred_element...  5.6 us
    dot_general x9, matrix products, outward(): lax.dot_general(rows, weight, (((1,), (0,)), ((), ())), preferred_element...  5.26 us
    concatenate x2, other arithmetic, gather_rows_behind(): rows = jnp.concatenate([rows, swap(rows, 'dp', dp, distance)], axis=0)  1.71 us
  transfers between devices with their start and end apart: 26, of which 8 were waited for; matrix products, arithmetic and copies ran while one was open for 20% of the time, Pallas kernels for 13%

profile of v4, /device:TPU:0, one launch (start us, length us, event | category | flops | bytes accessed | tf_op | source)
XLA Modules:
  0.0 82.5 jit_solution(623445091282324953)
XLA Ops:
  0.6 1.1 %fusion.27 = f32[16]{0:T(128)S(1)} fusion(bf16[16,2048]{1,0:T(8,128)(2,1)} %param.6), kind=kLoop, calls=%fused_computation.69 | loop fusion | flops 98288 | bytes 65600 | tf_op jit(solution)/shard_map/reduce_sum | solution.py:187
  1.8 3.0 %collective-permute-start = (f32[16]{0:T(128)S(1)}, f32[16]{0:T(128)S(1)}, u32[]{:S(2)}, u32[]{:S(2)}) collective-permute-start(f32[16]{0:T(128)S(1)} %fusion.27), channel_id=1, source_target_pairs={{0,1},{1,0},{2,3},{3,2},{4,5},{5,4},{6,7},{7,6},{8,9},{9,8},{10,11... | collective-permute-start | bytes 200 | tf_op jit(solution)/shard_map/ppermute | solution.py:28
  4.8 2.6 %collective-permute-start.6 = (bf16[16,2048]{1,0:T(8,128)(2,1)}, bf16[16,2048]{1,0:T(8,128)(2,1)S(1)}, u32[]{:S(2)}, u32[]{:S(2)}) collective-permute-start(bf16[16,2048]{1,0:T(8,128)(2,1)} %param.7), channel_id=1, source_target_pairs={{0,16},{2,18},{4,20},{6,22},{8,24},{10,26},{12,28},{14,30},{16,0},... | collective-permute-start | bytes 196616 | tf_op jit(solution)/shard_map/ppermute | solution.py:28
  7.4 0.9 %constant_dynamic-update-slice_fusion.4 = (bf16[128,2048]{1,0:T(8,128)(2,1)S(1)}, bf16[16,2048]{1,0:T(8,128)(2,1)S(1)}) fusion(f32[2048]{0:T(1024)} %param.8, f32[16]{0:T(128)S(1)} %add_rsqrt_fusion, bf16[16,2048]{1,0:T(8,128)(2,1)} %param.6), kind=kLoop, calls=%fused_computation.113 | loop fusion | flops 131071 | bytes 204864
  8.3 2.1 %collective-permute-start.1 = (bf16[16,2048]{1,0:T(8,128)(2,1)S(1)}, bf16[16,2048]{1,0:T(8,128)(2,1)S(1)}, u32[]{:S(2)}, u32[]{:S(2)}) collective-permute-start(bf16[16,2048]{1,0:T(8,128)(2,1)S(1)} %get-tuple-element.53), channel_id=1, source_target_pairs={{0,16},{2,18},{4,20},{6,22},{8,24},{10,26},{12,28},{14,30},{16,0},... | collective-permute-start | bytes 196616 | tf_op jit(solution)/shard_map/ppermute | solution.py:28
  10.4 1.6 %collective-permute-start.2 = (bf16[16,2048]{1,0:T(8,128)(2,1)S(1)}, bf16[16,2048]{1,0:T(8,128)(2,1)S(1)}, u32[]{:S(2)}, u32[]{:S(2)}) collective-permute-start(bf16[16,2048]{1,0:T(8,128)(2,1)S(1)} %get-tuple-element.53), channel_id=1, source_target_pairs={{0,8},{2,10},{4,12},{6,14},{8,0},{10,2},{12,4},{14,6},{16,24},{18,... | collective-permute-start | bytes 196616 | tf_op jit(solution)/shard_map/ppermute | solution.py:28
  14.4 1.1 %collective-permute-done.1 = bf16[16,2048]{1,0:T(8,128)(2,1)S(1)} collective-permute-done((bf16[16,2048]{1,0:T(8,128)(2,1)S(1)}, bf16[16,2048]{1,0:T(8,128)(2,1)S(1)}, u32[]{:S(2)}, u32[]{:S(2)}) %collective-permute-start.1) | collective-permute-done | bytes 65568 | tf_op jit(solution)/shard_map/ppermute | solution.py:28
  15.5 2.7 %collective-permute-done.3 = bf16[16,2048]{1,0:T(8,128)(2,1)S(1)} collective-permute-done((bf16[16,2048]{1,0:T(8,128)(2,1)S(1)}, bf16[16,2048]{1,0:T(8,128)(2,1)S(1)}, u32[]{:S(2)}, u32[]{:S(2)}) %collective-permute-start.3) | collective-permute-done | bytes 65568 | tf_op jit(solution)/shard_map/ppermute | solution.py:28
  18.2 1.6 %collective-permute-start.4 = (bf16[64,2048]{1,0:T(8,128)(2,1)S(1)}, bf16[64,2048]{1,0:T(8,128)(2,1)S(1)}, u32[]{:S(2)}, u32[]{:S(2)}) collective-permute-start(bf16[64,2048]{1,0:T(8,128)(2,1)S(1)} %pad_maximum_fusion.3), channel_id=1, source_target_pairs={{0,4},{2,6},{4,0},{6,2},{8,12},{10,14},{12,8},{14,10},{16,20},{18,... | collective-permute-start | bytes 786440 | tf_op jit(solution)/shard_map/ppermute | solution.py:28
  19.8 0.9 %pad_maximum_fusion.4 = bf16[64,2048]{1,0:T(8,128)(2,1)S(1)} fusion(bf16[32,2048]{1,0:T(8,128)(2,1)S(1)} %collective-permute-done.7, bf16[16,2048]{1,0:T(8,128)(2,1)S(1)} %collective-permute-done.6, bf16[16,2048]{1,0:T(8,128)(2,1)} %param.7), kind=kLoop, calls=%fused_computation.49 | loop fusion | flops 786432 | bytes 524288 | tf_op jit(solution)/shard_map/concatenate | solution.py:71
  20.7 1.1 %collective-permute-start.8 = (bf16[64,2048]{1,0:T(8,128)(2,1)S(1)}, bf16[64,2048]{1,0:T(8,128)(2,1)S(1)}, u32[]{:S(2)}, u32[]{:S(2)}) collective-permute-start(bf16[64,2048]{1,0:T(8,128)(2,1)S(1)} %pad_maximum_fusion.4), channel_id=1, source_target_pairs={{0,4},{2,6},{4,0},{6,2},{8,12},{10,14},{12,8},{14,10},{16,20},{18,... | collective-permute-start | bytes 786440 | tf_op jit(solution)/shard_map/ppermute | solution.py:28
  21.8 5.0 %collective-permute-done.4 = bf16[64,2048]{1,0:T(8,128)(2,1)S(1)} collective-permute-done((bf16[64,2048]{1,0:T(8,128)(2,1)S(1)}, bf16[64,2048]{1,0:T(8,128)(2,1)S(1)}, u32[]{:S(2)}, u32[]{:S(2)}) %collective-permute-start.4) | collective-permute-done | bytes 262176 | tf_op jit(solution)/shard_map/ppermute | solution.py:28
  26.9 0.9 %fusion.78 = f32[128,640]{1,0:T(8,128)S(1)} fusion(bf16[128,2048]{1,0:T(8,128)(2,1)S(1)} %constant_dynamic-update-slice_fusion.refs_3_.refs_6_, bf16[640,2048]{1,0:T(8,128)(2,1)S(1)} %copy-done), kind=kOutput, calls=%fused_computation.145 | convolution fusion | flops 335544320 | bytes 3473408 | tf_op jit(solution)/shard_map/dot_general | solution.py:77
  27.9 0.9 %fusion.79 = f32[128,640]{1,0:T(8,128)S(1)} fusion(bf16[128,2048]{1,0:T(8,128)(2,1)S(1)} %constant_dynamic-update-slice_fusion.refs_3_.refs_6_, bf16[640,2048]{1,0:T(8,128)(2,1)S(1)} %copy-done.2), kind=kOutput, calls=%fused_computation.146 | convolution fusion | flops 335544320 | bytes 3473408 | tf_op jit(solution)/shard_map/dot_general | solution.py:77
  28.9 1.2 %collective-permute-start.10 = (bf16[256,640]{1,0:T(8,128)(2,1)S(1)}, bf16[256,640]{1,0:T(8,128)(2,1)S(1)}, u32[]{:S(2)}, u32[]{:S(2)}) collective-permute-start(bf16[256,640]{1,0:T(8,128)(2,1)S(1)} %fusion.2), channel_id=1, source_target_pairs={{0,1},{1,0},{2,3},{3,2},{4,5},{5,4},{6,7},{7,6},{8,9},{9,8},{10,11... | collective-permute-start | bytes 983048 | tf_op jit(solution)/shard_map/ppermute | solution.py:28
  30.4 0.9 %fusion.80 = f32[128,640]{1,0:T(8,128)S(1)} fusion(bf16[128,2048]{1,0:T(8,128)(2,1)S(1)} %collective-permute-done.5.refs_4_.refs_7_, bf16[640,2048]{1,0:T(8,128)(2,1)S(1)} %copy-done), kind=kOutput, calls=%fused_computation.147 | convolution fusion | flops 335544320 | bytes 3473408 | tf_op jit(solution)/shard_map/dot_general | solution.py:77
  31.4 0.9 %fusion.77 = f32[128,640]{1,0:T(8,128)S(1)} fusion(bf16[128,2048]{1,0:T(8,128)(2,1)S(1)} %collective-permute-done.5.refs_4_.refs_7_, bf16[640,2048]{1,0:T(8,128)(2,1)S(1)} %copy-done.2), kind=kOutput, calls=%fused_computation.144 | convolution fusion | flops 335544320 | bytes 3473408 | tf_op jit(solution)/shard_map/dot_general | solution.py:77
  32.4 1.0 %collective-permute-start.11 = (bf16[256,640]{1,0:T(8,128)(2,1)S(1)}, bf16[256,640]{1,0:T(8,128)(2,1)S(1)}, u32[]{:S(2)}, u32[]{:S(2)}) collective-permute-start(bf16[256,640]{1,0:T(8,128)(2,1)S(1)} %fusion.1), channel_id=1, source_target_pairs={{0,1},{1,0},{2,3},{3,2},{4,5},{5,4},{6,7},{7,6},{8,9},{9,8},{10,11... | collective-permute-start | bytes 983048 | tf_op jit(solution)/shard_map/ppermute | solution.py:28
  33.4 0.9 %fusion.66 = (bf16[128,640]{1,0:T(8,128)(2,1)S(1)}, f32[128,640]{1,0:T(8,128)S(1)}) fusion(pred[640]{0:T(1024)(128)(4,1)S(1)} %compare_reduce_fusion.8, bf16[128,2048]{1,0:T(8,128)(2,1)S(1)} %collective-permute-done.9.refs_9_, bf16[640,2048]{1,0:T(8,128)(2,1)S(1)} %copy-done.3), kind=kOutput, calls=%fused_computation.136 | convolution fusion | flops 335708160 | bytes 3637888 | tf_op jit(solution)/shard_map/dot_general | solution.py:77
  34.3 0.9 %fusion.76 = (bf16[128,640]{1,0:T(8,128)(2,1)S(1)}, f32[128,640]{1,0:T(8,128)S(1)}) fusion(bf16[640,2048]{1,0:T(8,128)(2,1)S(1)} %copy-done.3, bf16[64,2048]{1,0:T(8,128)(2,1)S(1)} %broadcast_select_fusion.1, bf16[32,2048]{1,0:T(8,128)(2,1)S(1)} %collective-permute-done.7, bf16[16,2048]{1,0:T(8,128)(2,1)S(1)} %collective-permute-done.6, ...), kind=kOutput, calls=%fused_computation.143 | convolution fusion | flops 337805312 | bytes 3637888 | tf_op jit(solution)/shard_map/dot_general | solution.py:77
  35.3 4.1 %collective-permute-done.10 = bf16[256,640]{1,0:T(8,128)(2,1)S(1)} collective-permute-done((bf16[256,640]{1,0:T(8,128)(2,1)S(1)}, bf16[256,640]{1,0:T(8,128)(2,1)S(1)}, u32[]{:S(2)}, u32[]{:S(2)}) %collective-permute-start.10) | collective-permute-done | bytes 327712 | tf_op jit(solution)/shard_map/ppermute | solution.py:28
  39.8 1.2 %collective-permute-start.14 = (bf16[128,640]{1,0:T(8,128)(2,1)S(1)}, bf16[128,640]{1,0:T(8,128)(2,1)S(1)}, u32[]{:S(2)}, u32[]{:S(2)}) collective-permute-start(bf16[128,640]{1,0:T(8,128)(2,1)S(1)} %get-tuple-element.46), channel_id=1, source_target_pairs={{0,1},{1,0},{2,3},{3,2},{4,5},{5,4},{6,7},{7,6},{8,9},{9,8},{10,11... | collective-permute-start | bytes 491528 | tf_op jit(solution)/shard_map/ppermute | solution.py:28
  41.0 0.9 %collective-permute-start.15 = (bf16[128,640]{1,0:T(8,128)(2,1)S(1)}, bf16[128,640]{1,0:T(8,128)(2,1)S(1)}, u32[]{:S(2)}, u32[]{:S(2)}) collective-permute-start(bf16[128,640]{1,0:T(8,128)(2,1)S(1)} %get-tuple-element.88), channel_id=1, source_target_pairs={{0,1},{1,0},{2,3},{3,2},{4,5},{5,4},{6,7},{7,6},{8,9},{9,8},{10,11... | collective-permute-start | bytes 491528 | tf_op jit(solution)/shard_map/ppermute | solution.py:28
  41.9 4.6 %collective-permute-done.11 = bf16[256,640]{1,0:T(8,128)(2,1)S(1)} collective-permute-done((bf16[256,640]{1,0:T(8,128)(2,1)S(1)}, bf16[256,640]{1,0:T(8,128)(2,1)S(1)}, u32[]{:S(2)}, u32[]{:S(2)}) %collective-permute-start.11) | collective-permute-done | bytes 327712 | tf_op jit(solution)/shard_map/ppermute | solution.py:28
  47.5 2.5 %collective-permute-done.14.got_ref = bf16[128,640]{1,0:T(8,128)(2,1)S(1)} collective-permute-done((bf16[128,640]{1,0:T(8,128)(2,1)S(1)}, bf16[128,640]{1,0:T(8,128)(2,1)S(1)}, u32[]{:S(2)}, u32[]{:S(2)}) %collective-permute-start.14) | collective-permute-done | bytes 163872 | tf_op jit(solution)/shard_map/ppermute | solution.py:28
  54.5 1.6 %collective-permute-start.18 = (bf16[64,2048]{1,0:T(8,128)(2,1)S(1)}, bf16[64,2048]{1,0:T(8,128)(2,1)S(1)}, u32[]{:S(2)}, u32[]{:S(2)}) collective-permute-start(bf16[64,2048]{1,0:T(8,128)(2,1)S(1)} %get-tuple-element.90), channel_id=1, source_target_pairs={{0,4},{2,6},{4,0},{6,2},{8,12},{10,14},{12,8},{14,10},{16,20},{18,... | collective-permute-start | bytes 786440 | tf_op jit(solution)/shard_map/ppermute | solution.py:28
  58.3 1.5 %collective-permute-start.21 = (f32[1,2112]{1,0:T(1,128)S(1)}, f32[1,2112]{1,0:T(1,128)S(1)}, u32[]{:S(2)}, u32[]{:S(2)}) collective-permute-start(f32[1,2112]{1,0:T(1,128)S(1)} %get-tuple-element.78), channel_id=1, source_target_pairs={{0,4},{2,6},{4,0},{6,2},{8,12},{10,14},{12,8},{14,10},{16,20},{18,... | collective-permute-start | bytes 25352 | tf_op jit(solution)/shard_map/ppermute | solution.py:28
  61.0 1.6 %collective-permute-start.17 = (bf16[32,2048]{1,0:T(8,128)(2,1)S(1)}, bf16[32,2048]{1,0:T(8,128)(2,1)S(1)}, u32[]{:S(2)}, u32[]{:S(2)}) collective-permute-start(bf16[32,2048]{1,0:T(8,128)(2,1)S(1)} %slice.325), channel_id=1, source_target_pairs={{0,4},{2,6},{4,0},{6,2},{8,12},{10,14},{12,8},{14,10},{16,20},{18,... | collective-permute-start | bytes 393224 | tf_op jit(solution)/shard_map/ppermute | solution.py:28
  63.0 2.6 %collective-permute-start.25 = (bf16[16,2192]{1,0:T(8,128)(2,1)S(1)}, bf16[16,2192]{1,0:T(8,128)(2,1)S(1)}, u32[]{:S(2)}, u32[]{:S(2)}) collective-permute-start(bf16[16,2192]{1,0:T(8,128)(2,1)S(1)} %get-tuple-element.83.refs_10_), channel_id=1, source_target_pairs={{0,24},{2,26},{4,28},{6,30},{8,16},{10,18},{12,20},{14,22},{16,8},... | collective-permute-start | bytes 210440 | tf_op jit(solution)/shard_map/ppermute | solution.py:28
  65.6 1.2 %collective-permute-start.24 = (bf16[16,2192]{1,0:T(8,128)(2,1)S(1)}, bf16[16,2192]{1,0:T(8,128)(2,1)S(1)}, u32[]{:S(2)}, u32[]{:S(2)}) collective-permute-start(bf16[16,2192]{1,0:T(8,128)(2,1)S(1)} %get-tuple-element.82), channel_id=1, source_target_pairs={{0,8},{2,10},{4,12},{6,14},{8,0},{10,2},{12,4},{14,6},{16,24},{18,... | collective-permute-start | bytes 210440 | tf_op jit(solution)/shard_map/ppermute | solution.py:28
  67.6 2.3 %collective-permute-start.19 = (bf16[16,2048]{1,0:T(8,128)(2,1)S(1)}, bf16[16,2048]{1,0:T(8,128)(2,1)S(1)}, u32[]{:S(2)}, u32[]{:S(2)}) collective-permute-start(bf16[16,2048]{1,0:T(8,128)(2,1)S(1)} %fusion.56.refs_11_), channel_id=1, source_target_pairs={{0,16},{2,18},{4,20},{6,22},{8,24},{10,26},{12,28},{14,30},{16,0},... | collective-permute-start | bytes 196616 | tf_op jit(solution)/shard_map/ppermute | solution.py:28
  69.9 10.4 %weight_grads.1 = (f32[640,2048]{1,0:T(8,128)}, f32[640,2048]{1,0:T(8,128)}, f32[640,2048]{1,0:T(8,128)}, f32[8,2048]{1,0:T(8,128)S(1)}) custom-call(bf16[128,640]{1,0:T(8,128)(2,1)S(1)} %get-tuple-element.34.refs_0_, bf16[128,640]{1,0:T(8,128)(2,1)S(1)} %get-tuple-element.35.refs_1_, bf16[128,640]{1,0:T(8,128)(2,1)S(1)} %get-tuple-element.24.refs_2_, ...), custom_call_target="tpu_custom_call" | custom-call | flops 1 | bytes 60000000 | tf_op jit(solution)/shard_map/weight_grads/pallas_call | solution.py:118
  (106 shorter events, 15.3 us)
Async XLA Ops:
  0.6 26.3 %copy-start = (bf16[640,2048]{1,0:T(8,128)(2,1)S(1)}, bf16[640,2048]{1,0:T(8,128)(2,1)}, u32[]{:S(2)}) copy-start(bf16[640,2048]{1,0:T(8,128)(2,1)} %param.10) | copy-start | bytes 7864324
  1.8 5.6 %collective-permute-start = (f32[16]{0:T(128)S(1)}, f32[16]{0:T(128)S(1)}, u32[]{:S(2)}, u32[]{:S(2)}) collective-permute-start(f32[16]{0:T(128)S(1)} %fusion.27), channel_id=1, source_target_pairs={{0,1},{1,0},{2,3},{3,2},{4,5},{5,4},{6,7},{7,6},{8,9},{9,8},{10,11... | collective-permute-start | bytes 200 | tf_op jit(solution)/shard_map/ppermute | solution.py:28
  4.8 8.0 %collective-permute-start.6 = (bf16[16,2048]{1,0:T(8,128)(2,1)}, bf16[16,2048]{1,0:T(8,128)(2,1)S(1)}, u32[]{:S(2)}, u32[]{:S(2)}) collective-permute-start(bf16[16,2048]{1,0:T(8,128)(2,1)} %param.7), channel_id=1, source_target_pairs={{0,16},{2,18},{4,20},{6,22},{8,24},{10,26},{12,28},{14,30},{16,0},... | collective-permute-start | bytes 196616 | tf_op jit(solution)/shard_map/ppermute | solution.py:28
  8.3 7.1 %collective-permute-start.1 = (bf16[16,2048]{1,0:T(8,128)(2,1)S(1)}, bf16[16,2048]{1,0:T(8,128)(2,1)S(1)}, u32[]{:S(2)}, u32[]{:S(2)}) collective-permute-start(bf16[16,2048]{1,0:T(8,128)(2,1)S(1)} %get-tuple-element.53), channel_id=1, source_target_pairs={{0,16},{2,18},{4,20},{6,22},{8,24},{10,26},{12,28},{14,30},{16,0},... | collective-permute-start | bytes 196616 | tf_op jit(solution)/shard_map/ppermute | solution.py:28
  10.4 5.0 %collective-permute-start.2 = (bf16[16,2048]{1,0:T(8,128)(2,1)S(1)}, bf16[16,2048]{1,0:T(8,128)(2,1)S(1)}, u32[]{:S(2)}, u32[]{:S(2)}) collective-permute-start(bf16[16,2048]{1,0:T(8,128)(2,1)S(1)} %get-tuple-element.53), channel_id=1, source_target_pairs={{0,8},{2,10},{4,12},{6,14},{8,0},{10,2},{12,4},{14,6},{16,24},{18,... | collective-permute-start | bytes 196616 | tf_op jit(solution)/shard_map/ppermute | solution.py:28
  12.0 6.2 %collective-permute-start.3 = (bf16[16,2048]{1,0:T(8,128)(2,1)S(1)}, bf16[16,2048]{1,0:T(8,128)(2,1)S(1)}, u32[]{:S(2)}, u32[]{:S(2)}) collective-permute-start(bf16[16,2048]{1,0:T(8,128)(2,1)S(1)} %get-tuple-element.53), channel_id=1, source_target_pairs={{0,24},{2,26},{4,28},{6,30},{8,16},{10,18},{12,20},{14,22},{16,8},... | collective-permute-start | bytes 196616 | tf_op jit(solution)/shard_map/ppermute | solution.py:28
  13.6 14.2 %copy-start.2 = (bf16[640,2048]{1,0:T(8,128)(2,1)S(1)}, bf16[640,2048]{1,0:T(8,128)(2,1)}, u32[]{:S(2)}) copy-start(bf16[640,2048]{1,0:T(8,128)(2,1)} %param.9) | copy-start | bytes 7864324
  13.6 6.2 %collective-permute-start.7 = (bf16[32,2048]{1,0:T(8,128)(2,1)S(1)}, bf16[32,2048]{1,0:T(8,128)(2,1)S(1)}, u32[]{:S(2)}, u32[]{:S(2)}) collective-permute-start(bf16[32,2048]{1,0:T(8,128)(2,1)S(1)} %pad_maximum_fusion.5), channel_id=1, source_target_pairs={{0,8},{2,10},{4,12},{6,14},{8,0},{10,2},{12,4},{14,6},{16,24},{18,... | collective-permute-start | bytes 393224 | tf_op jit(solution)/shard_map/ppermute | solution.py:28
  18.2 8.6 %collective-permute-start.4 = (bf16[64,2048]{1,0:T(8,128)(2,1)S(1)}, bf16[64,2048]{1,0:T(8,128)(2,1)S(1)}, u32[]{:S(2)}, u32[]{:S(2)}) collective-permute-start(bf16[64,2048]{1,0:T(8,128)(2,1)S(1)} %pad_maximum_fusion.3), channel_id=1, source_target_pairs={{0,4},{2,6},{4,0},{6,2},{8,12},{10,14},{12,8},{14,10},{16,20},{18,... | collective-permute-start | bytes 786440 | tf_op jit(solution)/shard_map/ppermute | solution.py:28
  20.7 9.4 %collective-permute-start.8 = (bf16[64,2048]{1,0:T(8,128)(2,1)S(1)}, bf16[64,2048]{1,0:T(8,128)(2,1)S(1)}, u32[]{:S(2)}, u32[]{:S(2)}) collective-permute-start(bf16[64,2048]{1,0:T(8,128)(2,1)S(1)} %pad_maximum_fusion.4), channel_id=1, source_target_pairs={{0,4},{2,6},{4,0},{6,2},{8,12},{10,14},{12,8},{14,10},{16,20},{18,... | collective-permute-start | bytes 786440 | tf_op jit(solution)/shard_map/ppermute | solution.py:28
  26.8 3.6 %collective-permute-start.5 = (bf16[128,2048]{1,0:T(8,128)(2,1)S(1)}, bf16[128,2048]{1,0:T(8,128)(2,1)S(1)}, u32[]{:S(2)}, u32[]{:S(2)}) collective-permute-start(bf16[128,2048]{1,0:T(8,128)(2,1)S(1)} %constant_dynamic-update-slice_fusion.refs_3_.refs_6_), channel_id=1, source_target_pairs={{0,2},{2,0},{4,6},{6,4},{8,10},{10,8},{12,14},{14,12},{16,18},{18,... | collective-permute-start | bytes 1572872 | tf_op jit(solution)/shard_map/ppermute | solution.py:28
  27.9 2.2 %copy-start.5 = (bf16[16,2048]{1,0:T(8,128)(2,1)S(1)}, bf16[16,2048]{1,0:T(8,128)(2,1)}, u32[]{:S(2)}) copy-start(bf16[16,2048]{1,0:T(8,128)(2,1)} %param.7) | copy-start | bytes 196612
  28.9 10.6 %collective-permute-start.10 = (bf16[256,640]{1,0:T(8,128)(2,1)S(1)}, bf16[256,640]{1,0:T(8,128)(2,1)S(1)}, u32[]{:S(2)}, u32[]{:S(2)}) collective-permute-start(bf16[256,640]{1,0:T(8,128)(2,1)S(1)} %fusion.2), channel_id=1, source_target_pairs={{0,1},{1,0},{2,3},{3,2},{4,5},{5,4},{6,7},{7,6},{8,9},{9,8},{10,11... | collective-permute-start | bytes 983048 | tf_op jit(solution)/shard_map/ppermute | solution.py:28
  30.2 3.2 %collective-permute-start.9 = (bf16[128,2048]{1,0:T(8,128)(2,1)S(1)}, bf16[128,2048]{1,0:T(8,128)(2,1)S(1)}, u32[]{:S(2)}, u32[]{:S(2)}) collective-permute-start(bf16[128,2048]{1,0:T(8,128)(2,1)S(1)} %pad_maximum_fusion.2.refs_8_), channel_id=1, source_target_pairs={{0,2},{2,0},{4,6},{6,4},{8,10},{10,8},{12,14},{14,12},{16,18},{18,... | collective-permute-start | bytes 1572872 | tf_op jit(solution)/shard_map/ppermute | solution.py:28
  31.4 2.0 %copy-start.3 = (bf16[640,2048]{1,0:T(8,128)(2,1)S(1)}, bf16[640,2048]{1,0:T(8,128)(2,1)}, u32[]{:S(2)}) copy-start(bf16[640,2048]{1,0:T(8,128)(2,1)} %param.11) | copy-start | bytes 7864324
  32.4 14.1 %collective-permute-start.11 = (bf16[256,640]{1,0:T(8,128)(2,1)S(1)}, bf16[256,640]{1,0:T(8,128)(2,1)S(1)}, u32[]{:S(2)}, u32[]{:S(2)}) collective-permute-start(bf16[256,640]{1,0:T(8,128)(2,1)S(1)} %fusion.1), channel_id=1, source_target_pairs={{0,1},{1,0},{2,3},{3,2},{4,5},{5,4},{6,7},{7,6},{8,9},{9,8},{10,11... | collective-permute-start | bytes 983048 | tf_op jit(solution)/shard_map/ppermute | solution.py:28
  39.8 10.2 %collective-permute-start.14 = (bf16[128,640]{1,0:T(8,128)(2,1)S(1)}, bf16[128,640]{1,0:T(8,128)(2,1)S(1)}, u32[]{:S(2)}, u32[]{:S(2)}) collective-permute-start(bf16[128,640]{1,0:T(8,128)(2,1)S(1)} %get-tuple-element.46), channel_id=1, source_target_pairs={{0,1},{1,0},{2,3},{3,2},{4,5},{5,4},{6,7},{7,6},{8,9},{9,8},{10,11... | collective-permute-start | bytes 491528 | tf_op jit(solution)/shard_map/ppermute | solution.py:28
  41.0 12.1 %collective-permute-start.15 = (bf16[128,640]{1,0:T(8,128)(2,1)S(1)}, bf16[128,640]{1,0:T(8,128)(2,1)S(1)}, u32[]{:S(2)}, u32[]{:S(2)}) collective-permute-start(bf16[128,640]{1,0:T(8,128)(2,1)S(1)} %get-tuple-element.88), channel_id=1, source_target_pairs={{0,1},{1,0},{2,3},{3,2},{4,5},{5,4},{6,7},{7,6},{8,9},{9,8},{10,11... | collective-permute-start | bytes 491528 | tf_op jit(solution)/shard_map/ppermute | solution.py:28
  47.4 4.1 %collective-permute-start.12 = (bf16[128,2048]{1,0:T(8,128)(2,1)S(1)}, bf16[128,2048]{1,0:T(8,128)(2,1)S(1)}, u32[]{:S(2)}, u32[]{:S(2)}) collective-permute-start(bf16[128,2048]{1,0:T(8,128)(2,1)S(1)} %convolution_convert_fusion.refs_0_), channel_id=1, source_target_pairs={{0,2},{2,0},{4,6},{6,4},{8,10},{10,8},{12,14},{14,12},{16,18},{18,... | collective-permute-start | bytes 1572872 | tf_op jit(solution)/shard_map/ppermute | solution.py:28
  51.4 2.5 %collective-permute-start.16 = (bf16[128,2048]{1,0:T(8,128)(2,1)S(1)}, bf16[128,2048]{1,0:T(8,128)(2,1)S(1)}, u32[]{:S(2)}, u32[]{:S(2)}) collective-permute-start(bf16[128,2048]{1,0:T(8,128)(2,1)S(1)} %fusion.refs_2_), channel_id=1, source_target_pairs={{0,2},{2,0},{4,6},{6,4},{8,10},{10,8},{12,14},{14,12},{16,18},{18,... | collective-permute-start | bytes 1572872 | tf_op jit(solution)/shard_map/ppermute | solution.py:28
  52.2 8.8 %collective-permute-start.13 = (bf16[64,2048]{1,0:T(8,128)(2,1)S(1)}, bf16[64,2048]{1,0:T(8,128)(2,1)S(1)}, u32[]{:S(2)}, u32[]{:S(2)}) collective-permute-start(bf16[64,2048]{1,0:T(8,128)(2,1)S(1)} %add_convert_fusion.1), channel_id=1, source_target_pairs={{0,8},{2,10},{4,12},{6,14},{8,0},{10,2},{12,4},{14,6},{16,24},{18,... | collective-permute-start | bytes 786440 | tf_op jit(solution)/shard_map/ppermute | solution.py:28
  54.5 8.2 %collective-permute-start.18 = (bf16[64,2048]{1,0:T(8,128)(2,1)S(1)}, bf16[64,2048]{1,0:T(8,128)(2,1)S(1)}, u32[]{:S(2)}, u32[]{:S(2)}) collective-permute-start(bf16[64,2048]{1,0:T(8,128)(2,1)S(1)} %get-tuple-element.90), channel_id=1, source_target_pairs={{0,4},{2,6},{4,0},{6,2},{8,12},{10,14},{12,8},{14,10},{16,20},{18,... | collective-permute-start | bytes 786440 | tf_op jit(solution)/shard_map/ppermute | solution.py:28
  56.7 0.7 copy-start.1
  57.6 5.2 %collective-permute-start.22 = (f32[1,2112]{1,0:T(1,128)S(1)}, f32[1,2112]{1,0:T(1,128)S(1)}, u32[]{:S(2)}, u32[]{:S(2)}) collective-permute-start(f32[1,2112]{1,0:T(1,128)S(1)} %get-tuple-element.79), channel_id=1, source_target_pairs={{0,6},{2,4},{4,2},{6,0},{8,14},{10,12},{12,10},{14,8},{16,22},{18,... | collective-permute-start | bytes 25352 | tf_op jit(solution)/shard_map/ppermute | solution.py:28
  57.7 5.1 %collective-permute-start.20 = (f32[1,2112]{1,0:T(1,128)S(1)}, f32[1,2112]{1,0:T(1,128)S(1)}, u32[]{:S(2)}, u32[]{:S(2)}) collective-permute-start(f32[1,2112]{1,0:T(1,128)S(1)} %get-tuple-element.80), channel_id=1, source_target_pairs={{0,2},{2,0},{4,6},{6,4},{8,10},{10,8},{12,14},{14,12},{16,18},{18,... | collective-permute-start | bytes 25352 | tf_op jit(solution)/shard_map/ppermute | solution.py:28
  58.3 4.5 %collective-permute-start.21 = (f32[1,2112]{1,0:T(1,128)S(1)}, f32[1,2112]{1,0:T(1,128)S(1)}, u32[]{:S(2)}, u32[]{:S(2)}) collective-permute-start(f32[1,2112]{1,0:T(1,128)S(1)} %get-tuple-element.78), channel_id=1, source_target_pairs={{0,4},{2,6},{4,0},{6,2},{8,12},{10,14},{12,8},{14,10},{16,20},{18,... | collective-permute-start | bytes 25352 | tf_op jit(solution)/shard_map/ppermute | solution.py:28
  61.0 6.5 %collective-permute-start.17 = (bf16[32,2048]{1,0:T(8,128)(2,1)S(1)}, bf16[32,2048]{1,0:T(8,128)(2,1)S(1)}, u32[]{:S(2)}, u32[]{:S(2)}) collective-permute-start(bf16[32,2048]{1,0:T(8,128)(2,1)S(1)} %slice.325), channel_id=1, source_target_pairs={{0,4},{2,6},{4,0},{6,2},{8,12},{10,14},{12,8},{14,10},{16,20},{18,... | collective-permute-start | bytes 393224 | tf_op jit(solution)/shard_map/ppermute | solution.py:28
  63.0 17.5 %copy-start.4 = (bf16[16,2048]{1,0:T(8,128)(2,1)S(1)}, bf16[16,2048]{1,0:T(8,128)(2,1)}, u32[]{:S(2)}) copy-start(bf16[16,2048]{1,0:T(8,128)(2,1)} %param.6) | copy-start | bytes 196612
  63.0 17.4 %collective-permute-start.25 = (bf16[16,2192]{1,0:T(8,128)(2,1)S(1)}, bf16[16,2192]{1,0:T(8,128)(2,1)S(1)}, u32[]{:S(2)}, u32[]{:S(2)}) collective-permute-start(bf16[16,2192]{1,0:T(8,128)(2,1)S(1)} %get-tuple-element.83.refs_10_), channel_id=1, source_target_pairs={{0,24},{2,26},{4,28},{6,30},{8,16},{10,18},{12,20},{14,22},{16,8},... | collective-permute-start | bytes 210440 | tf_op jit(solution)/shard_map/ppermute | solution.py:28
  65.6 14.8 %collective-permute-start.24 = (bf16[16,2192]{1,0:T(8,128)(2,1)S(1)}, bf16[16,2192]{1,0:T(8,128)(2,1)S(1)}, u32[]{:S(2)}, u32[]{:S(2)}) collective-permute-start(bf16[16,2192]{1,0:T(8,128)(2,1)S(1)} %get-tuple-element.82), channel_id=1, source_target_pairs={{0,8},{2,10},{4,12},{6,14},{8,0},{10,2},{12,4},{14,6},{16,24},{18,... | collective-permute-start | bytes 210440 | tf_op jit(solution)/shard_map/ppermute | solution.py:28
  66.9 13.6 %collective-permute-start.23 = (bf16[16,2192]{1,0:T(8,128)(2,1)S(1)}, bf16[16,2192]{1,0:T(8,128)(2,1)S(1)}, u32[]{:S(2)}, u32[]{:S(2)}) collective-permute-start(bf16[16,2192]{1,0:T(8,128)(2,1)S(1)} %get-tuple-element.81), channel_id=1, source_target_pairs={{0,16},{2,18},{4,20},{6,22},{8,24},{10,26},{12,28},{14,30},{16,0},... | collective-permute-start | bytes 210440 | tf_op jit(solution)/shard_map/ppermute | solution.py:28
  67.6 14.3 %collective-permute-start.19 = (bf16[16,2048]{1,0:T(8,128)(2,1)S(1)}, bf16[16,2048]{1,0:T(8,128)(2,1)S(1)}, u32[]{:S(2)}, u32[]{:S(2)}) collective-permute-start(bf16[16,2048]{1,0:T(8,128)(2,1)S(1)} %fusion.56.refs_11_), channel_id=1, source_target_pairs={{0,16},{2,18},{4,20},{6,22},{8,24},{10,26},{12,28},{14,30},{16,0},... | collective-permute-start | bytes 196616 | tf_op jit(solution)/shard_map/ppermute | solution.py:28
